TPU v7x, 512 devices: a whole 4x8x8 slice. The times are simulated.
512 devices in a mesh: section: 2 (over z_hi), ctx: 32 (over y, z_lo), tp: 8 (over x, core).
Axes of the slice: x: 4, y: 8, z: 8 (z_hi: 2, z_lo: 4; z = z_hi * 4 + z_lo), core: 2. Of those that a mesh axis runs over, the one named last changes fastest.
Arguments:
- inputs: bfloat16 [2, 4096, 8192], P('section', 'ctx', 'tp'), may hold values from -6 to 6
- kv_weight: bfloat16 [2, 8192, 1024], P('section', 'tp'), may hold values from -0.06629126 to 0.06629126
- queries_a: bfloat16 [2, 4096, 4096], P('section', 'ctx', 'tp'), may hold values from -160 to 160
- queries_b: bfloat16 [2, 4096, 4096], P('section', 'ctx', 'tp'), may hold values from -160 to 160
- grads_a: bfloat16 [2, 4096, 4096], P('section', 'ctx', 'tp'), may hold values from -6 to 6
- grads_b: bfloat16 [2, 4096, 4096], P('section', 'ctx', 'tp'), may hold values from -6 to 6
- span_order: int32 [64], replicated, may hold values from 0 to 63, each once
Outputs:
- out_a: bfloat16 [2, 4096, 4096], P('section', 'ctx', 'tp')
- out_b: bfloat16 [2, 4096, 4096], P('section', 'ctx', 'tp')
- grad_qa: bfloat16 [2, 4096, 4096], P('section', 'ctx', 'tp')
- grad_qb: bfloat16 [2, 4096, 4096], P('section', 'ctx', 'tp')
- grad_x: bfloat16 [2, 4096, 8192], P('section', 'ctx', 'tp')
All inputs are finite; a program needn't handle non-finite values.
Results may differ from a plain program's by a relative error of at most 0.04.
The roundings to bfloat16 on the way count: a program that leaves them out, or rounds other values in their place, can miss the bound.
Values may be sent and summed in bfloat16 or wider, within the bound.
No kernel may reach another device: no remote copies, remote signals or barrier semaphores. Data moves between devices by JAX's collectives and lax.ppermute only.
A program may use at most 128 MiB of HBM per device.

v0:
```python
import jax
import jax.numpy as jnp
from jax import lax
from jax.sharding import PartitionSpec as P

HEADS = 32
KVH = 4
HD = 128
SPANS_DEV = 2


def from_behind(value, axis, steps):
    count = lax.axis_size(axis)
    pairs = [(source, (source + steps) % count) for source in range(count)]
    return lax.ppermute(value, axis, pairs)


def split_heads(matrix, kv_count, per_kv):
    return matrix.reshape(matrix.shape[0], kv_count, per_kv, HD)


def attend(queries, keyvals, query_pos, key_pos, kv_count, per_kv):
    query_heads = split_heads(queries, kv_count, per_kv)
    key_value = keyvals.reshape(keyvals.shape[0], kv_count, 2, HD)
    score_scale = HD ** (-0.5)
    scores = (
        jnp.einsum(
            "rghe,tge->ghrt", query_heads, key_value[:, :, 0], preferred_element_type=jnp.float32
        )
        * score_scale
    )
    visible = key_pos[None, :] <= query_pos[:, None]
    scores = jnp.where(visible, scores, -1e30)
    row_max = jnp.max(scores, axis=3, keepdims=True)
    weights = jnp.exp(scores - row_max)
    probabilities = (weights / jnp.sum(weights, axis=3, keepdims=True)).astype(jnp.bfloat16)
    mixed = jnp.einsum(
        "ghrt,tge->rghe", probabilities, key_value[:, :, 1], preferred_element_type=jnp.float32
    )
    return (mixed.astype(jnp.bfloat16).reshape(queries.shape), probabilities)


def retrace(queries, grads, mixed, probabilities, keyvals, kv_count, per_kv):
    query_heads = split_heads(queries, kv_count, per_kv)
    grad_heads = split_heads(grads, kv_count, per_kv)
    key_value = keyvals.reshape(keyvals.shape[0], kv_count, 2, HD)
    score_scale = HD ** (-0.5)
    row_delta = jnp.sum(
        grad_heads.astype(jnp.float32) * split_heads(mixed, kv_count, per_kv).astype(jnp.float32),
        axis=3,
    )
    row_delta = jnp.transpose(row_delta, (1, 2, 0))[..., None]
    grad_prob = jnp.einsum(
        "rghe,tge->ghrt", grad_heads, key_value[:, :, 1], preferred_element_type=jnp.float32
    )
    grad_score = (probabilities.astype(jnp.float32) * (grad_prob - row_delta)).astype(jnp.bfloat16)
    grad_query = (
        jnp.einsum(
            "ghrt,tge->rghe", grad_score, key_value[:, :, 0], preferred_element_type=jnp.float32
        )
        * score_scale
    )
    key_grad = (
        jnp.einsum("ghrt,rghe->tge", grad_score, query_heads, preferred_element_type=jnp.float32)
        * score_scale
    )
    value_grad = jnp.einsum(
        "ghrt,rghe->tge", probabilities, grad_heads, preferred_element_type=jnp.float32
    )
    key_terms = jnp.stack([key_grad, value_grad], axis=2).reshape(
        keyvals.shape[0], kv_count * 2 * HD
    )
    return (grad_query.astype(jnp.bfloat16).reshape(queries.shape), key_terms)


def reduce_keys(key_terms):
    return lax.psum_scatter(
        key_terms.astype(jnp.bfloat16), "ctx", scatter_dimension=0, tiled=True
    ).astype(jnp.float32)


def on_device(inputs, kv_weight, queries_a, queries_b, grads_a, grads_b, span_order):
    features = inputs[0]
    weight_rows = kv_weight[0]
    local_rows = features.shape[0]
    tp_size = lax.axis_size("tp")
    heads_here = HEADS // tp_size
    group_size = HEADS // KVH
    kv_count = max(1, heads_here // group_size)
    per_kv = heads_here // kv_count
    share_count = max(1, group_size // heads_here)
    kv_width = kv_count * 2 * HD
    partial_value = jnp.dot(features, weight_rows, preferred_element_type=jnp.float32)
    kv_whole = lax.psum(partial_value, "tp").astype(jnp.bfloat16)
    first_head = lax.axis_index("tp") * heads_here // group_size
    kv_own = lax.dynamic_slice_in_dim(kv_whole, first_head * 2 * HD, kv_width, 1)
    span_rows = local_rows // SPANS_DEV
    within = jnp.tile(jnp.arange(span_rows, dtype=jnp.int32), span_order.shape[0])
    key_pos = jnp.repeat(span_order * span_rows, span_rows) + within
    query_pos = lax.dynamic_slice_in_dim(key_pos, lax.axis_index("ctx") * local_rows, local_rows)
    kv_prev = from_behind(kv_own, "section", 1)
    keys_a = lax.all_gather(kv_own, "ctx", axis=0, tiled=True)
    out_a, probs_a = attend(queries_a[0], keys_a, query_pos, key_pos, kv_count, per_kv)
    keys_b = lax.all_gather(kv_prev, "ctx", axis=0, tiled=True)
    out_b, probs_b = attend(queries_b[0], keys_b, query_pos, key_pos, kv_count, per_kv)
    again_a, again_b = (
        lax.all_gather(kv_own, "ctx", axis=0, tiled=True),
        lax.all_gather(kv_prev, "ctx", axis=0, tiled=True),
    )
    grad_qa, terms_a = retrace(queries_a[0], grads_a[0], out_a, probs_a, again_a, kv_count, per_kv)
    own_grads = reduce_keys(terms_a)
    grad_qb, terms_b = retrace(queries_b[0], grads_b[0], out_b, probs_b, again_b, kv_count, per_kv)
    prev_grads = reduce_keys(terms_b)
    returned = from_behind(prev_grads.astype(jnp.bfloat16), "section", -1).astype(prev_grads.dtype)
    section_sum = own_grads + returned
    gathered = lax.all_gather(section_sum.astype(jnp.bfloat16), "tp", axis=1, tiled=True).astype(
        section_sum.dtype
    )
    head_sums = jnp.sum(gathered.reshape(local_rows, KVH, share_count, 2 * HD), axis=2)
    kv_grads = head_sums.astype(jnp.bfloat16).reshape(local_rows, KVH * 2 * HD)
    grad_x = lax.dot_general(
        kv_grads, weight_rows, (((1,), (1,)), ((), ())), preferred_element_type=jnp.float32
    )
    return (
        out_a[None],
        out_b[None],
        grad_qa[None],
        grad_qb[None],
        grad_x.astype(jnp.bfloat16)[None],
    )


def solution(mesh):
    in_specs = (
        P("section", "ctx", "tp"),
        P("section", "tp", None),
        P("section", "ctx", "tp"),
        P("section", "ctx", "tp"),
        P("section", "ctx", "tp"),
        P("section", "ctx", "tp"),
        P(),
    )
    out_specs = (
        P("section", "ctx", "tp"),
        P("section", "ctx", "tp"),
        P("section", "ctx", "tp"),
        P("section", "ctx", "tp"),
        P("section", "ctx", "tp"),
    )
    return jax.shard_map(
        on_device, mesh=mesh, in_specs=in_specs, out_specs=out_specs, check_vma=False
    )
```

profile of v0, /device:TPU:1, one launch (start us, length us, event | category | flops | bytes accessed | tf_op | source)
XLA Modules:
  0.0 743.9 jit_solution(14056911039352429495)
XLA Ops:
  7.3 1.5 copy-done
  10.2 32.4 %all-reduce.1 = bf16[128,1024]{1,0:T(8,128)(2,1)S(1)} all-reduce(f32[128,1024]{1,0:T(8,128)S(1)} %fusion.26), channel_id=1, replica_groups=mesh['section'=2,'ctx'=32,'tp'=8] {'tp'}, use_global_device_ids=true, to_apply=%region_0.0 | all-reduce | flops 131072 | bytes 786432 | tf_op jit(solution)/shard_map/psum | solution.py:94
  43.3 7.2 collective-permute-start
  50.5 2.0 collective-permute-done
  57.2 1.7 copy.97
  58.9 2.5 broadcast_compare_fusion
  61.5 117.3 %all-gather.3.cloned.1.call-done = bf16[4096,256]{1,0:T(8,128)(2,1)} async-done(((bf16[128,256]{1,0:T(8,128)(2,1)}), bf16[4096,256]{1,0:T(8,128)(2,1)}) %all-gather.3.cloned.1.call-update) | async-done | bytes 2097168 | tf_op jit(solution)/shard_map/all_gather | solution.py:102
  178.8 4.0 reshape.201
  182.7 6.8 fusion.48
  189.5 4.7 copy.92
  194.2 143.7 %all-gather.5.cloned.1.call-done = bf16[4096,256]{1,0:T(8,128)(2,1)} async-done(((bf16[128,256]{1,0:T(8,128)(2,1)}), bf16[4096,256]{1,0:T(8,128)(2,1)}) %all-gather.5.cloned.1.call-update) | async-done | bytes 2097168 | tf_op jit(solution)/shard_map/all_gather | solution.py:104
  337.9 4.0 reshape.206
  341.9 6.7 fusion.47
  348.6 5.4 copy.94
  354.0 3.0 fusion.50
  358.1 1.4 divide_convert_fusion
  359.6 1.5 fusion.14
  363.8 1.5 fusion.15
  365.3 1.5 pad_maximum_fusion.1
  366.8 4.1 copy.90
  371.1 2.9 fusion.49
  376.6 1.5 fusion.16
  380.2 1.5 fusion.17
  381.7 1.5 pad_maximum_fusion
  383.2 4.1 copy.88
  388.1 3.6 fusion.40
  392.4 139.5 %reduce-scatter.9.cloned.1.call-done = bf16[128,256]{1,0:T(8,128)(2,1)} async-done(((bf16[4096,256]{1,0:T(8,128)(2,1)}), bf16[128,256]{1,0:T(8,128)(2,1)}) %reduce-scatter.9.cloned.1.call-update) | async-done | bytes 65552
  532.9 6.2 collective-permute-start.1
  539.2 3.6 fusion.41
  544.3 152.2 %reduce-scatter.7.cloned.1.call-done = bf16[128,256]{1,0:T(8,128)(2,1)} async-done(((bf16[4096,256]{1,0:T(8,128)(2,1)}), bf16[128,256]{1,0:T(8,128)(2,1)}) %reduce-scatter.7.cloned.1.call-update) | async-done | bytes 65552
  697.5 38.1 %all_gather.13 = bf16[128,2048]{0,1:T(8,128)(2,1)S(1)} all-gather(bf16[128,256]{0,1:T(8,128)(2,1)S(1)} %add_convert_fusion), channel_id=1, replica_groups=mesh['section'=2,'ctx'=32,'tp'=8] {'tp'}, dimensions={1}, use_global_device_ids=true | all-gather | bytes 589824 | tf_op jit(solution)/shard_map/all_gather | solution.py:116
  735.8 1.5 fusion.31
  (58 shorter events, 20.7 us)
Async XLA Ops:
  7.2 1.6 copy-start
  7.2 47.1 %copy-start.6 = (bf16[1,128,512]{2,1,0:T(8,128)(2,1)S(1)}, bf16[1,128,512]{2,1,0:T(8,128)(2,1)}, u32[]{:S(2)}) copy-start(bf16[1,128,512]{2,1,0:T(8,128)(2,1)} %param.11) | copy-start | bytes 393220
  7.2 47.9 %copy-start.7 = (bf16[1,128,512]{2,1,0:T(8,128)(2,1)S(1)}, bf16[1,128,512]{2,1,0:T(8,128)(2,1)}, u32[]{:S(2)}) copy-start(bf16[1,128,512]{2,1,0:T(8,128)(2,1)} %param.12) | copy-start | bytes 393220
  7.2 48.8 %copy-start.11 = (s32[64]{0:T(128)S(1)}, s32[64]{0:T(128)}, u32[]{:S(2)}) copy-start(s32[64]{0:T(128)} %param.13) | copy-start | bytes 772
  7.2 171.6 %all-gather.3.cloned.1.call-start = ((), (), s32[]{:S(2)}) async-start(), calls=%async_computation.2 | async-start | bytes 2162688 | tf_op jit(solution)/shard_map/all_gather | solution.py:102
  43.2 294.7 %all-gather.5.cloned.1.call-start = ((), (), s32[]{:S(2)}) async-start(), calls=%async_computation.3 | async-start | bytes 2162688 | tf_op jit(solution)/shard_map/all_gather | solution.py:104
  43.3 9.2 %collective-permute-start = (bf16[128,256]{1,0:T(8,128)(2,1)}, bf16[128,256]{1,0:T(8,128)(2,1)S(1)}, u32[]{:S(2)}, u32[]{:S(2)}) collective-permute-start(bf16[128,256]{1,0:T(8,128)(2,1)} %dynamic-slice_convert_fusion), channel_id=1, source_target_pairs={{0,256},{256,0},{1,257},{257,1},{2,258},{258,2},{3,259},{259,3},{4... | collective-permute-start | bytes 196616 | tf_op jit(solution)/shard_map/ppermute | solution.py:15
  52.5 0.6 copy-start.10
  53.2 478.8 %reduce-scatter.9.cloned.1.call-start = ((), (), s32[]{:S(2)}) async-start(), calls=%async_computation.5 | async-start | bytes 2162688
  359.5 1.5 copy-start.3
  359.5 1.5 copy-start.5
  362.4 1.3 copy-start.9
  363.8 3.0 copy-start.1
  370.9 325.6 %reduce-scatter.7.cloned.1.call-start = ((), (), s32[]{:S(2)}) async-start(), calls=%async_computation.4 | async-start | bytes 2162688
  376.6 1.5 copy-start.4
  380.2 3.0 copy-start.2
  391.7 151.1 %copy-start.8 = (bf16[128,4,128]{2,0,1:T(8,128)(2,1)S(1)}, bf16[128,4,128]{2,0,1:T(8,128)(2,1)}, u32[]{:S(2)}) copy-start(bf16[128,4,128]{2,0,1:T(8,128)(2,1)} %get-tuple-element.26) | copy-start | bytes 393220
  532.9 164.5 %collective-permute-start.1 = (bf16[128,256]{0,1:T(8,128)(2,1)S(1)}, bf16[128,256]{0,1:T(8,128)(2,1)S(1)}, u32[]{:S(2)}, u32[]{:S(2)}) collective-permute-start(bf16[128,256]{0,1:T(8,128)(2,1)S(1)} %copy.91), channel_id=1, source_target_pairs={{0,256},{256,0},{1,257},{257,1},{2,258},{258,2},{3,259},{259,3},{4... | collective-permute-start | bytes 196616 | tf_op jit(solution)/shard_map/ppermute | solution.py:15
Sparse Core Ops, SparseCore 0:
  43.3 135.4 all-gather.2
  181.4 156.4 all-gather.4
  371.0 160.9 reduce-scatter.8
  534.9 161.5 reduce-scatter.6
where the time goes:
time: 745 us; the launch traced here: 744 us
  waiting for transfers between devices  555 us (74%)
  blocking collectives  70.5 us (9%)
  local copies, waits for them, and re-layouts  53 us (7%)
  matrix products  26.7 us (4%)
  between operations  14.1 us (2%)
  starting transfers between devices  13.8 us (2%)
  other arithmetic  10.9 us (1%)
    unnamed x6, waiting for transfers between devices  292 us
    all_gather x1, waiting for transfers between devices, on_device(): keys_b = lax.all_gather(kv_prev, 'ctx', axis=0, tiled=True)  144 us
    all_gather x1, waiting for transfers between devices, on_device(): keys_a = lax.all_gather(kv_own, 'ctx', axis=0, tiled=True)  117 us
    all_gather x1, blocking collectives, on_device(): lax.all_gather(section_sum.astype(jnp.bfloat16), 'tp', axis=1, tiled=True)  38.1 us
    psum x1, blocking collectives, on_device(): kv_whole = lax.psum(partial_value, 'tp').astype(jnp.bfloat16)  32.4 us
    unnamed x34, local copies, waits for them, and re-layouts  25.4 us
  transfers between devices with their start and end apart: 6, of which 5 were waited for; matrix products, arithmetic and copies ran while one was open for 7% of the time, Pallas kernels for 0%

commit v1 on v0

v1 whole, which is shorter than its diff:
```python
import math

import jax
import jax.numpy as jnp
from jax import lax
from jax.experimental import pallas as pl
from jax.experimental.pallas import tpu as pltpu
from jax.sharding import PartitionSpec as P

HEADS = 32
KVH = 4
HD = 128
SPAN = 64
N_SECTION = 2
N_Y = 8
N_Z = 4
N_CTX = 32
N_X = 4
N_CORE = 2
N_TP = 8
KEYS = N_CTX * SPAN * 2
ROWS = 128
HPD = 4
QROWS = HPD * ROWS
CHUNK = 512
NCHUNK = KEYS // CHUNK
EVERY = ("section", "ctx", "tp")
SCALE = HD ** (-0.5)
SCALE2 = SCALE * math.log2(math.e)
MIB = 1024 * 1024


def device_index(section, y, z, x, core):
    return (section * N_CTX + y * N_Z + z) * N_TP + x * N_CORE + core


def wide_groups():
    groups = []
    for section in range(N_SECTION):
        for x in range(N_X):
            for u in range(4):
                groups.append(
                    [device_index(section, u + 4 * w, z, x, 0) for w in range(2) for z in range(N_Z)]
                )
            for z in range(N_Z):
                groups.append([device_index(section, y, z, x, 1) for y in range(N_Y)])
    return groups


def narrow_groups():
    groups = []
    for section in range(N_SECTION):
        for x in range(N_X):
            for w in range(2):
                for z in range(N_Z):
                    groups.append([device_index(section, u + 4 * w, z, x, 0) for u in range(4)])
            for y in range(N_Y):
                groups.append([device_index(section, y, z, x, 1) for z in range(N_Z)])
    return groups


def block_owner(core):
    block = jnp.arange(N_CTX, dtype=jnp.int32)
    first, second = block // 8, block % 8
    owner_0 = (first + 4 * (second // 4)) * N_Z + second % 4
    owner_1 = second * N_Z + first
    return jnp.where(core == 0, owner_0, owner_1)


def swap_core(value):
    return lax.ppermute(value, "tp", [(i, i ^ 1) for i in range(N_TP)])


def swap_section(value):
    return lax.ppermute(value, "section", [(0, 1), (1, 0)])


def exchange(value, groups):
    return lax.all_to_all(value, EVERY, 0, 0, axis_index_groups=groups, tiled=True)


def project_kernel(x_ref, w_ref, o_ref):
    o_ref[0] = jnp.dot(x_ref[...], w_ref[...], preferred_element_type=jnp.float32)


def project(features, weight):
    return pl.pallas_call(
        project_kernel,
        grid=(KVH,),
        in_specs=[
            pl.BlockSpec((ROWS, 1024), lambda g: (0, 0)),
            pl.BlockSpec((1024, 2 * HD), lambda g: (0, g)),
        ],
        out_specs=pl.BlockSpec((1, ROWS, 2 * HD), lambda g: (g, 0, 0)),
        out_shape=jax.ShapeDtypeStruct((KVH, ROWS, 2 * HD), jnp.float32),
        name="kv_project",
    )(features, weight)


def unproject_kernel(g_ref, w_ref, o_ref):
    total = jnp.zeros((ROWS, 256), jnp.float32)
    for head in range(KVH):
        total += lax.dot_general(
            g_ref[head],
            w_ref[:, head * 256 : (head + 1) * 256],
            (((1,), (1,)), ((), ())),
            preferred_element_type=jnp.float32,
        )
    o_ref[...] = total.astype(jnp.bfloat16)


def unproject(kv_grads, weight):
    return pl.pallas_call(
        unproject_kernel,
        grid=(4,),
        in_specs=[
            pl.BlockSpec((KVH, ROWS, 2 * HD), lambda j: (0, 0, 0)),
            pl.BlockSpec((256, 1024), lambda j: (j, 0)),
        ],
        out_specs=pl.BlockSpec((ROWS, 256), lambda j: (0, j)),
        out_shape=jax.ShapeDtypeStruct((ROWS, 1024), jnp.bfloat16),
        name="kv_unproject",
    )(kv_grads, weight)


def nt(a, b):
    return lax.dot_general(a, b, (((1,), (1,)), ((), ())), preferred_element_type=jnp.float32)


def nn(a, b):
    return jnp.dot(a, b, preferred_element_type=jnp.float32)


def attention_kernel(
    base_ref, qa_ref, qgb_ref, ga_ref, own_ref, other_ref,
    oa_ref, gqa_ref, back_ref, gown_ref, gother_ref,
    q_s, g_s, kv_s, kt_s, vt_s, s_s, dk_s, dv_s,
):
    width = HPD * HD
    for head in range(HPD):
        cols = slice(head * HD, (head + 1) * HD)
        rows = slice(head * ROWS, (head + 1) * ROWS)
        q_s[0, rows, :] = qa_ref[:, cols]
        g_s[0, rows, :] = ga_ref[:, cols]
        q_s[1, rows, :] = qgb_ref[:, cols]
        g_s[1, rows, :] = qgb_ref[:, width + head * HD : width + (head + 1) * HD]
    half = KEYS // 2
    kv_s[:half, :] = own_ref[...]
    kv_s[half:, :] = other_ref[...]
    for c in range(NCHUNK):
        rows = slice(c * CHUNK, (c + 1) * CHUNK)
        kt_s[:, rows] = kv_s[rows, :HD].T
        vt_s[:, rows] = kv_s[rows, HD:].T

    lane = lax.broadcasted_iota(jnp.int32, (1, QROWS), 1) % ROWS
    q_pos = jnp.where(lane < SPAN, base_ref[64], base_ref[65]) + lane % SPAN
    key_row = lax.broadcasted_iota(jnp.int32, (SPAN, QROWS), 0)

    for unit in range(2):
        queries = q_s[unit]
        grads = g_s[unit]

        def scores(c, top):
            start = pl.multiple_of(c * CHUNK, CHUNK)
            tile = nt(kv_s[pl.ds(start, CHUNK), :HD], queries) * SCALE2
            for b in range(CHUNK // SPAN):
                base = base_ref[c * (CHUNK // SPAN) + b]
                part = jnp.where(
                    key_row <= q_pos - base, tile[b * SPAN : (b + 1) * SPAN], -1e30
                )
                s_s[pl.ds(start + b * SPAN, SPAN), :] = part
                top = jnp.maximum(top, jnp.max(part.reshape(SPAN // 8, 8, QROWS), axis=0))
            return top

        top = lax.fori_loop(0, NCHUNK, scores, jnp.full((8, QROWS), -1e30, jnp.float32))
        top = jnp.max(top, axis=0, keepdims=True)

        def mix(c, carry):
            total, out = carry
            start = pl.multiple_of(c * CHUNK, CHUNK)
            p = jnp.exp2(s_s[pl.ds(start, CHUNK), :] - top)
            total = total + jnp.sum(p.reshape(CHUNK // 8, 8, QROWS), axis=0)
            out = out + nn(vt_s[:, pl.ds(start, CHUNK)], p.astype(jnp.bfloat16))
            return total, out

        total, out = lax.fori_loop(
            0, NCHUNK, mix, (jnp.zeros((8, QROWS), jnp.float32), jnp.zeros((HD, QROWS), jnp.float32))
        )
        inverse = 1.0 / jnp.sum(total, axis=0, keepdims=True)
        mixed = (out * inverse).astype(jnp.bfloat16).astype(jnp.float32)
        delta = jnp.sum(mixed * grads.astype(jnp.float32).T, axis=0, keepdims=True)

        def back(c, grad_q):
            start = pl.multiple_of(c * CHUNK, CHUNK)
            rows = pl.ds(start, CHUNK)
            p = jnp.exp2(s_s[rows, :] - top) * inverse
            grad_p = nt(kv_s[rows, HD:], grads)
            grad_s = (p * (grad_p - delta)).astype(jnp.bfloat16)
            value_part = nn(p.astype(jnp.bfloat16), grads)
            key_part = nn(grad_s, queries)
            if unit == 0:
                dv_s[rows, :] = value_part
                dk_s[rows, :] = key_part
            else:
                dv_s[rows, :] += value_part
                dk_s[rows, :] += key_part
            return grad_q + nn(kt_s[:, rows], grad_s)

        grad_q = lax.fori_loop(0, NCHUNK, back, jnp.zeros((HD, QROWS), jnp.float32)) * SCALE
        for head in range(HPD):
            cols = slice(head * HD, (head + 1) * HD)
            lanes = slice(head * ROWS, (head + 1) * ROWS)
            o_head = mixed[:, lanes].T.astype(jnp.bfloat16)
            g_head = grad_q[:, lanes].T.astype(jnp.bfloat16)
            if unit == 0:
                oa_ref[:, cols] = o_head
                gqa_ref[:, cols] = g_head
            else:
                back_ref[:, cols] = o_head
                back_ref[:, width + head * HD : width + (head + 1) * HD] = g_head

    for ref, rows in ((gown_ref, slice(0, half)), (gother_ref, slice(half, KEYS))):
        ref[:, :HD] = (dk_s[rows, :] * SCALE).astype(jnp.bfloat16)
        ref[:, HD:] = dv_s[rows, :].astype(jnp.bfloat16)


def attention(bases, qa, qgb, ga, own, other):
    half = KEYS // 2
    bf = jnp.bfloat16
    whole = pl.BlockSpec(memory_space=pltpu.VMEM)
    return pl.pallas_call(
        attention_kernel,
        in_specs=[pl.BlockSpec(memory_space=pltpu.SMEM)] + [whole] * 5,
        out_specs=[whole] * 5,
        out_shape=[
            jax.ShapeDtypeStruct((ROWS, HPD * HD), bf),
            jax.ShapeDtypeStruct((ROWS, HPD * HD), bf),
            jax.ShapeDtypeStruct((ROWS, 2 * HPD * HD), bf),
            jax.ShapeDtypeStruct((half, 2 * HD), bf),
            jax.ShapeDtypeStruct((half, 2 * HD), bf),
        ],
        scratch_shapes=[
            pltpu.VMEM((2, QROWS, HD), bf),
            pltpu.VMEM((2, QROWS, HD), bf),
            pltpu.VMEM((KEYS, 2 * HD), bf),
            pltpu.VMEM((HD, KEYS), bf),
            pltpu.VMEM((HD, KEYS), bf),
            pltpu.VMEM((KEYS, QROWS), jnp.float32),
            pltpu.VMEM((KEYS, HD), jnp.float32),
            pltpu.VMEM((KEYS, HD), jnp.float32),
        ],
        compiler_params=pltpu.CompilerParams(vmem_limit_bytes=48 * MIB),
        cost_estimate=pl.CostEstimate(
            flops=24 * QROWS * KEYS * HD, bytes_accessed=6 * MIB, transcendentals=4 * QROWS * KEYS
        ),
        name="attention",
    )(bases, qa, qgb, ga, own, other)


def on_device(inputs, kv_weight, queries_a, queries_b, grads_a, grads_b, span_order):
    bf, f32 = jnp.bfloat16, jnp.float32
    weight = kv_weight[0]
    core = lax.axis_index("tp") % N_CORE
    ctx = lax.axis_index("ctx")
    wide, narrow = wide_groups(), narrow_groups()

    moved = swap_section(jnp.concatenate([queries_b[0], grads_b[0]], axis=1))

    partial = project(inputs[0], weight).reshape(N_TP * SPAN, 2 * HD)
    partial = lax.all_to_all(partial, "tp", 0, 0, tiled=True)
    own = jnp.sum(partial.reshape(N_TP, SPAN, 2 * HD), axis=0).astype(bf)

    own = exchange(jnp.broadcast_to(own[None], (8, SPAN, 2 * HD)), wide)
    own = exchange(jnp.broadcast_to(own[None], (4, 8, SPAN, 2 * HD)), narrow)
    own = own.reshape(N_CTX * SPAN, 2 * HD)
    other = swap_core(own)

    slots = jnp.concatenate(
        [2 * block_owner(core) + core, 2 * block_owner(1 - core) + 1 - core, 2 * ctx + jnp.arange(2)]
    )
    bases = span_order[slots] * SPAN

    out_a, grad_qa, back, grad_own, grad_other = attention(
        bases, queries_a[0], moved, grads_a[0], own, other
    )
    back = swap_section(back)
    grad_in = swap_core(grad_other)
    total = (grad_own.astype(f32) + grad_in.astype(f32)).astype(bf)
    total = exchange(total.reshape(4, 8, SPAN, 2 * HD), narrow)
    total = jnp.sum(total.astype(f32), axis=0).astype(bf)
    total = exchange(total, wide)
    total = jnp.sum(total.astype(f32), axis=0).astype(bf)
    total = lax.all_to_all(jnp.broadcast_to(total[None], (N_TP, SPAN, 2 * HD)), "tp", 0, 0, tiled=True)
    grad_x = unproject(total.reshape(KVH, ROWS, 2 * HD), weight)
    half = HPD * HD
    return (
        out_a[None],
        back[None, :, :half],
        grad_qa[None],
        back[None, :, half:],
        grad_x[None],
    )


def solution(mesh):
    split = P("section", "ctx", "tp")
    return jax.shard_map(
        on_device,
        mesh=mesh,
        in_specs=(split, P("section", "tp", None), split, split, split, split, P()),
        out_specs=(split,) * 5,
        check_vma=False,
    )
```

time: 745 us -> 168 us (0.23)
  waiting for transfers between devices: 555 us -> 18.3 us
  local copies, waits for them, and re-layouts: 53 us -> 3.51 us
  Pallas kernels: 0 us -> 32.1 us
  matrix products: 26.7 us -> 0 us
  starting transfers between devices: 13.8 us -> 39.2 us
  between operations: 14.1 us -> 0.8 us
  other arithmetic: 10.9 us -> 1.41 us
    unnamed x6 -> x0, waiting for transfers between devices: 292 us -> none
    all_gather x2 -> x0, waiting for transfers between devices: 261 us -> none  [the longest x1 144 us: on_device(): keys_b = lax.all_gather(kv_prev, 'ctx', axis=0, tiled=True)]
    all_to_all x0 -> x4, blocking collectives: none -> 70.4 us  [the longest x3 50.8 us: exchange(): lax.all_to_all(value, EVERY, 0, 0, axis_index_groups=groups, tiled=True)]
    all_gather x1 -> x0, blocking collectives: 38.1 us -> none  [on_device(): lax.all_gather(section_sum.astype(jnp.bfloat16), 'tp', axis=1, tiled=True)]
    psum x1 -> x0, blocking collectives: 32.4 us -> none  [on_device(): kv_whole = lax.psum(partial_value, 'tp').astype(jnp.bfloat16)]
    pallas_call x0 -> x3, Pallas kernels: none -> 32.1 us  [the longest x1 24.1 us: attention(): pl.pallas_call(attention_kernel, in_specs=[pl.BlockSpec(memory_space=pltp...]
    dot_general x14 -> x0, matrix products: 26.7 us -> none  [the longest x2 7.16 us: retrace(): jnp.einsum('ghrt,tge->rghe', grad_score, key_value[:, :, 0], preferred_el...]
    unnamed x34 -> x12, local copies, waits for them, and re-layouts: 25.4 us -> 0.72 us
  transfers between devices with their start and end apart: 6 -> 6, of which waited for: 5 -> 5; matrix products, arithmetic and copies ran while one was open for 7% -> 2% of each run, Pallas kernels for 0% -> 0%
where the time goes in v1:
time: 168 us; the launch traced here: 166 us
  blocking collectives  70.4 us (42%)
  starting transfers between devices  39.2 us (23%)
  Pallas kernels  32.1 us (19%)
  waiting for transfers between devices  18.3 us (11%)
  local copies, waits for them, and re-layouts  3.51 us (2%)
    all_to_all x3, blocking collectives, exchange(): lax.all_to_all(value, EVERY, 0, 0, axis_index_groups=groups, tiled=True)  50.8 us
    pallas_call x1, Pallas kernels, attention(): pl.pallas_call(attention_kernel, in_specs=[pl.BlockSpec(memory_space=pltp...  24.1 us
    all_to_all x1, blocking collectives, on_device(): partial = lax.all_to_all(partial, 'tp', 0, 0, tiled=True)  19.6 us
    ppermute x2, starting transfers between devices, swap_section(): return lax.ppermute(value, 'section', [(0, 1), (1, 0)])  14.1 us
    ppermute x2, starting transfers between devices, swap_core(): return lax.ppermute(value, 'tp', [(i, i ^ 1) for i in range(N_TP)])  13.2 us
    ppermute x2, waiting for transfers between devices, swap_section(): return lax.ppermute(value, 'section', [(0, 1), (1, 0)])  8.98 us
    all_to_all x1, starting transfers between devices, on_device(): lax.all_to_all(jnp.broadcast_to(total[None], (N_TP, SPAN, 2 * HD)), 'tp',...  8.49 us
    all_to_all x1, waiting for transfers between devices, on_device(): lax.all_to_all(jnp.broadcast_to(total[None], (N_TP, SPAN, 2 * HD)), 'tp',...  4.57 us
  transfers between devices with their start and end apart: 6, of which 5 were waited for; matrix products, arithmetic and copies ran while one was open for 2% of the time, Pallas kernels for 0%

profile of v1, /device:TPU:1, one launch (start us, length us, event | category | flops | bytes accessed | tf_op | source)
XLA Modules:
  0.0 165.7 jit_solution(15587906744804530854)
XLA Ops:
  0.6 0.0 copy-start
  0.6 4.0 %kv_project.1 = f32[4,128,256]{2,1,0:T(8,128)} custom-call(bf16[128,1024]{1,0:T(8,128)(2,1)} %bitcast.35, bf16[1024,1024]{1,0:T(8,128)(2,1)} %bitcast.29), custom_call_target="tpu_custom_call" | custom-call | tf_op jit(solution)/shard_map/kv_project/pallas_call | solution.py:87
  4.6 19.6 %all_to_all.34 = f32[8,64,256]{2,1,0:T(8,128)S(1)} all-to-all(f32[8,64,256]{2,1,0:T(8,128)} %bitcast.32), channel_id=1, replica_groups=mesh['section'=2,'ctx'=32,'tp'=8] {'tp'}, dimensions={0} | all-to-all | bytes 1048576 | tf_op jit(solution)/shard_map/all_to_all | solution.py:270
  24.3 0.0 copy-start.4
  24.3 0.0 copy-start.5
  24.3 11.9 %all_to_all.35 = bf16[8,64,256]{2,1,0:T(8,128)(2,1)S(1)} all-to-all(bf16[8,64,256]{2,1,0:T(8,128)(2,1)S(1)} %broadcast_in_dim.16), channel_id=1, replica_groups={{0,8,16,24,128,136,144,152},{32,40,48,56,160,168,176,184},{64,72,80,88,..., dimensions={0} | all-to-all | bytes 524288 | tf_op jit(solution)/shard_map/all_to_all | solution.py:79
  36.2 0.1 broadcast_in_dim.17
  36.3 21.5 %all_to_all.36 = bf16[4,8,64,256]{3,2,1,0:T(8,128)(2,1)S(1)} all-to-all(bf16[4,8,64,256]{3,2,1,0:T(8,128)(2,1)S(1)} %broadcast_in_dim.17), channel_id=1, replica_groups={{0,32,64,96},{8,40,72,104},{16,48,80,112},{24,56,88,120},{128,160,192,2..., dimensions={0} | all-to-all | bytes 2097152 | tf_op jit(solution)/shard_map/all_to_all | solution.py:79
  57.8 8.1 %collective-permute-start.1 = (bf16[2048,256]{1,0:T(8,128)(2,1)S(1)}, bf16[2048,256]{1,0:T(8,128)(2,1)S(1)}, u32[]{:S(2)}, u32[]{:S(2)}) collective-permute-start(bf16[2048,256]{1,0:T(8,128)(2,1)S(1)} %bitcast.25), channel_id=1, source_target_pairs={{0,1},{1,0},{2,3},{3,2},{4,5},{5,4},{6,7},{7,6},{8,9},{9,8},{10,11... | collective-permute-start | bytes 3145736 | tf_op jit(solution)/shard_map/ppermute | solution.py:71
  65.9 0.0 copy-done.4
  65.9 0.0 copy-done.5
  65.9 7.9 %collective-permute-start = (bf16[128,1024]{1,0:T(8,128)(2,1)S(1)}, bf16[128,1024]{1,0:T(8,128)(2,1)S(1)}, u32[]{:S(2)}, u32[]{:S(2)}) collective-permute-start(bf16[128,1024]{1,0:T(8,128)(2,1)S(1)} %pad_maximum_fusion), channel_id=1, source_target_pairs={{0,256},{256,0},{1,257},{257,1},{2,258},{258,2},{3,259},{259,3},{4... | collective-permute-start | bytes 786440 | tf_op jit(solution)/shard_map/ppermute | solution.py:75
  73.9 0.1 fusion.5
  74.0 1.2 gather_fusion
  75.3 7.7 %collective-permute-done.qgb_ref = bf16[128,1024]{1,0:T(8,128)(2,1)S(1)} collective-permute-done((bf16[128,1024]{1,0:T(8,128)(2,1)S(1)}, bf16[128,1024]{1,0:T(8,128)(2,1)S(1)}, u32[]{:S(2)}, u32[]{:S(2)}) %collective-permute-start) | collective-permute-done | bytes 262176 | tf_op jit(solution)/shard_map/ppermute | solution.py:75
  83.0 0.0 collective-permute-done.1.other_ref
  83.0 24.1 %attention.1 = (bf16[128,512]{1,0:T(8,128)(2,1)}, bf16[128,512]{1,0:T(8,128)(2,1)}, bf16[128,1024]{1,0:T(8,128)(2,1)S(1)}, bf16[2048,256]{1,0:T(8,128)(2,1)S(1)}, bf16[2048,256]{1,0:T(8,128)(2,1)S(1)}) custom-call(s32[66]{0:T(128)S(1)} %broadcast_multiply_fusion.base_ref, bf16[128,512]{1,0:T(8,128)(2,1)S(1)} %bitcast.27, ...), custom_call_target="tpu_custom_call" | custom-call | flops 6442450944 | bytes 6291456 | tf_op jit(solution)/shard_map/attention/pallas_call | solution.py:231
  107.1 5.1 %collective-permute-start.3 = (bf16[2048,256]{1,0:T(8,128)(2,1)S(1)}, bf16[2048,256]{1,0:T(8,128)(2,1)S(1)}, u32[]{:S(2)}, u32[]{:S(2)}) collective-permute-start(bf16[2048,256]{1,0:T(8,128)(2,1)S(1)} %get-tuple-element.14), channel_id=1, source_target_pairs={{0,1},{1,0},{2,3},{3,2},{4,5},{5,4},{6,7},{7,6},{8,9},{9,8},{10,11... | collective-permute-start | bytes 3145736 | tf_op jit(solution)/shard_map/ppermute | solution.py:71
  112.2 2.3 %collective-permute-done.3 = bf16[2048,256]{1,0:T(8,128)(2,1)S(1)} collective-permute-done((bf16[2048,256]{1,0:T(8,128)(2,1)S(1)}, bf16[2048,256]{1,0:T(8,128)(2,1)S(1)}, u32[]{:S(2)}, u32[]{:S(2)}) %collective-permute-start.3) | collective-permute-done | bytes 1048608 | tf_op jit(solution)/shard_map/ppermute | solution.py:71
  114.5 0.3 add_convert_fusion
  114.7 17.5 %all_to_all.37 = bf16[4,8,64,256]{3,2,1,0:T(8,128)(2,1)S(1)} all-to-all(bf16[4,8,64,256]{3,2,1,0:T(8,128)(2,1)S(1)} %bitcast.31), channel_id=1, replica_groups={{0,32,64,96},{8,40,72,104},{16,48,80,112},{24,56,88,120},{128,160,192,2..., dimensions={0} | all-to-all | bytes 2097152 | tf_op jit(solution)/shard_map/all_to_all | solution.py:79
  132.2 0.9 reduce_sum.34
  133.1 3.4 %all-to-all-start.4 = ((bf16[8,64,256]{2,1,0:T(8,128)(2,1)}), bf16[8,64,256]{2,1,0:T(8,128)(2,1)S(1)}, u32[]{:S(2)}, u32[]{:S(2)}) async-start(bf16[8,64,256]{2,1,0:T(8,128)(2,1)} %reduce_sum.34), calls=%async_computation.4 | async-start | bytes 524288 | tf_op jit(solution)/shard_map/all_to_all | solution.py:79
  136.6 6.2 %collective-permute-start.2 = (bf16[128,1024]{1,0:T(8,128)(2,1)S(1)}, bf16[128,1024]{1,0:T(8,128)(2,1)S(1)}, u32[]{:S(2)}, u32[]{:S(2)}) collective-permute-start(bf16[128,1024]{1,0:T(8,128)(2,1)S(1)} %get-tuple-element.11), channel_id=1, source_target_pairs={{0,256},{256,0},{1,257},{257,1},{2,258},{258,2},{3,259},{259,3},{4... | collective-permute-start | bytes 786440 | tf_op jit(solution)/shard_map/ppermute | solution.py:75
  142.7 2.4 %all-to-all-done.4 = bf16[8,64,256]{2,1,0:T(8,128)(2,1)S(1)} async-done(((bf16[8,64,256]{2,1,0:T(8,128)(2,1)}), bf16[8,64,256]{2,1,0:T(8,128)(2,1)S(1)}, u32[]{:S(2)}, u32[]{:S(2)}) %all-to-all-start.4) | async-done | bytes 262176 | tf_op jit(solution)/shard_map/all_to_all | solution.py:79
  145.2 0.7 broadcast_in_dim.40
  145.9 8.5 %all-to-all-start.5 = ((bf16[8,64,256]{2,1,0:T(8,128)(2,1)}), bf16[8,64,256]{2,1,0:T(8,128)(2,1)S(1)}, u32[]{:S(2)}, u32[]{:S(2)}) async-start(bf16[8,64,256]{2,1,0:T(8,128)(2,1)} %broadcast_in_dim.40), calls=%async_computation.5 | async-start | bytes 524288 | tf_op jit(solution)/shard_map/all_to_all | solution.py:293
  154.4 1.2 collective-permute-done.2
  155.7 0.7 slice_bitcast_fusion
  156.4 4.6 %all-to-all-done.5 = bf16[8,64,256]{2,1,0:T(8,128)(2,1)S(1)} async-done(((bf16[8,64,256]{2,1,0:T(8,128)(2,1)}), bf16[8,64,256]{2,1,0:T(8,128)(2,1)S(1)}, u32[]{:S(2)}, u32[]{:S(2)}) %all-to-all-start.5) | async-done | bytes 262176 | tf_op jit(solution)/shard_map/all_to_all | solution.py:293
  161.0 0.7 copy-done.3
  161.7 4.1 %kv_unproject.1 = bf16[128,1024]{1,0:T(8,128)(2,1)} custom-call(bf16[4,128,256]{2,1,0:T(8,128)(2,1)} %bitcast.33, bf16[1024,1024]{1,0:T(8,128)(2,1)} %bitcast.30), custom_call_target="tpu_custom_call" | custom-call | tf_op jit(solution)/shard_map/kv_unproject/pallas_call | solution.py:113
  (14 shorter events, 0.2 us)
Async XLA Ops:
  0.6 73.4 %copy-start = (s32[64]{0:T(128)S(1)}, s32[64]{0:T(128)}, u32[]{:S(2)}) copy-start(s32[64]{0:T(128)} %param.13) | copy-start | bytes 772
  24.3 41.6 %copy-start.4 = (bf16[1,128,512]{2,1,0:T(8,128)(2,1)S(1)}, bf16[1,128,512]{2,1,0:T(8,128)(2,1)}, u32[]{:S(2)}) copy-start(bf16[1,128,512]{2,1,0:T(8,128)(2,1)} %param.12) | copy-start | bytes 393220
  24.3 41.6 %copy-start.5 = (bf16[1,128,512]{2,1,0:T(8,128)(2,1)S(1)}, bf16[1,128,512]{2,1,0:T(8,128)(2,1)}, u32[]{:S(2)}) copy-start(bf16[1,128,512]{2,1,0:T(8,128)(2,1)} %param.10) | copy-start | bytes 393220
  36.2 46.8 %copy-start.1 = (bf16[1,128,512]{2,1,0:T(8,128)(2,1)S(1)}, bf16[1,128,512]{2,1,0:T(8,128)(2,1)}, u32[]{:S(2)}) copy-start(bf16[1,128,512]{2,1,0:T(8,128)(2,1)} %param.9) | copy-start | bytes 393220
  36.2 46.8 %copy-start.2 = (bf16[1,128,512]{2,1,0:T(8,128)(2,1)S(1)}, bf16[1,128,512]{2,1,0:T(8,128)(2,1)}, u32[]{:S(2)}) copy-start(bf16[1,128,512]{2,1,0:T(8,128)(2,1)} %param.11) | copy-start | bytes 393220
  57.8 25.2 %collective-permute-start.1 = (bf16[2048,256]{1,0:T(8,128)(2,1)S(1)}, bf16[2048,256]{1,0:T(8,128)(2,1)S(1)}, u32[]{:S(2)}, u32[]{:S(2)}) collective-permute-start(bf16[2048,256]{1,0:T(8,128)(2,1)S(1)} %bitcast.25), channel_id=1, source_target_pairs={{0,1},{1,0},{2,3},{3,2},{4,5},{5,4},{6,7},{7,6},{8,9},{9,8},{10,11... | collective-permute-start | bytes 3145736 | tf_op jit(solution)/shard_map/ppermute | solution.py:71
  65.9 17.1 %collective-permute-start = (bf16[128,1024]{1,0:T(8,128)(2,1)S(1)}, bf16[128,1024]{1,0:T(8,128)(2,1)S(1)}, u32[]{:S(2)}, u32[]{:S(2)}) collective-permute-start(bf16[128,1024]{1,0:T(8,128)(2,1)S(1)} %pad_maximum_fusion), channel_id=1, source_target_pairs={{0,256},{256,0},{1,257},{257,1},{2,258},{258,2},{3,259},{259,3},{4... | collective-permute-start | bytes 786440 | tf_op jit(solution)/shard_map/ppermute | solution.py:75
  107.1 7.4 %collective-permute-start.3 = (bf16[2048,256]{1,0:T(8,128)(2,1)S(1)}, bf16[2048,256]{1,0:T(8,128)(2,1)S(1)}, u32[]{:S(2)}, u32[]{:S(2)}) collective-permute-start(bf16[2048,256]{1,0:T(8,128)(2,1)S(1)} %get-tuple-element.14), channel_id=1, source_target_pairs={{0,1},{1,0},{2,3},{3,2},{4,5},{5,4},{6,7},{7,6},{8,9},{9,8},{10,11... | collective-permute-start | bytes 3145736 | tf_op jit(solution)/shard_map/ppermute | solution.py:71
  133.1 12.1 %all-to-all-start.4 = ((bf16[8,64,256]{2,1,0:T(8,128)(2,1)}), bf16[8,64,256]{2,1,0:T(8,128)(2,1)S(1)}, u32[]{:S(2)}, u32[]{:S(2)}) async-start(bf16[8,64,256]{2,1,0:T(8,128)(2,1)} %reduce_sum.34), calls=%async_computation.4 | async-start | bytes 524288 | tf_op jit(solution)/shard_map/all_to_all | solution.py:79
  136.6 19.1 %collective-permute-start.2 = (bf16[128,1024]{1,0:T(8,128)(2,1)S(1)}, bf16[128,1024]{1,0:T(8,128)(2,1)S(1)}, u32[]{:S(2)}, u32[]{:S(2)}) collective-permute-start(bf16[128,1024]{1,0:T(8,128)(2,1)S(1)} %get-tuple-element.11), channel_id=1, source_target_pairs={{0,256},{256,0},{1,257},{257,1},{2,258},{258,2},{3,259},{259,3},{4... | collective-permute-start | bytes 786440 | tf_op jit(solution)/shard_map/ppermute | solution.py:75
  145.9 15.0 %all-to-all-start.5 = ((bf16[8,64,256]{2,1,0:T(8,128)(2,1)}), bf16[8,64,256]{2,1,0:T(8,128)(2,1)S(1)}, u32[]{:S(2)}, u32[]{:S(2)}) async-start(bf16[8,64,256]{2,1,0:T(8,128)(2,1)} %broadcast_in_dim.40), calls=%async_computation.5 | async-start | bytes 524288 | tf_op jit(solution)/shard_map/all_to_all | solution.py:293
  161.0 0.7 copy-start.3

commit v2 on v1

--- a/solution.py
+++ b/solution.py
@@ -40,7 +40,7 @@
         for x in range(N_X):
             for u in range(4):
                 groups.append(
-                    [device_index(section, u + 4 * w, z, x, 0) for w in range(2) for z in range(N_Z)]
+                    [device_index(section, 2 * u + w, z, x, 0) for w in range(2) for z in range(N_Z)]
                 )
             for z in range(N_Z):
                 groups.append([device_index(section, y, z, x, 1) for y in range(N_Y)])
@@ -53,7 +53,7 @@
         for x in range(N_X):
             for w in range(2):
                 for z in range(N_Z):
-                    groups.append([device_index(section, u + 4 * w, z, x, 0) for u in range(4)])
+                    groups.append([device_index(section, 2 * u + w, z, x, 0) for u in range(4)])
             for y in range(N_Y):
                 groups.append([device_index(section, y, z, x, 1) for z in range(N_Z)])
     return groups
@@ -62,7 +62,7 @@
 def block_owner(core):
     block = jnp.arange(N_CTX, dtype=jnp.int32)
     first, second = block // 8, block % 8
-    owner_0 = (first + 4 * (second // 4)) * N_Z + second % 4
+    owner_0 = (2 * first + second // 4) * N_Z + second % 4
     owner_1 = second * N_Z + first
     return jnp.where(core == 0, owner_0, owner_1)
 
@@ -80,49 +80,47 @@
 
 
 def project_kernel(x_ref, w_ref, o_ref):
-    o_ref[0] = jnp.dot(x_ref[...], w_ref[...], preferred_element_type=jnp.float32)
+    for g in range(KVH):
+        o_ref[g] = nn(x_ref[...], w_ref[:, g * 2 * HD : (g + 1) * 2 * HD])
 
 
 def project(features, weight):
+    whole = pl.BlockSpec(memory_space=pltpu.VMEM)
     return pl.pallas_call(
         project_kernel,
-        grid=(KVH,),
-        in_specs=[
-            pl.BlockSpec((ROWS, 1024), lambda g: (0, 0)),
-            pl.BlockSpec((1024, 2 * HD), lambda g: (0, g)),
-        ],
-        out_specs=pl.BlockSpec((1, ROWS, 2 * HD), lambda g: (g, 0, 0)),
+        in_specs=[whole] * 2,
+        out_specs=whole,
         out_shape=jax.ShapeDtypeStruct((KVH, ROWS, 2 * HD), jnp.float32),
+        compiler_params=pltpu.CompilerParams(vmem_limit_bytes=16 * MIB),
         name="kv_project",
     )(features, weight)
 
 
 def unproject_kernel(g_ref, w_ref, o_ref):
-    total = jnp.zeros((ROWS, 256), jnp.float32)
-    for head in range(KVH):
-        total += lax.dot_general(
-            g_ref[head],
-            w_ref[:, head * 256 : (head + 1) * 256],
-            (((1,), (1,)), ((), ())),
-            preferred_element_type=jnp.float32,
-        )
+    total = nt(g_ref[0], w_ref[:, : 2 * HD])
+    for g in range(1, KVH):
+        total += nt(g_ref[g], w_ref[:, g * 2 * HD : (g + 1) * 2 * HD])
     o_ref[...] = total.astype(jnp.bfloat16)
 
 
 def unproject(kv_grads, weight):
+    whole = pl.BlockSpec(memory_space=pltpu.VMEM)
     return pl.pallas_call(
         unproject_kernel,
-        grid=(4,),
-        in_specs=[
-            pl.BlockSpec((KVH, ROWS, 2 * HD), lambda j: (0, 0, 0)),
-            pl.BlockSpec((256, 1024), lambda j: (j, 0)),
-        ],
-        out_specs=pl.BlockSpec((ROWS, 256), lambda j: (0, j)),
-        out_shape=jax.ShapeDtypeStruct((ROWS, 1024), jnp.bfloat16),
+        in_specs=[whole] * 2,
+        out_specs=whole,
+        out_shape=jax.ShapeDtypeStruct((ROWS, weight.shape[0]), jnp.bfloat16),
+        compiler_params=pltpu.CompilerParams(vmem_limit_bytes=16 * MIB),
         name="kv_unproject",
     )(kv_grads, weight)
 
 
+def loop(body, carry):
+    for c in range(NCHUNK):
+        carry = body(c, carry)
+    return carry
+
+
 def nt(a, b):
     return lax.dot_general(a, b, (((1,), (1,)), ((), ())), preferred_element_type=jnp.float32)
 
@@ -132,18 +130,17 @@
 
 
 def attention_kernel(
-    base_ref, qa_ref, qgb_ref, ga_ref, own_ref, other_ref,
+    base_ref, qa_ref, qb_ref, ga_ref, gb_ref, own_ref, other_ref,
     oa_ref, gqa_ref, back_ref, gown_ref, gother_ref,
     q_s, g_s, kv_s, kt_s, vt_s, s_s, dk_s, dv_s,
 ):
-    width = HPD * HD
     for head in range(HPD):
         cols = slice(head * HD, (head + 1) * HD)
         rows = slice(head * ROWS, (head + 1) * ROWS)
         q_s[0, rows, :] = qa_ref[:, cols]
         g_s[0, rows, :] = ga_ref[:, cols]
-        q_s[1, rows, :] = qgb_ref[:, cols]
-        g_s[1, rows, :] = qgb_ref[:, width + head * HD : width + (head + 1) * HD]
+        q_s[1, rows, :] = qb_ref[:, cols]
+        g_s[1, rows, :] = gb_ref[:, cols]
     half = KEYS // 2
     kv_s[:half, :] = own_ref[...]
     kv_s[half:, :] = other_ref[...]
@@ -161,7 +158,7 @@
         grads = g_s[unit]
 
         def scores(c, top):
-            start = pl.multiple_of(c * CHUNK, CHUNK)
+            start = c * CHUNK
             tile = nt(kv_s[pl.ds(start, CHUNK), :HD], queries) * SCALE2
             for b in range(CHUNK // SPAN):
                 base = base_ref[c * (CHUNK // SPAN) + b]
@@ -172,26 +169,25 @@
                 top = jnp.maximum(top, jnp.max(part.reshape(SPAN // 8, 8, QROWS), axis=0))
             return top
 
-        top = lax.fori_loop(0, NCHUNK, scores, jnp.full((8, QROWS), -1e30, jnp.float32))
+        top = loop(scores, jnp.full((8, QROWS), -1e30, jnp.float32))
         top = jnp.max(top, axis=0, keepdims=True)
 
         def mix(c, carry):
             total, out = carry
-            start = pl.multiple_of(c * CHUNK, CHUNK)
+            start = c * CHUNK
             p = jnp.exp2(s_s[pl.ds(start, CHUNK), :] - top)
             total = total + jnp.sum(p.reshape(CHUNK // 8, 8, QROWS), axis=0)
             out = out + nn(vt_s[:, pl.ds(start, CHUNK)], p.astype(jnp.bfloat16))
             return total, out
 
-        total, out = lax.fori_loop(
-            0, NCHUNK, mix, (jnp.zeros((8, QROWS), jnp.float32), jnp.zeros((HD, QROWS), jnp.float32))
+        total, out = loop(mix, (jnp.zeros((8, QROWS), jnp.float32), jnp.zeros((HD, QROWS), jnp.float32))
         )
         inverse = 1.0 / jnp.sum(total, axis=0, keepdims=True)
         mixed = (out * inverse).astype(jnp.bfloat16).astype(jnp.float32)
         delta = jnp.sum(mixed * grads.astype(jnp.float32).T, axis=0, keepdims=True)
 
         def back(c, grad_q):
-            start = pl.multiple_of(c * CHUNK, CHUNK)
+            start = c * CHUNK
             rows = pl.ds(start, CHUNK)
             p = jnp.exp2(s_s[rows, :] - top) * inverse
             grad_p = nt(kv_s[rows, HD:], grads)
@@ -206,7 +202,7 @@
                 dk_s[rows, :] += key_part
             return grad_q + nn(kt_s[:, rows], grad_s)
 
-        grad_q = lax.fori_loop(0, NCHUNK, back, jnp.zeros((HD, QROWS), jnp.float32)) * SCALE
+        grad_q = loop(back, jnp.zeros((HD, QROWS), jnp.float32)) * SCALE
         for head in range(HPD):
             cols = slice(head * HD, (head + 1) * HD)
             lanes = slice(head * ROWS, (head + 1) * ROWS)
@@ -217,20 +213,20 @@
                 gqa_ref[:, cols] = g_head
             else:
                 back_ref[:, cols] = o_head
-                back_ref[:, width + head * HD : width + (head + 1) * HD] = g_head
+                back_ref[:, QROWS + head * HD : QROWS + (head + 1) * HD] = g_head
 
     for ref, rows in ((gown_ref, slice(0, half)), (gother_ref, slice(half, KEYS))):
         ref[:, :HD] = (dk_s[rows, :] * SCALE).astype(jnp.bfloat16)
         ref[:, HD:] = dv_s[rows, :].astype(jnp.bfloat16)
 
 
-def attention(bases, qa, qgb, ga, own, other):
+def attention(bases, qa, qb, ga, gb, own, other):
     half = KEYS // 2
     bf = jnp.bfloat16
     whole = pl.BlockSpec(memory_space=pltpu.VMEM)
     return pl.pallas_call(
         attention_kernel,
-        in_specs=[pl.BlockSpec(memory_space=pltpu.SMEM)] + [whole] * 5,
+        in_specs=[pl.BlockSpec(memory_space=pltpu.SMEM)] + [whole] * 6,
         out_specs=[whole] * 5,
         out_shape=[
             jax.ShapeDtypeStruct((ROWS, HPD * HD), bf),
@@ -249,12 +245,12 @@
             pltpu.VMEM((KEYS, HD), jnp.float32),
             pltpu.VMEM((KEYS, HD), jnp.float32),
         ],
-        compiler_params=pltpu.CompilerParams(vmem_limit_bytes=48 * MIB),
+        compiler_params=pltpu.CompilerParams(vmem_limit_bytes=36 * MIB),
         cost_estimate=pl.CostEstimate(
             flops=24 * QROWS * KEYS * HD, bytes_accessed=6 * MIB, transcendentals=4 * QROWS * KEYS
         ),
         name="attention",
-    )(bases, qa, qgb, ga, own, other)
+    )(bases, qa, qb, ga, gb, own, other)
 
 
 def on_device(inputs, kv_weight, queries_a, queries_b, grads_a, grads_b, span_order):
@@ -264,13 +260,16 @@
     ctx = lax.axis_index("ctx")
     wide, narrow = wide_groups(), narrow_groups()
 
-    moved = swap_section(jnp.concatenate([queries_b[0], grads_b[0]], axis=1))
-
-    partial = project(inputs[0], weight).reshape(N_TP * SPAN, 2 * HD)
-    partial = lax.all_to_all(partial, "tp", 0, 0, tiled=True)
-    own = jnp.sum(partial.reshape(N_TP, SPAN, 2 * HD), axis=0).astype(bf)
-
+    moved_q = swap_section(queries_b[0])
+    moved_g = swap_section(grads_b[0])
+
+    partial = project(inputs[0], weight)
+    partial = lax.all_to_all(partial.reshape(N_TP, SPAN, 2 * HD), "tp", 0, 0, tiled=True)
+    own = jnp.sum(partial, axis=0).astype(bf)
+
+    own, moved_q = lax.optimization_barrier((own, moved_q))
     own = exchange(jnp.broadcast_to(own[None], (8, SPAN, 2 * HD)), wide)
+    own, moved_g = lax.optimization_barrier((own, moved_g))
     own = exchange(jnp.broadcast_to(own[None], (4, 8, SPAN, 2 * HD)), narrow)
     own = own.reshape(N_CTX * SPAN, 2 * HD)
     other = swap_core(own)
@@ -281,7 +280,7 @@
     bases = span_order[slots] * SPAN
 
     out_a, grad_qa, back, grad_own, grad_other = attention(
-        bases, queries_a[0], moved, grads_a[0], own, other
+        bases, queries_a[0], moved_q, grads_a[0], moved_g, own, other
     )
     back = swap_section(back)
     grad_in = swap_core(grad_other)

time: 168 us -> 160 us (0.952)
  blocking collectives: 70.4 us -> 43.4 us
  starting transfers between devices: 39.2 us -> 63.9 us
  Pallas kernels: 32.1 us -> 19.1 us
  waiting for transfers between devices: 18.3 us -> 22.9 us
  local copies, waits for them, and re-layouts: 3.51 us -> 6.06 us
    all_to_all x1 -> x0, blocking collectives: 19.6 us -> none  [on_device(): partial = lax.all_to_all(partial, 'tp', 0, 0, tiled=True)]
    all_to_all x0 -> x1, starting transfers between devices: none -> 10.3 us  [on_device(): lax.all_to_all(partial.reshape(N_TP, SPAN, 2 * HD), 'tp', 0, 0, tiled=True)]
    all_to_all x1, starting transfers between devices: 8.49 us -> 16.6 us  [on_device(): lax.all_to_all(jnp.broadcast_to(total[None], (N_TP, SPAN, 2 * HD)), 'tp',...]
    pallas_call x1, Pallas kernels: 24.1 us -> 16.4 us  [attention(): pl.pallas_call(attention_kernel, in_specs=[pl.BlockSpec(memory_space=pltp...]
    all_to_all x3 -> x2, blocking collectives: 50.8 us -> 43.4 us  [exchange(): lax.all_to_all(value, EVERY, 0, 0, axis_index_groups=groups, tiled=True)]
    all_to_all x1 -> x2, starting transfers between devices: 3.41 us -> 9.48 us  [exchange(): lax.all_to_all(value, EVERY, 0, 0, axis_index_groups=groups, tiled=True)]
    pallas_call x2, Pallas kernels: 8.05 us -> 2.76 us  [the longest x1 1.52 us: unproject(): pl.pallas_call(unproject_kernel, in_specs=[whole] * 2, out_specs=whole, o...]
    ppermute x2 -> x3, starting transfers between devices: 14.1 us -> 19.3 us  [swap_section(): return lax.ppermute(value, 'section', [(0, 1), (1, 0)])]
  transfers between devices with their start and end apart: 6 -> 9, of which waited for: 5 -> 7; matrix products, arithmetic and copies ran while one was open for 2% -> 2% of each run, Pallas kernels for 0% -> 0%
where the time goes in v2:
time: 160 us; the launch traced here: 159 us
  starting transfers between devices  63.9 us (40%)
  blocking collectives  43.4 us (27%)
  waiting for transfers between devices  22.9 us (14%)
  Pallas kernels  19.1 us (12%)
  local copies, waits for them, and re-layouts  6.06 us (4%)
  other arithmetic  2.84 us (2%)
    all_to_all x2, blocking collectives, exchange(): lax.all_to_all(value, EVERY, 0, 0, axis_index_groups=groups, tiled=True)  43.4 us
    ppermute x3, starting transfers between devices, swap_section(): return lax.ppermute(value, 'section', [(0, 1), (1, 0)])  19.3 us
    all_to_all x1, starting transfers between devices, on_device(): lax.all_to_all(jnp.broadcast_to(total[None], (N_TP, SPAN, 2 * HD)), 'tp',...  16.6 us
    pallas_call x1, Pallas kernels, attention(): pl.pallas_call(attention_kernel, in_specs=[pl.BlockSpec(memory_space=pltp...  16.4 us
    all_to_all x1, starting transfers between devices, on_device(): lax.all_to_all(partial.reshape(N_TP, SPAN, 2 * HD), 'tp', 0, 0, tiled=True)  10.3 us
    all_to_all x2, starting transfers between devices, exchange(): lax.all_to_all(value, EVERY, 0, 0, axis_index_groups=groups, tiled=True)  9.48 us
    ppermute x2, starting transfers between devices, swap_core(): return lax.ppermute(value, 'tp', [(i, i ^ 1) for i in range(N_TP)])  8.34 us
    ppermute x3, waiting for transfers between devices, swap_section(): return lax.ppermute(value, 'section', [(0, 1), (1, 0)])  6.24 us
  transfers between devices with their start and end apart: 9, of which 7 were waited for; matrix products, arithmetic and copies ran while one was open for 2% of the time, Pallas kernels for 0%

profile of v2, /device:TPU:1, one launch (start us, length us, event | category | flops | bytes accessed | tf_op | source)
XLA Modules:
  0.0 159.1 jit_solution(10208296121182873814)
XLA Ops:
  0.6 0.0 copy-start
  0.7 1.6 copy-done.1
  2.2 0.9 copy-done.3
  3.2 1.2 kv_project.1
  4.4 10.3 %all-to-all-start = ((f32[8,64,256]{2,1,0:T(8,128)}), f32[8,64,256]{2,1,0:T(8,128)S(1)}, u32[]{:S(2)}, u32[]{:S(2)}) async-start(f32[8,64,256]{2,1,0:T(8,128)} %bitcast.7), calls=%async_computation | async-start | bytes 1048576 | tf_op jit(solution)/shard_map/all_to_all | solution.py:267
  14.7 6.2 %collective-permute-start = (bf16[128,512]{1,0:T(8,128)(2,1)S(1)}, bf16[128,512]{1,0:T(8,128)(2,1)S(1)}, u32[]{:S(2)}, u32[]{:S(2)}) collective-permute-start(bf16[128,512]{1,0:T(8,128)(2,1)S(1)} %bitcast.35), channel_id=1, source_target_pairs={{0,256},{256,0},{1,257},{257,1},{2,258},{258,2},{3,259},{259,3},{4... | collective-permute-start | bytes 393224 | tf_op jit(solution)/shard_map/ppermute | solution.py:75
  20.9 3.3 %all-to-all-done = f32[8,64,256]{2,1,0:T(8,128)S(1)} async-done(((f32[8,64,256]{2,1,0:T(8,128)}), f32[8,64,256]{2,1,0:T(8,128)S(1)}, u32[]{:S(2)}, u32[]{:S(2)}) %all-to-all-start) | async-done | bytes 524320 | tf_op jit(solution)/shard_map/all_to_all | solution.py:267
  24.2 1.2 collective-permute-done.qb_ref
  25.5 0.7 broadcast_in_dim.16
  26.2 6.1 %all-to-all-start.1 = ((bf16[8,64,256]{2,1,0:T(8,128)(2,1)}), bf16[8,64,256]{2,1,0:T(8,128)(2,1)S(1)}, u32[]{:S(2)}, u32[]{:S(2)}) async-start(bf16[8,64,256]{2,1,0:T(8,128)(2,1)} %broadcast_in_dim.16), calls=%async_computation.1 | async-start | bytes 524288 | tf_op jit(solution)/shard_map/all_to_all | solution.py:79
  32.3 7.3 %collective-permute-start.1 = (bf16[128,512]{1,0:T(8,128)(2,1)S(1)}, bf16[128,512]{1,0:T(8,128)(2,1)S(1)}, u32[]{:S(2)}, u32[]{:S(2)}) collective-permute-start(bf16[128,512]{1,0:T(8,128)(2,1)S(1)} %bitcast.36), channel_id=1, source_target_pairs={{0,256},{256,0},{1,257},{257,1},{2,258},{258,2},{3,259},{259,3},{4... | collective-permute-start | bytes 393224 | tf_op jit(solution)/shard_map/ppermute | solution.py:75
  39.6 5.0 %collective-permute-done.1.gb_ref = bf16[128,512]{1,0:T(8,128)(2,1)S(1)} collective-permute-done((bf16[128,512]{1,0:T(8,128)(2,1)S(1)}, bf16[128,512]{1,0:T(8,128)(2,1)S(1)}, u32[]{:S(2)}, u32[]{:S(2)}) %collective-permute-start.1) | collective-permute-done | bytes 131104 | tf_op jit(solution)/shard_map/ppermute | solution.py:75
  44.6 0.1 broadcast_in_dim.17
  44.8 22.3 %all_to_all.30 = bf16[4,8,64,256]{3,2,1,0:T(8,128)(2,1)S(1)} all-to-all(bf16[4,8,64,256]{3,2,1,0:T(8,128)(2,1)S(1)} %broadcast_in_dim.17), channel_id=1, replica_groups={{0,64,128,192},{8,72,136,200},{16,80,144,208},{24,88,152,216},{32,96,16..., dimensions={0} | all-to-all | bytes 2097152 | tf_op jit(solution)/shard_map/all_to_all | solution.py:79
  67.0 6.1 %collective-permute-start.2 = (bf16[2048,256]{1,0:T(8,128)(2,1)S(1)}, bf16[2048,256]{1,0:T(8,128)(2,1)S(1)}, u32[]{:S(2)}, u32[]{:S(2)}) collective-permute-start(bf16[2048,256]{1,0:T(8,128)(2,1)S(1)} %bitcast.28), channel_id=1, source_target_pairs={{0,1},{1,0},{2,3},{3,2},{4,5},{5,4},{6,7},{7,6},{8,9},{9,8},{10,11... | collective-permute-start | bytes 3145736 | tf_op jit(solution)/shard_map/ppermute | solution.py:71
  73.1 0.1 fusion.5
  73.2 1.2 gather_fusion
  74.5 0.9 collective-permute-done.2.other_ref
  75.4 16.4 %attention.1 = (bf16[128,512]{1,0:T(8,128)(2,1)}, bf16[128,512]{1,0:T(8,128)(2,1)}, bf16[128,1024]{1,0:T(8,128)(2,1)S(1)}, bf16[2048,256]{1,0:T(8,128)(2,1)S(1)}, bf16[2048,256]{1,0:T(8,128)(2,1)S(1)}) custom-call(s32[66]{0:T(128)S(1)} %broadcast_multiply_fusion.base_ref, bf16[128,512]{1,0:T(8,128)(2,1)S(1)} %bitcast.31, ...), custom_call_target="tpu_custom_call" | custom-call | flops 6442450944 | bytes 6291456 | tf_op jit(solution)/shard_map/attention/pallas_call | solution.py:227
  91.7 2.3 %collective-permute-start.4 = (bf16[2048,256]{1,0:T(8,128)(2,1)S(1)}, bf16[2048,256]{1,0:T(8,128)(2,1)S(1)}, u32[]{:S(2)}, u32[]{:S(2)}) collective-permute-start(bf16[2048,256]{1,0:T(8,128)(2,1)S(1)} %get-tuple-element.22), channel_id=1, source_target_pairs={{0,1},{1,0},{2,3},{3,2},{4,5},{5,4},{6,7},{7,6},{8,9},{9,8},{10,11... | collective-permute-start | bytes 3145736 | tf_op jit(solution)/shard_map/ppermute | solution.py:71
  94.0 2.3 %collective-permute-done.4 = bf16[2048,256]{1,0:T(8,128)(2,1)S(1)} collective-permute-done((bf16[2048,256]{1,0:T(8,128)(2,1)S(1)}, bf16[2048,256]{1,0:T(8,128)(2,1)S(1)}, u32[]{:S(2)}, u32[]{:S(2)}) %collective-permute-start.4) | collective-permute-done | bytes 1048608 | tf_op jit(solution)/shard_map/ppermute | solution.py:71
  96.3 0.3 add_convert_fusion
  96.6 21.1 %all_to_all.31 = bf16[4,8,64,256]{3,2,1,0:T(8,128)(2,1)} all-to-all(bf16[4,8,64,256]{3,2,1,0:T(8,128)(2,1)S(1)} %bitcast.33), channel_id=1, replica_groups={{0,64,128,192},{8,72,136,200},{16,80,144,208},{24,88,152,216},{32,96,16..., dimensions={0} | all-to-all | bytes 2097152 | tf_op jit(solution)/shard_map/all_to_all | solution.py:79
  117.7 2.3 %reduce_sum.34 = bf16[8,64,256]{2,1,0:T(8,128)(2,1)} reduce(bf16[4,8,64,256]{3,2,1,0:T(8,128)(2,1)} %all_to_all.31, bf16[]{:T(256)} %constant.91.clone.1), dimensions={0}, to_apply=%region_1.2 | reduce | flops 393216 | bytes 1310722 | tf_op jit(solution)/shard_map/reduce_sum | solution.py:289
  120.1 3.4 %all-to-all-start.4 = ((bf16[8,64,256]{2,1,0:T(8,128)(2,1)}), bf16[8,64,256]{2,1,0:T(8,128)(2,1)S(1)}, u32[]{:S(2)}, u32[]{:S(2)}) async-start(bf16[8,64,256]{2,1,0:T(8,128)(2,1)} %reduce_sum.34), calls=%async_computation.4 | async-start | bytes 524288 | tf_op jit(solution)/shard_map/all_to_all | solution.py:79
  123.5 5.8 %collective-permute-start.3 = (bf16[128,1024]{1,0:T(8,128)(2,1)S(1)}, bf16[128,1024]{1,0:T(8,128)(2,1)S(1)}, u32[]{:S(2)}, u32[]{:S(2)}) collective-permute-start(bf16[128,1024]{1,0:T(8,128)(2,1)S(1)} %get-tuple-element.19), channel_id=1, source_target_pairs={{0,256},{256,0},{1,257},{257,1},{2,258},{258,2},{3,259},{259,3},{4... | collective-permute-start | bytes 786440 | tf_op jit(solution)/shard_map/ppermute | solution.py:75
  129.3 4.4 %all-to-all-done.4 = bf16[8,64,256]{2,1,0:T(8,128)(2,1)S(1)} async-done(((bf16[8,64,256]{2,1,0:T(8,128)(2,1)}), bf16[8,64,256]{2,1,0:T(8,128)(2,1)S(1)}, u32[]{:S(2)}, u32[]{:S(2)}) %all-to-all-start.4) | async-done | bytes 262176 | tf_op jit(solution)/shard_map/all_to_all | solution.py:79
  133.7 0.7 broadcast_in_dim.40
  134.5 16.6 %all-to-all-start.5 = ((bf16[8,64,256]{2,1,0:T(8,128)(2,1)}), bf16[8,64,256]{2,1,0:T(8,128)(2,1)S(1)}, u32[]{:S(2)}, u32[]{:S(2)}) async-start(bf16[8,64,256]{2,1,0:T(8,128)(2,1)} %broadcast_in_dim.40), calls=%async_computation.5 | async-start | bytes 524288 | tf_op jit(solution)/shard_map/all_to_all | solution.py:292
  151.0 0.7 slice_bitcast_fusion
  151.7 5.8 %all-to-all-done.5 = bf16[8,64,256]{2,1,0:T(8,128)(2,1)S(1)} async-done(((bf16[8,64,256]{2,1,0:T(8,128)(2,1)}), bf16[8,64,256]{2,1,0:T(8,128)(2,1)S(1)}, u32[]{:S(2)}, u32[]{:S(2)}) %all-to-all-start.5) | async-done | bytes 262176 | tf_op jit(solution)/shard_map/all_to_all | solution.py:292
  157.5 1.5 kv_unproject.1
  (21 shorter events, 0.1 us)
Async XLA Ops:
  0.6 72.6 %copy-start = (s32[64]{0:T(128)S(1)}, s32[64]{0:T(128)}, u32[]{:S(2)}) copy-start(s32[64]{0:T(128)} %param.13) | copy-start | bytes 772
  0.6 1.6 %copy-start.1 = (bf16[1,1024,1024]{2,1,0:T(8,128)(2,1)S(1)}, bf16[1,1024,1024]{2,1,0:T(8,128)(2,1)}, u32[]{:S(2)}) copy-start(bf16[1,1024,1024]{2,1,0:T(8,128)(2,1)} %param.8) | copy-start | bytes 6291460
  2.2 0.9 copy-start.3
  3.2 11.5 %copy-start.6 = (bf16[1,128,512]{2,1,0:T(8,128)(2,1)S(1)}, bf16[1,128,512]{2,1,0:T(8,128)(2,1)}, u32[]{:S(2)}) copy-start(bf16[1,128,512]{2,1,0:T(8,128)(2,1)} %param.10) | copy-start | bytes 393220
  3.2 29.1 %copy-start.7 = (bf16[1,128,512]{2,1,0:T(8,128)(2,1)S(1)}, bf16[1,128,512]{2,1,0:T(8,128)(2,1)}, u32[]{:S(2)}) copy-start(bf16[1,128,512]{2,1,0:T(8,128)(2,1)} %param.12) | copy-start | bytes 393220
  4.4 19.8 %all-to-all-start = ((f32[8,64,256]{2,1,0:T(8,128)}), f32[8,64,256]{2,1,0:T(8,128)S(1)}, u32[]{:S(2)}, u32[]{:S(2)}) async-start(f32[8,64,256]{2,1,0:T(8,128)} %bitcast.7), calls=%async_computation | async-start | bytes 1048576 | tf_op jit(solution)/shard_map/all_to_all | solution.py:267
  14.7 10.8 %collective-permute-start = (bf16[128,512]{1,0:T(8,128)(2,1)S(1)}, bf16[128,512]{1,0:T(8,128)(2,1)S(1)}, u32[]{:S(2)}, u32[]{:S(2)}) collective-permute-start(bf16[128,512]{1,0:T(8,128)(2,1)S(1)} %bitcast.35), channel_id=1, source_target_pairs={{0,256},{256,0},{1,257},{257,1},{2,258},{258,2},{3,259},{259,3},{4... | collective-permute-start | bytes 393224 | tf_op jit(solution)/shard_map/ppermute | solution.py:75
  26.2 18.5 %all-to-all-start.1 = ((bf16[8,64,256]{2,1,0:T(8,128)(2,1)}), bf16[8,64,256]{2,1,0:T(8,128)(2,1)S(1)}, u32[]{:S(2)}, u32[]{:S(2)}) async-start(bf16[8,64,256]{2,1,0:T(8,128)(2,1)} %broadcast_in_dim.16), calls=%async_computation.1 | async-start | bytes 524288 | tf_op jit(solution)/shard_map/all_to_all | solution.py:79
  32.3 43.1 %copy-start.4 = (bf16[1,128,512]{2,1,0:T(8,128)(2,1)S(1)}, bf16[1,128,512]{2,1,0:T(8,128)(2,1)}, u32[]{:S(2)}) copy-start(bf16[1,128,512]{2,1,0:T(8,128)(2,1)} %param.9) | copy-start | bytes 393220
  32.3 43.1 %copy-start.5 = (bf16[1,128,512]{2,1,0:T(8,128)(2,1)S(1)}, bf16[1,128,512]{2,1,0:T(8,128)(2,1)}, u32[]{:S(2)}) copy-start(bf16[1,128,512]{2,1,0:T(8,128)(2,1)} %param.11) | copy-start | bytes 393220
  32.3 12.4 %collective-permute-start.1 = (bf16[128,512]{1,0:T(8,128)(2,1)S(1)}, bf16[128,512]{1,0:T(8,128)(2,1)S(1)}, u32[]{:S(2)}, u32[]{:S(2)}) collective-permute-start(bf16[128,512]{1,0:T(8,128)(2,1)S(1)} %bitcast.36), channel_id=1, source_target_pairs={{0,256},{256,0},{1,257},{257,1},{2,258},{258,2},{3,259},{259,3},{4... | collective-permute-start | bytes 393224 | tf_op jit(solution)/shard_map/ppermute | solution.py:75
  67.0 8.3 %collective-permute-start.2 = (bf16[2048,256]{1,0:T(8,128)(2,1)S(1)}, bf16[2048,256]{1,0:T(8,128)(2,1)S(1)}, u32[]{:S(2)}, u32[]{:S(2)}) collective-permute-start(bf16[2048,256]{1,0:T(8,128)(2,1)S(1)} %bitcast.28), channel_id=1, source_target_pairs={{0,1},{1,0},{2,3},{3,2},{4,5},{5,4},{6,7},{7,6},{8,9},{9,8},{10,11... | collective-permute-start | bytes 3145736 | tf_op jit(solution)/shard_map/ppermute | solution.py:71
  91.7 4.5 %collective-permute-start.4 = (bf16[2048,256]{1,0:T(8,128)(2,1)S(1)}, bf16[2048,256]{1,0:T(8,128)(2,1)S(1)}, u32[]{:S(2)}, u32[]{:S(2)}) collective-permute-start(bf16[2048,256]{1,0:T(8,128)(2,1)S(1)} %get-tuple-element.22), channel_id=1, source_target_pairs={{0,1},{1,0},{2,3},{3,2},{4,5},{5,4},{6,7},{7,6},{8,9},{9,8},{10,11... | collective-permute-start | bytes 3145736 | tf_op jit(solution)/shard_map/ppermute | solution.py:71
  117.7 39.8 %copy-start.2 = (bf16[1,1024,1024]{2,1,0:T(8,128)(2,1)S(1)}, bf16[1,1024,1024]{2,1,0:T(8,128)(2,1)}, u32[]{:S(2)}) copy-start(bf16[1,1024,1024]{2,1,0:T(8,128)(2,1)} %param.8) | copy-start | bytes 6291460
  120.1 13.6 %all-to-all-start.4 = ((bf16[8,64,256]{2,1,0:T(8,128)(2,1)}), bf16[8,64,256]{2,1,0:T(8,128)(2,1)S(1)}, u32[]{:S(2)}, u32[]{:S(2)}) async-start(bf16[8,64,256]{2,1,0:T(8,128)(2,1)} %reduce_sum.34), calls=%async_computation.4 | async-start | bytes 524288 | tf_op jit(solution)/shard_map/all_to_all | solution.py:79
  123.5 27.5 %collective-permute-start.3 = (bf16[128,1024]{1,0:T(8,128)(2,1)S(1)}, bf16[128,1024]{1,0:T(8,128)(2,1)S(1)}, u32[]{:S(2)}, u32[]{:S(2)}) collective-permute-start(bf16[128,1024]{1,0:T(8,128)(2,1)S(1)} %get-tuple-element.19), channel_id=1, source_target_pairs={{0,256},{256,0},{1,257},{257,1},{2,258},{258,2},{3,259},{259,3},{4... | collective-permute-start | bytes 786440 | tf_op jit(solution)/shard_map/ppermute | solution.py:75
  134.5 23.1 %all-to-all-start.5 = ((bf16[8,64,256]{2,1,0:T(8,128)(2,1)}), bf16[8,64,256]{2,1,0:T(8,128)(2,1)S(1)}, u32[]{:S(2)}, u32[]{:S(2)}) async-start(bf16[8,64,256]{2,1,0:T(8,128)(2,1)} %broadcast_in_dim.40), calls=%async_computation.5 | async-start | bytes 524288 | tf_op jit(solution)/shard_map/all_to_all | solution.py:292

commit v3 on v2

--- a/solution.py
+++ b/solution.py
@@ -34,13 +34,17 @@
     return (section * N_CTX + y * N_Z + z) * N_TP + x * N_CORE + core
 
 
+def fold(u, w):
+    return u + w * (N_Y - 1 - 2 * u)
+
+
 def wide_groups():
     groups = []
     for section in range(N_SECTION):
         for x in range(N_X):
             for u in range(4):
                 groups.append(
-                    [device_index(section, 2 * u + w, z, x, 0) for w in range(2) for z in range(N_Z)]
+                    [device_index(section, fold(u, w), z, x, 0) for w in range(2) for z in range(N_Z)]
                 )
             for z in range(N_Z):
                 groups.append([device_index(section, y, z, x, 1) for y in range(N_Y)])
@@ -53,7 +57,7 @@
         for x in range(N_X):
             for w in range(2):
                 for z in range(N_Z):
-                    groups.append([device_index(section, 2 * u + w, z, x, 0) for u in range(4)])
+                    groups.append([device_index(section, fold(u, w), z, x, 0) for u in range(4)])
             for y in range(N_Y):
                 groups.append([device_index(section, y, z, x, 1) for z in range(N_Z)])
     return groups
@@ -62,7 +66,7 @@
 def block_owner(core):
     block = jnp.arange(N_CTX, dtype=jnp.int32)
     first, second = block // 8, block % 8
-    owner_0 = (2 * first + second // 4) * N_Z + second % 4
+    owner_0 = fold(first, second // 4) * N_Z + second % 4
     owner_1 = second * N_Z + first
     return jnp.where(core == 0, owner_0, owner_1)
 
@@ -96,23 +100,29 @@
     )(features, weight)
 
 
-def unproject_kernel(g_ref, w_ref, o_ref):
+def unproject_kernel(g_ref, w_ref, a_in, b_in, o_ref, a_out, b_out):
+    a_out[...] = a_in[...]
+    b_out[...] = b_in[...]
     total = nt(g_ref[0], w_ref[:, : 2 * HD])
     for g in range(1, KVH):
         total += nt(g_ref[g], w_ref[:, g * 2 * HD : (g + 1) * 2 * HD])
     o_ref[...] = total.astype(jnp.bfloat16)
 
 
-def unproject(kv_grads, weight):
+def unproject(kv_grads, weight, out_b, grad_qb):
     whole = pl.BlockSpec(memory_space=pltpu.VMEM)
     return pl.pallas_call(
         unproject_kernel,
-        in_specs=[whole] * 2,
-        out_specs=whole,
-        out_shape=jax.ShapeDtypeStruct((ROWS, weight.shape[0]), jnp.bfloat16),
+        in_specs=[whole] * 4,
+        out_specs=[whole] * 3,
+        out_shape=[
+            jax.ShapeDtypeStruct((ROWS, weight.shape[0]), jnp.bfloat16),
+            jax.ShapeDtypeStruct(out_b.shape, jnp.bfloat16),
+            jax.ShapeDtypeStruct(grad_qb.shape, jnp.bfloat16),
+        ],
         compiler_params=pltpu.CompilerParams(vmem_limit_bytes=16 * MIB),
         name="kv_unproject",
-    )(kv_grads, weight)
+    )(kv_grads, weight, out_b, grad_qb)
 
 
 def loop(body, carry):
@@ -131,7 +141,7 @@
 
 def attention_kernel(
     base_ref, qa_ref, qb_ref, ga_ref, gb_ref, own_ref, other_ref,
-    oa_ref, gqa_ref, back_ref, gown_ref, gother_ref,
+    oa_ref, gqa_ref, ob_ref, gqb_ref, gown_ref, gother_ref,
     q_s, g_s, kv_s, kt_s, vt_s, s_s, dk_s, dv_s,
 ):
     for head in range(HPD):
@@ -212,8 +222,8 @@
                 oa_ref[:, cols] = o_head
                 gqa_ref[:, cols] = g_head
             else:
-                back_ref[:, cols] = o_head
-                back_ref[:, QROWS + head * HD : QROWS + (head + 1) * HD] = g_head
+                ob_ref[:, cols] = o_head
+                gqb_ref[:, cols] = g_head
 
     for ref, rows in ((gown_ref, slice(0, half)), (gother_ref, slice(half, KEYS))):
         ref[:, :HD] = (dk_s[rows, :] * SCALE).astype(jnp.bfloat16)
@@ -227,11 +237,12 @@
     return pl.pallas_call(
         attention_kernel,
         in_specs=[pl.BlockSpec(memory_space=pltpu.SMEM)] + [whole] * 6,
-        out_specs=[whole] * 5,
+        out_specs=[whole] * 6,
         out_shape=[
             jax.ShapeDtypeStruct((ROWS, HPD * HD), bf),
             jax.ShapeDtypeStruct((ROWS, HPD * HD), bf),
-            jax.ShapeDtypeStruct((ROWS, 2 * HPD * HD), bf),
+            jax.ShapeDtypeStruct((ROWS, HPD * HD), bf),
+            jax.ShapeDtypeStruct((ROWS, HPD * HD), bf),
             jax.ShapeDtypeStruct((half, 2 * HD), bf),
             jax.ShapeDtypeStruct((half, 2 * HD), bf),
         ],
@@ -245,7 +256,7 @@
             pltpu.VMEM((KEYS, HD), jnp.float32),
             pltpu.VMEM((KEYS, HD), jnp.float32),
         ],
-        compiler_params=pltpu.CompilerParams(vmem_limit_bytes=36 * MIB),
+        compiler_params=pltpu.CompilerParams(vmem_limit_bytes=28 * MIB),
         cost_estimate=pl.CostEstimate(
             flops=24 * QROWS * KEYS * HD, bytes_accessed=6 * MIB, transcendentals=4 * QROWS * KEYS
         ),
@@ -269,8 +280,8 @@
 
     own, moved_q = lax.optimization_barrier((own, moved_q))
     own = exchange(jnp.broadcast_to(own[None], (8, SPAN, 2 * HD)), wide)
+    own = exchange(jnp.broadcast_to(own[None], (4, 8, SPAN, 2 * HD)), narrow)
     own, moved_g = lax.optimization_barrier((own, moved_g))
-    own = exchange(jnp.broadcast_to(own[None], (4, 8, SPAN, 2 * HD)), narrow)
     own = own.reshape(N_CTX * SPAN, 2 * HD)
     other = swap_core(own)
 
@@ -279,26 +290,23 @@
     )
     bases = span_order[slots] * SPAN
 
-    out_a, grad_qa, back, grad_own, grad_other = attention(
+    out_a, grad_qa, out_b, grad_qb, grad_own, grad_other = attention(
         bases, queries_a[0], moved_q, grads_a[0], moved_g, own, other
     )
-    back = swap_section(back)
+    out_b = swap_section(out_b)
+    grad_qb = swap_section(grad_qb)
     grad_in = swap_core(grad_other)
     total = (grad_own.astype(f32) + grad_in.astype(f32)).astype(bf)
     total = exchange(total.reshape(4, 8, SPAN, 2 * HD), narrow)
+    total, out_b = lax.optimization_barrier((total, out_b))
     total = jnp.sum(total.astype(f32), axis=0).astype(bf)
     total = exchange(total, wide)
     total = jnp.sum(total.astype(f32), axis=0).astype(bf)
     total = lax.all_to_all(jnp.broadcast_to(total[None], (N_TP, SPAN, 2 * HD)), "tp", 0, 0, tiled=True)
-    grad_x = unproject(total.reshape(KVH, ROWS, 2 * HD), weight)
-    half = HPD * HD
-    return (
-        out_a[None],
-        back[None, :, :half],
-        grad_qa[None],
-        back[None, :, half:],
-        grad_x[None],
+    grad_x, out_b, grad_qb = unproject(
+        total.reshape(KVH, ROWS, 2 * HD), weight, out_b, grad_qb
     )
+    return out_a[None], out_b[None], grad_qa[None], grad_qb[None], grad_x[None]
 
 
 def solution(mesh):

time: 160 us -> 156 us (0.975)
  waiting for transfers between devices: 22.9 us -> 42.6 us
  blocking collectives: 43.4 us -> 27.1 us
  starting transfers between devices: 63.9 us -> 57.3 us
    ppermute x3 -> x4, waiting for transfers between devices: 6.24 us -> 35 us  [swap_section(): return lax.ppermute(value, 'section', [(0, 1), (1, 0)])]
    all_to_all x2, blocking collectives: 43.4 us -> 27.1 us  [exchange(): lax.all_to_all(value, EVERY, 0, 0, axis_index_groups=groups, tiled=True)]
    all_to_all x1, starting transfers between devices: 16.6 us -> 4.32 us  [on_device(): lax.all_to_all(jnp.broadcast_to(total[None], (N_TP, SPAN, 2 * HD)), 'tp',...]
    ppermute x3 -> x4, starting transfers between devices: 19.3 us -> 26.5 us  [swap_section(): return lax.ppermute(value, 'section', [(0, 1), (1, 0)])]
    all_to_all x1, waiting for transfers between devices: 5.78 us -> 0.01 us  [on_device(): lax.all_to_all(jnp.broadcast_to(total[None], (N_TP, SPAN, 2 * HD)), 'tp',...]
    ppermute x2, starting transfers between devices: 8.34 us -> 3.95 us  [swap_core(): return lax.ppermute(value, 'tp', [(i, i ^ 1) for i in range(N_TP)])]
    all_to_all x2, waiting for transfers between devices: 4.43 us -> 0.49 us  [exchange(): lax.all_to_all(value, EVERY, 0, 0, axis_index_groups=groups, tiled=True)]
    all_to_all x2, starting transfers between devices: 9.48 us -> 12.3 us  [exchange(): lax.all_to_all(value, EVERY, 0, 0, axis_index_groups=groups, tiled=True)]
  transfers between devices with their start and end apart: 9 -> 10, of which waited for: 7 -> 8; matrix products, arithmetic and copies ran while one was open for 2% -> 1% of each run, Pallas kernels for 0% -> 0%
where the time goes in v3:
time: 156 us; the launch traced here: 155 us
  starting transfers between devices  57.3 us (37%)
  waiting for transfers between devices  42.6 us (27%)
  blocking collectives  27.1 us (17%)
  Pallas kernels  19.1 us (12%)
  local copies, waits for them, and re-layouts  5.63 us (4%)
  other arithmetic  2.86 us (2%)
    ppermute x4, waiting for transfers between devices, swap_section(): return lax.ppermute(value, 'section', [(0, 1), (1, 0)])  35 us
    all_to_all x2, blocking collectives, exchange(): lax.all_to_all(value, EVERY, 0, 0, axis_index_groups=groups, tiled=True)  27.1 us
    ppermute x4, starting transfers between devices, swap_section(): return lax.ppermute(value, 'section', [(0, 1), (1, 0)])  26.5 us
    pallas_call x1, Pallas kernels, attention(): pl.pallas_call(attention_kernel, in_specs=[pl.BlockSpec(memory_space=pltp...  16.4 us
    all_to_all x2, starting transfers between devices, exchange(): lax.all_to_all(value, EVERY, 0, 0, axis_index_groups=groups, tiled=True)  12.3 us
    all_to_all x1, starting transfers between devices, on_device(): lax.all_to_all(partial.reshape(N_TP, SPAN, 2 * HD), 'tp', 0, 0, tiled=True)  10.3 us
    all_to_all x1, starting transfers between devices, on_device(): lax.all_to_all(jnp.broadcast_to(total[None], (N_TP, SPAN, 2 * HD)), 'tp',...  4.32 us
    ppermute x2, starting transfers between devices, swap_core(): return lax.ppermute(value, 'tp', [(i, i ^ 1) for i in range(N_TP)])  3.95 us
  transfers between devices with their start and end apart: 10, of which 8 were waited for; matrix products, arithmetic and copies ran while one was open for 1% of the time, Pallas kernels for 0%

profile of v3, /device:TPU:1, one launch (start us, length us, event | category | flops | bytes accessed | tf_op | source)
XLA Modules:
  0.0 155.4 jit_solution(10138156312429772250)
XLA Ops:
  0.6 0.0 copy-start
  0.7 1.6 %copy-done.1 = bf16[1,1024,1024]{2,1,0:T(8,128)(2,1)S(1)} copy-done((bf16[1,1024,1024]{2,1,0:T(8,128)(2,1)S(1)}, bf16[1,1024,1024]{2,1,0:T(8,128)(2,1)}, u32[]{:S(2)}) %copy-start.1) | copy-done | bytes 2097176
  2.2 0.9 copy-done.3
  3.2 1.2 kv_project.1
  4.4 10.3 %all-to-all-start = ((f32[8,64,256]{2,1,0:T(8,128)}), f32[8,64,256]{2,1,0:T(8,128)S(1)}, u32[]{:S(2)}, u32[]{:S(2)}) async-start(f32[8,64,256]{2,1,0:T(8,128)} %bitcast.7), calls=%async_computation | async-start | bytes 1048576 | tf_op jit(solution)/shard_map/all_to_all | solution.py:278
  14.7 6.2 %collective-permute-start = (bf16[128,512]{1,0:T(8,128)(2,1)S(1)}, bf16[128,512]{1,0:T(8,128)(2,1)S(1)}, u32[]{:S(2)}, u32[]{:S(2)}) collective-permute-start(bf16[128,512]{1,0:T(8,128)(2,1)S(1)} %bitcast.33), channel_id=1, source_target_pairs={{0,256},{256,0},{1,257},{257,1},{2,258},{258,2},{3,259},{259,3},{4... | collective-permute-start | bytes 393224 | tf_op jit(solution)/shard_map/ppermute | solution.py:79
  20.9 3.3 %all-to-all-done = f32[8,64,256]{2,1,0:T(8,128)S(1)} async-done(((f32[8,64,256]{2,1,0:T(8,128)}), f32[8,64,256]{2,1,0:T(8,128)S(1)}, u32[]{:S(2)}, u32[]{:S(2)}) %all-to-all-start) | async-done | bytes 524320 | tf_op jit(solution)/shard_map/all_to_all | solution.py:278
  24.3 1.2 collective-permute-done.qb_ref
  25.5 15.2 %all_to_all.30 = bf16[8,64,256]{2,1,0:T(8,128)(2,1)S(1)} all-to-all(bf16[8,64,256]{2,1,0:T(8,128)(2,1)S(1)} %broadcast_in_dim.16), channel_id=1, replica_groups={{0,8,16,24,224,232,240,248},{32,40,48,56,192,200,208,216},{64,72,80,88,..., dimensions={0} | all-to-all | bytes 524288 | tf_op jit(solution)/shard_map/all_to_all | solution.py:83
  40.7 1.1 broadcast_in_dim.17
  41.8 7.6 %all-to-all-start.2 = ((bf16[4,8,64,256]{3,2,1,0:T(8,128)(2,1)}), bf16[4,8,64,256]{3,2,1,0:T(8,128)(2,1)S(1)}, u32[]{:S(2)}, u32[]{:S(2)}) async-start(bf16[4,8,64,256]{3,2,1,0:T(8,128)(2,1)} %broadcast_in_dim.17), calls=%async_computation.2 | async-start | bytes 2097152 | tf_op jit(solution)/shard_map/all_to_all | solution.py:83
  49.3 7.0 %collective-permute-start.1 = (bf16[128,512]{1,0:T(8,128)(2,1)S(1)}, bf16[128,512]{1,0:T(8,128)(2,1)S(1)}, u32[]{:S(2)}, u32[]{:S(2)}) collective-permute-start(bf16[128,512]{1,0:T(8,128)(2,1)S(1)} %bitcast.34), channel_id=1, source_target_pairs={{0,256},{256,0},{1,257},{257,1},{2,258},{258,2},{3,259},{259,3},{4... | collective-permute-start | bytes 393224 | tf_op jit(solution)/shard_map/ppermute | solution.py:79
  56.4 13.4 %collective-permute-done.1.gb_ref = bf16[128,512]{1,0:T(8,128)(2,1)S(1)} collective-permute-done((bf16[128,512]{1,0:T(8,128)(2,1)S(1)}, bf16[128,512]{1,0:T(8,128)(2,1)S(1)}, u32[]{:S(2)}, u32[]{:S(2)}) %collective-permute-start.1) | collective-permute-done | bytes 131104 | tf_op jit(solution)/shard_map/ppermute | solution.py:79
  69.8 1.9 %collective-permute-start.2 = (bf16[2048,256]{1,0:T(8,128)(2,1)S(1)}, bf16[2048,256]{1,0:T(8,128)(2,1)S(1)}, u32[]{:S(2)}, u32[]{:S(2)}) collective-permute-start(bf16[2048,256]{1,0:T(8,128)(2,1)S(1)} %bitcast.26), channel_id=1, source_target_pairs={{0,1},{1,0},{2,3},{3,2},{4,5},{5,4},{6,7},{7,6},{8,9},{9,8},{10,11... | collective-permute-start | bytes 3145736 | tf_op jit(solution)/shard_map/ppermute | solution.py:75
  71.7 0.1 fusion.5
  71.8 1.2 gather_fusion
  73.1 1.2 collective-permute-done.2.other_ref
  74.3 16.4 %attention.1 = (bf16[128,512]{1,0:T(8,128)(2,1)}, bf16[128,512]{1,0:T(8,128)(2,1)}, bf16[128,512]{1,0:T(8,128)(2,1)S(1)}, bf16[128,512]{1,0:T(8,128)(2,1)S(1)}, ...) custom-call(s32[66]{0:T(128)S(1)} %broadcast_multiply_fusion.base_ref, bf16[128,512]{1,0:T(8,128)(2,1)S(1)} %bitcast.29, ...), custom_call_target="tpu_custom_call" | custom-call | flops 6442450944 | bytes 6291456 | tf_op jit(solution)/shard_map/attention/pallas_call | solution.py:237
  90.7 2.0 %collective-permute-start.3 = (bf16[2048,256]{1,0:T(8,128)(2,1)S(1)}, bf16[2048,256]{1,0:T(8,128)(2,1)S(1)}, u32[]{:S(2)}, u32[]{:S(2)}) collective-permute-start(bf16[2048,256]{1,0:T(8,128)(2,1)S(1)} %get-tuple-element.26), channel_id=1, source_target_pairs={{0,1},{1,0},{2,3},{3,2},{4,5},{5,4},{6,7},{7,6},{8,9},{9,8},{10,11... | collective-permute-start | bytes 3145736 | tf_op jit(solution)/shard_map/ppermute | solution.py:75
  92.7 2.5 %collective-permute-done.3 = bf16[2048,256]{1,0:T(8,128)(2,1)S(1)} collective-permute-done((bf16[2048,256]{1,0:T(8,128)(2,1)S(1)}, bf16[2048,256]{1,0:T(8,128)(2,1)S(1)}, u32[]{:S(2)}, u32[]{:S(2)}) %collective-permute-start.3) | collective-permute-done | bytes 1048608 | tf_op jit(solution)/shard_map/ppermute | solution.py:75
  95.2 1.3 add_convert_fusion
  96.5 4.7 %all-to-all-start.3 = ((bf16[4,8,64,256]{3,2,1,0:T(8,128)(2,1)}), bf16[4,8,64,256]{3,2,1,0:T(8,128)(2,1)}, u32[]{:S(2)}, u32[]{:S(2)}) async-start(bf16[4,8,64,256]{3,2,1,0:T(8,128)(2,1)} %bitcast.31), calls=%async_computation.3 | async-start | bytes 2097152 | tf_op jit(solution)/shard_map/all_to_all | solution.py:83
  101.2 6.6 %collective-permute-start.4 = (bf16[128,512]{1,0:T(8,128)(2,1)S(1)}, bf16[128,512]{1,0:T(8,128)(2,1)S(1)}, u32[]{:S(2)}, u32[]{:S(2)}) collective-permute-start(bf16[128,512]{1,0:T(8,128)(2,1)S(1)} %get-tuple-element.27), channel_id=1, source_target_pairs={{0,256},{256,0},{1,257},{257,1},{2,258},{258,2},{3,259},{259,3},{4... | collective-permute-start | bytes 393224 | tf_op jit(solution)/shard_map/ppermute | solution.py:79
  107.8 13.4 %collective-permute-done.4.a_in = bf16[128,512]{1,0:T(8,128)(2,1)S(1)} collective-permute-done((bf16[128,512]{1,0:T(8,128)(2,1)S(1)}, bf16[128,512]{1,0:T(8,128)(2,1)S(1)}, u32[]{:S(2)}, u32[]{:S(2)}) %collective-permute-start.4) | collective-permute-done | bytes 131104 | tf_op jit(solution)/shard_map/ppermute | solution.py:79
  121.2 0.5 all-to-all-done.3
  121.7 1.4 reduce_sum.34
  123.1 11.9 %all_to_all.31 = bf16[8,64,256]{2,1,0:T(8,128)(2,1)S(1)} all-to-all(bf16[8,64,256]{2,1,0:T(8,128)(2,1)S(1)} %reduce_sum.34), channel_id=1, replica_groups={{0,8,16,24,224,232,240,248},{32,40,48,56,192,200,208,216},{64,72,80,88,..., dimensions={0} | all-to-all | bytes 524288 | tf_op jit(solution)/shard_map/all_to_all | solution.py:83
  135.1 0.7 broadcast_in_dim.37
  135.8 4.3 %all-to-all-start.5 = ((bf16[8,64,256]{2,1,0:T(8,128)(2,1)}), bf16[8,64,256]{2,1,0:T(8,128)(2,1)S(1)}, u32[]{:S(2)}, u32[]{:S(2)}) async-start(bf16[8,64,256]{2,1,0:T(8,128)(2,1)} %broadcast_in_dim.37), calls=%async_computation.5 | async-start | bytes 524288 | tf_op jit(solution)/shard_map/all_to_all | solution.py:305
  140.1 6.6 %collective-permute-start.5 = (bf16[128,512]{1,0:T(8,128)(2,1)S(1)}, bf16[128,512]{1,0:T(8,128)(2,1)S(1)}, u32[]{:S(2)}, u32[]{:S(2)}) collective-permute-start(bf16[128,512]{1,0:T(8,128)(2,1)S(1)} %get-tuple-element.30), channel_id=1, source_target_pairs={{0,256},{256,0},{1,257},{257,1},{2,258},{258,2},{3,259},{259,3},{4... | collective-permute-start | bytes 393224 | tf_op jit(solution)/shard_map/ppermute | solution.py:79
  146.8 7.1 %collective-permute-done.5.b_in = bf16[128,512]{1,0:T(8,128)(2,1)S(1)} collective-permute-done((bf16[128,512]{1,0:T(8,128)(2,1)S(1)}, bf16[128,512]{1,0:T(8,128)(2,1)S(1)}, u32[]{:S(2)}, u32[]{:S(2)}) %collective-permute-start.5) | collective-permute-done | bytes 131104 | tf_op jit(solution)/shard_map/ppermute | solution.py:79
  153.9 1.5 kv_unproject.1
  (22 shorter events, 0.2 us)
Async XLA Ops:
  0.6 71.2 %copy-start = (s32[64]{0:T(128)S(1)}, s32[64]{0:T(128)}, u32[]{:S(2)}) copy-start(s32[64]{0:T(128)} %param.13) | copy-start | bytes 772
  0.6 1.6 %copy-start.1 = (bf16[1,1024,1024]{2,1,0:T(8,128)(2,1)S(1)}, bf16[1,1024,1024]{2,1,0:T(8,128)(2,1)}, u32[]{:S(2)}) copy-start(bf16[1,1024,1024]{2,1,0:T(8,128)(2,1)} %param.8) | copy-start | bytes 6291460
  2.2 0.9 copy-start.3
  3.2 11.5 %copy-start.6 = (bf16[1,128,512]{2,1,0:T(8,128)(2,1)S(1)}, bf16[1,128,512]{2,1,0:T(8,128)(2,1)}, u32[]{:S(2)}) copy-start(bf16[1,128,512]{2,1,0:T(8,128)(2,1)} %param.10) | copy-start | bytes 393220
  4.4 19.8 %all-to-all-start = ((f32[8,64,256]{2,1,0:T(8,128)}), f32[8,64,256]{2,1,0:T(8,128)S(1)}, u32[]{:S(2)}, u32[]{:S(2)}) async-start(f32[8,64,256]{2,1,0:T(8,128)} %bitcast.7), calls=%async_computation | async-start | bytes 1048576 | tf_op jit(solution)/shard_map/all_to_all | solution.py:278
  14.7 10.8 %collective-permute-start = (bf16[128,512]{1,0:T(8,128)(2,1)S(1)}, bf16[128,512]{1,0:T(8,128)(2,1)S(1)}, u32[]{:S(2)}, u32[]{:S(2)}) collective-permute-start(bf16[128,512]{1,0:T(8,128)(2,1)S(1)} %bitcast.33), channel_id=1, source_target_pairs={{0,256},{256,0},{1,257},{257,1},{2,258},{258,2},{3,259},{259,3},{4... | collective-permute-start | bytes 393224 | tf_op jit(solution)/shard_map/ppermute | solution.py:79
  24.2 25.1 %copy-start.7 = (bf16[1,128,512]{2,1,0:T(8,128)(2,1)S(1)}, bf16[1,128,512]{2,1,0:T(8,128)(2,1)}, u32[]{:S(2)}) copy-start(bf16[1,128,512]{2,1,0:T(8,128)(2,1)} %param.12) | copy-start | bytes 393220
  40.7 33.6 %copy-start.4 = (bf16[1,128,512]{2,1,0:T(8,128)(2,1)S(1)}, bf16[1,128,512]{2,1,0:T(8,128)(2,1)}, u32[]{:S(2)}) copy-start(bf16[1,128,512]{2,1,0:T(8,128)(2,1)} %param.9) | copy-start | bytes 393220
  40.7 33.6 %copy-start.5 = (bf16[1,128,512]{2,1,0:T(8,128)(2,1)S(1)}, bf16[1,128,512]{2,1,0:T(8,128)(2,1)}, u32[]{:S(2)}) copy-start(bf16[1,128,512]{2,1,0:T(8,128)(2,1)} %param.11) | copy-start | bytes 393220
  41.8 28.0 %all-to-all-start.2 = ((bf16[4,8,64,256]{3,2,1,0:T(8,128)(2,1)}), bf16[4,8,64,256]{3,2,1,0:T(8,128)(2,1)S(1)}, u32[]{:S(2)}, u32[]{:S(2)}) async-start(bf16[4,8,64,256]{3,2,1,0:T(8,128)(2,1)} %broadcast_in_dim.17), calls=%async_computation.2 | async-start | bytes 2097152 | tf_op jit(solution)/shard_map/all_to_all | solution.py:83
  49.3 20.4 %collective-permute-start.1 = (bf16[128,512]{1,0:T(8,128)(2,1)S(1)}, bf16[128,512]{1,0:T(8,128)(2,1)S(1)}, u32[]{:S(2)}, u32[]{:S(2)}) collective-permute-start(bf16[128,512]{1,0:T(8,128)(2,1)S(1)} %bitcast.34), channel_id=1, source_target_pairs={{0,256},{256,0},{1,257},{257,1},{2,258},{258,2},{3,259},{259,3},{4... | collective-permute-start | bytes 393224 | tf_op jit(solution)/shard_map/ppermute | solution.py:79
  69.8 4.5 %collective-permute-start.2 = (bf16[2048,256]{1,0:T(8,128)(2,1)S(1)}, bf16[2048,256]{1,0:T(8,128)(2,1)S(1)}, u32[]{:S(2)}, u32[]{:S(2)}) collective-permute-start(bf16[2048,256]{1,0:T(8,128)(2,1)S(1)} %bitcast.26), channel_id=1, source_target_pairs={{0,1},{1,0},{2,3},{3,2},{4,5},{5,4},{6,7},{7,6},{8,9},{9,8},{10,11... | collective-permute-start | bytes 3145736 | tf_op jit(solution)/shard_map/ppermute | solution.py:75
  90.7 4.5 %collective-permute-start.3 = (bf16[2048,256]{1,0:T(8,128)(2,1)S(1)}, bf16[2048,256]{1,0:T(8,128)(2,1)S(1)}, u32[]{:S(2)}, u32[]{:S(2)}) collective-permute-start(bf16[2048,256]{1,0:T(8,128)(2,1)S(1)} %get-tuple-element.26), channel_id=1, source_target_pairs={{0,1},{1,0},{2,3},{3,2},{4,5},{5,4},{6,7},{7,6},{8,9},{9,8},{10,11... | collective-permute-start | bytes 3145736 | tf_op jit(solution)/shard_map/ppermute | solution.py:75
  96.5 57.4 %copy-start.2 = (bf16[1,1024,1024]{2,1,0:T(8,128)(2,1)S(1)}, bf16[1,1024,1024]{2,1,0:T(8,128)(2,1)}, u32[]{:S(2)}) copy-start(bf16[1,1024,1024]{2,1,0:T(8,128)(2,1)} %param.8) | copy-start | bytes 6291460
  96.5 25.2 %all-to-all-start.3 = ((bf16[4,8,64,256]{3,2,1,0:T(8,128)(2,1)}), bf16[4,8,64,256]{3,2,1,0:T(8,128)(2,1)}, u32[]{:S(2)}, u32[]{:S(2)}) async-start(bf16[4,8,64,256]{3,2,1,0:T(8,128)(2,1)} %bitcast.31), calls=%async_computation.3 | async-start | bytes 2097152 | tf_op jit(solution)/shard_map/all_to_all | solution.py:83
  101.2 20.0 %collective-permute-start.4 = (bf16[128,512]{1,0:T(8,128)(2,1)S(1)}, bf16[128,512]{1,0:T(8,128)(2,1)S(1)}, u32[]{:S(2)}, u32[]{:S(2)}) collective-permute-start(bf16[128,512]{1,0:T(8,128)(2,1)S(1)} %get-tuple-element.27), channel_id=1, source_target_pairs={{0,256},{256,0},{1,257},{257,1},{2,258},{258,2},{3,259},{259,3},{4... | collective-permute-start | bytes 393224 | tf_op jit(solution)/shard_map/ppermute | solution.py:79
  135.8 18.0 %all-to-all-start.5 = ((bf16[8,64,256]{2,1,0:T(8,128)(2,1)}), bf16[8,64,256]{2,1,0:T(8,128)(2,1)S(1)}, u32[]{:S(2)}, u32[]{:S(2)}) async-start(bf16[8,64,256]{2,1,0:T(8,128)(2,1)} %broadcast_in_dim.37), calls=%async_computation.5 | async-start | bytes 524288 | tf_op jit(solution)/shard_map/all_to_all | solution.py:305
  140.1 13.7 %collective-permute-start.5 = (bf16[128,512]{1,0:T(8,128)(2,1)S(1)}, bf16[128,512]{1,0:T(8,128)(2,1)S(1)}, u32[]{:S(2)}, u32[]{:S(2)}) collective-permute-start(bf16[128,512]{1,0:T(8,128)(2,1)S(1)} %get-tuple-element.30), channel_id=1, source_target_pairs={{0,256},{256,0},{1,257},{257,1},{2,258},{258,2},{3,259},{259,3},{4... | collective-permute-start | bytes 393224 | tf_op jit(solution)/shard_map/ppermute | solution.py:79

commit v4 on v3

--- a/solution.py
+++ b/solution.py
@@ -75,8 +75,17 @@
     return lax.ppermute(value, "tp", [(i, i ^ 1) for i in range(N_TP)])
 
 
+def mirror(ctx):
+    return ctx - ctx % N_Z + N_Z - 1 - ctx % N_Z
+
+
 def swap_section(value):
-    return lax.ppermute(value, "section", [(0, 1), (1, 0)])
+    pairs = [
+        (section * N_CTX + ctx, (1 - section) * N_CTX + mirror(ctx))
+        for section in range(N_SECTION)
+        for ctx in range(N_CTX)
+    ]
+    return lax.ppermute(value, ("section", "ctx"), pairs)
 
 
 def exchange(value, groups):
@@ -100,29 +109,29 @@
     )(features, weight)
 
 
-def unproject_kernel(g_ref, w_ref, a_in, b_in, o_ref, a_out, b_out):
-    a_out[...] = a_in[...]
-    b_out[...] = b_in[...]
+def unproject_kernel(g_ref, w_ref, back_ref, o_ref, a_out, b_out):
+    a_out[...] = back_ref[:, :QROWS]
+    b_out[...] = back_ref[:, QROWS:]
     total = nt(g_ref[0], w_ref[:, : 2 * HD])
     for g in range(1, KVH):
         total += nt(g_ref[g], w_ref[:, g * 2 * HD : (g + 1) * 2 * HD])
     o_ref[...] = total.astype(jnp.bfloat16)
 
 
-def unproject(kv_grads, weight, out_b, grad_qb):
+def unproject(kv_grads, weight, back):
     whole = pl.BlockSpec(memory_space=pltpu.VMEM)
     return pl.pallas_call(
         unproject_kernel,
-        in_specs=[whole] * 4,
+        in_specs=[whole] * 3,
         out_specs=[whole] * 3,
         out_shape=[
             jax.ShapeDtypeStruct((ROWS, weight.shape[0]), jnp.bfloat16),
-            jax.ShapeDtypeStruct(out_b.shape, jnp.bfloat16),
-            jax.ShapeDtypeStruct(grad_qb.shape, jnp.bfloat16),
+            jax.ShapeDtypeStruct((ROWS, QROWS), jnp.bfloat16),
+            jax.ShapeDtypeStruct((ROWS, QROWS), jnp.bfloat16),
         ],
         compiler_params=pltpu.CompilerParams(vmem_limit_bytes=16 * MIB),
         name="kv_unproject",
-    )(kv_grads, weight, out_b, grad_qb)
+    )(kv_grads, weight, back)
 
 
 def loop(body, carry):
@@ -141,7 +150,7 @@
 
 def attention_kernel(
     base_ref, qa_ref, qb_ref, ga_ref, gb_ref, own_ref, other_ref,
-    oa_ref, gqa_ref, ob_ref, gqb_ref, gown_ref, gother_ref,
+    oa_ref, gqa_ref, back_ref, gown_ref, gother_ref,
     q_s, g_s, kv_s, kt_s, vt_s, s_s, dk_s, dv_s,
 ):
     for head in range(HPD):
@@ -160,12 +169,12 @@
         vt_s[:, rows] = kv_s[rows, HD:].T
 
     lane = lax.broadcasted_iota(jnp.int32, (1, QROWS), 1) % ROWS
-    q_pos = jnp.where(lane < SPAN, base_ref[64], base_ref[65]) + lane % SPAN
     key_row = lax.broadcasted_iota(jnp.int32, (SPAN, QROWS), 0)
 
     for unit in range(2):
         queries = q_s[unit]
         grads = g_s[unit]
+        q_pos = jnp.where(lane < SPAN, base_ref[64 + 2 * unit], base_ref[65 + 2 * unit]) + lane % SPAN
 
         def scores(c, top):
             start = c * CHUNK
@@ -222,8 +231,8 @@
                 oa_ref[:, cols] = o_head
                 gqa_ref[:, cols] = g_head
             else:
-                ob_ref[:, cols] = o_head
-                gqb_ref[:, cols] = g_head
+                back_ref[:, cols] = o_head
+                back_ref[:, QROWS + head * HD : QROWS + (head + 1) * HD] = g_head
 
     for ref, rows in ((gown_ref, slice(0, half)), (gother_ref, slice(half, KEYS))):
         ref[:, :HD] = (dk_s[rows, :] * SCALE).astype(jnp.bfloat16)
@@ -237,12 +246,11 @@
     return pl.pallas_call(
         attention_kernel,
         in_specs=[pl.BlockSpec(memory_space=pltpu.SMEM)] + [whole] * 6,
-        out_specs=[whole] * 6,
+        out_specs=[whole] * 5,
         out_shape=[
             jax.ShapeDtypeStruct((ROWS, HPD * HD), bf),
             jax.ShapeDtypeStruct((ROWS, HPD * HD), bf),
-            jax.ShapeDtypeStruct((ROWS, HPD * HD), bf),
-            jax.ShapeDtypeStruct((ROWS, HPD * HD), bf),
+            jax.ShapeDtypeStruct((ROWS, 2 * HPD * HD), bf),
             jax.ShapeDtypeStruct((half, 2 * HD), bf),
             jax.ShapeDtypeStruct((half, 2 * HD), bf),
         ],
@@ -286,25 +294,24 @@
     other = swap_core(own)
 
     slots = jnp.concatenate(
-        [2 * block_owner(core) + core, 2 * block_owner(1 - core) + 1 - core, 2 * ctx + jnp.arange(2)]
+        [2 * block_owner(core) + core, 2 * block_owner(1 - core) + 1 - core, 2 * ctx + jnp.arange(2), 2 * mirror(ctx) + jnp.arange(2)]
     )
     bases = span_order[slots] * SPAN
 
-    out_a, grad_qa, out_b, grad_qb, grad_own, grad_other = attention(
+    out_a, grad_qa, back, grad_own, grad_other = attention(
         bases, queries_a[0], moved_q, grads_a[0], moved_g, own, other
     )
-    out_b = swap_section(out_b)
-    grad_qb = swap_section(grad_qb)
+    back = swap_section(back)
     grad_in = swap_core(grad_other)
     total = (grad_own.astype(f32) + grad_in.astype(f32)).astype(bf)
     total = exchange(total.reshape(4, 8, SPAN, 2 * HD), narrow)
-    total, out_b = lax.optimization_barrier((total, out_b))
+    total, back = lax.optimization_barrier((total, back))
     total = jnp.sum(total.astype(f32), axis=0).astype(bf)
     total = exchange(total, wide)
     total = jnp.sum(total.astype(f32), axis=0).astype(bf)
     total = lax.all_to_all(jnp.broadcast_to(total[None], (N_TP, SPAN, 2 * HD)), "tp", 0, 0, tiled=True)
     grad_x, out_b, grad_qb = unproject(
-        total.reshape(KVH, ROWS, 2 * HD), weight, out_b, grad_qb
+        total.reshape(KVH, ROWS, 2 * HD), weight, back
     )
     return out_a[None], out_b[None], grad_qa[None], grad_qb[None], grad_x[None]
 

time: 156 us -> 143 us (0.917)
  blocking collectives: 27.1 us -> 41 us
  waiting for transfers between devices: 42.6 us -> 28.8 us
  starting transfers between devices: 57.3 us -> 43.6 us
    ppermute x4 -> x3, waiting for transfers between devices: 35 us -> 19.2 us  [swap_section(): return lax.ppermute(value, ('section', 'ctx'), pairs)]
    all_to_all x0 -> x1, blocking collectives: none -> 10.5 us  [on_device(): lax.all_to_all(jnp.broadcast_to(total[None], (N_TP, SPAN, 2 * HD)), 'tp',...]
    ppermute x4 -> x3, starting transfers between devices: 26.5 us -> 19.6 us  [swap_section(): return lax.ppermute(value, ('section', 'ctx'), pairs)]
    all_to_all x2, starting transfers between devices: 12.3 us -> 7.89 us  [exchange(): lax.all_to_all(value, EVERY, 0, 0, axis_index_groups=groups, tiled=True)]
    all_to_all x1 -> x0, starting transfers between devices: 4.32 us -> none  [on_device(): lax.all_to_all(jnp.broadcast_to(total[None], (N_TP, SPAN, 2 * HD)), 'tp',...]
    all_to_all x2, blocking collectives: 27.1 us -> 30.5 us  [exchange(): lax.all_to_all(value, EVERY, 0, 0, axis_index_groups=groups, tiled=True)]
    all_to_all x2, waiting for transfers between devices: 0.49 us -> 3.19 us  [exchange(): lax.all_to_all(value, EVERY, 0, 0, axis_index_groups=groups, tiled=True)]
    ppermute x2, starting transfers between devices: 3.95 us -> 5.82 us  [swap_core(): return lax.ppermute(value, 'tp', [(i, i ^ 1) for i in range(N_TP)])]
  transfers between devices with their start and end apart: 10 -> 8, of which waited for: 8 -> 7; matrix products, arithmetic and copies ran while one was open for 1% -> 1% of each run, Pallas kernels for 0% -> 0%
where the time goes in v4:
time: 143 us; the launch traced here: 141 us
  starting transfers between devices  43.6 us (30%)
  blocking collectives  41 us (29%)
  waiting for transfers between devices  28.8 us (20%)
  Pallas kernels  19.1 us (13%)
  local copies, waits for them, and re-layouts  4.94 us (3%)
  other arithmetic  2.88 us (2%)
    all_to_all x2, blocking collectives, exchange(): lax.all_to_all(value, EVERY, 0, 0, axis_index_groups=groups, tiled=True)  30.5 us
    ppermute x3, starting transfers between devices, swap_section(): return lax.ppermute(value, ('section', 'ctx'), pairs)  19.6 us
    ppermute x3, waiting for transfers between devices, swap_section(): return lax.ppermute(value, ('section', 'ctx'), pairs)  19.2 us
    pallas_call x1, Pallas kernels, attention(): pl.pallas_call(attention_kernel, in_specs=[pl.BlockSpec(memory_space=pltp...  16.4 us
    all_to_all x1, blocking collectives, on_device(): lax.all_to_all(jnp.broadcast_to(total[None], (N_TP, SPAN, 2 * HD)), 'tp',...  10.5 us
    all_to_all x1, starting transfers between devices, on_device(): lax.all_to_all(partial.reshape(N_TP, SPAN, 2 * HD), 'tp', 0, 0, tiled=True)  10.3 us
    all_to_all x2, starting transfers between devices, exchange(): lax.all_to_all(value, EVERY, 0, 0, axis_index_groups=groups, tiled=True)  7.89 us
    ppermute x2, starting transfers between devices, swap_core(): return lax.ppermute(value, 'tp', [(i, i ^ 1) for i in range(N_TP)])  5.82 us
  transfers between devices with their start and end apart: 8, of which 7 were waited for; matrix products, arithmetic and copies ran while one was open for 1% of the time, Pallas kernels for 0%

profile of v4, /device:TPU:1, one launch (start us, length us, event | category | flops | bytes accessed | tf_op | source)
XLA Modules:
  0.0 141.1 jit_solution(1656251924362595811)
XLA Ops:
  0.6 0.0 copy-start
  0.6 0.0 copy-start.1
  0.7 1.6 %copy-done.1 = bf16[1,1024,1024]{2,1,0:T(8,128)(2,1)S(1)} copy-done((bf16[1,1024,1024]{2,1,0:T(8,128)(2,1)S(1)}, bf16[1,1024,1024]{2,1,0:T(8,128)(2,1)}, u32[]{:S(2)}) %copy-start.1) | copy-done | bytes 2097176
  2.2 0.9 copy-done.3
  3.2 1.2 kv_project.1
  4.4 10.3 %all-to-all-start = ((f32[8,64,256]{2,1,0:T(8,128)}), f32[8,64,256]{2,1,0:T(8,128)S(1)}, u32[]{:S(2)}, u32[]{:S(2)}) async-start(f32[8,64,256]{2,1,0:T(8,128)} %bitcast.8), calls=%async_computation | async-start | bytes 1048576 | tf_op jit(solution)/shard_map/all_to_all | solution.py:286
  14.7 6.2 %collective-permute-start = (bf16[128,512]{1,0:T(8,128)(2,1)S(1)}, bf16[128,512]{1,0:T(8,128)(2,1)S(1)}, u32[]{:S(2)}, u32[]{:S(2)}) collective-permute-start(bf16[128,512]{1,0:T(8,128)(2,1)S(1)} %bitcast.35), channel_id=1, source_target_pairs={{0,280},{8,272},{16,264},{24,256},{32,312},{40,304},{48,296},{56,2... | collective-permute-start | bytes 393224 | tf_op jit(solution)/shard_map/ppermute | solution.py:88
  20.9 3.3 %all-to-all-done = f32[8,64,256]{2,1,0:T(8,128)S(1)} async-done(((f32[8,64,256]{2,1,0:T(8,128)}), f32[8,64,256]{2,1,0:T(8,128)S(1)}, u32[]{:S(2)}, u32[]{:S(2)}) %all-to-all-start) | async-done | bytes 524320 | tf_op jit(solution)/shard_map/all_to_all | solution.py:286
  24.2 0.0 copy-start.7
  24.3 3.5 %collective-permute-done.qb_ref = bf16[128,512]{1,0:T(8,128)(2,1)S(1)} collective-permute-done((bf16[128,512]{1,0:T(8,128)(2,1)S(1)}, bf16[128,512]{1,0:T(8,128)(2,1)S(1)}, u32[]{:S(2)}, u32[]{:S(2)}) %collective-permute-start) | collective-permute-done | bytes 131104 | tf_op jit(solution)/shard_map/ppermute | solution.py:88
  27.7 16.4 %all_to_all.30 = bf16[8,64,256]{2,1,0:T(8,128)(2,1)S(1)} all-to-all(bf16[8,64,256]{2,1,0:T(8,128)(2,1)S(1)} %broadcast_in_dim.16), channel_id=1, replica_groups={{0,8,16,24,224,232,240,248},{32,40,48,56,192,200,208,216},{64,72,80,88,..., dimensions={0} | all-to-all | bytes 524288 | tf_op jit(solution)/shard_map/all_to_all | solution.py:92
  44.2 1.1 broadcast_in_dim.17
  45.3 3.5 %all-to-all-start.2 = ((bf16[4,8,64,256]{3,2,1,0:T(8,128)(2,1)}), bf16[4,8,64,256]{3,2,1,0:T(8,128)(2,1)S(1)}, u32[]{:S(2)}, u32[]{:S(2)}) async-start(bf16[4,8,64,256]{3,2,1,0:T(8,128)(2,1)} %broadcast_in_dim.17), calls=%async_computation.2 | async-start | bytes 2097152 | tf_op jit(solution)/shard_map/all_to_all | solution.py:92
  48.8 6.1 %collective-permute-start.1 = (bf16[128,512]{1,0:T(8,128)(2,1)S(1)}, bf16[128,512]{1,0:T(8,128)(2,1)S(1)}, u32[]{:S(2)}, u32[]{:S(2)}) collective-permute-start(bf16[128,512]{1,0:T(8,128)(2,1)S(1)} %bitcast.36), channel_id=1, source_target_pairs={{0,280},{8,272},{16,264},{24,256},{32,312},{40,304},{48,296},{56,2... | collective-permute-start | bytes 393224 | tf_op jit(solution)/shard_map/ppermute | solution.py:88
  54.9 5.7 %collective-permute-done.1.gb_ref = bf16[128,512]{1,0:T(8,128)(2,1)S(1)} collective-permute-done((bf16[128,512]{1,0:T(8,128)(2,1)S(1)}, bf16[128,512]{1,0:T(8,128)(2,1)S(1)}, u32[]{:S(2)}, u32[]{:S(2)}) %collective-permute-start.1) | collective-permute-done | bytes 131104 | tf_op jit(solution)/shard_map/ppermute | solution.py:88
  60.6 3.2 %all-to-all-done.2 = bf16[4,8,64,256]{3,2,1,0:T(8,128)(2,1)S(1)} async-done(((bf16[4,8,64,256]{3,2,1,0:T(8,128)(2,1)}), bf16[4,8,64,256]{3,2,1,0:T(8,128)(2,1)S(1)}, u32[]{:S(2)}, u32[]{:S(2)}) %all-to-all-start.2) | async-done | bytes 1048608 | tf_op jit(solution)/shard_map/all_to_all | solution.py:92
  63.8 3.5 %collective-permute-start.2 = (bf16[2048,256]{1,0:T(8,128)(2,1)S(1)}, bf16[2048,256]{1,0:T(8,128)(2,1)S(1)}, u32[]{:S(2)}, u32[]{:S(2)}) collective-permute-start(bf16[2048,256]{1,0:T(8,128)(2,1)S(1)} %bitcast.28), channel_id=1, source_target_pairs={{0,1},{1,0},{2,3},{3,2},{4,5},{5,4},{6,7},{7,6},{8,9},{9,8},{10,11... | collective-permute-start | bytes 3145736 | tf_op jit(solution)/shard_map/ppermute | solution.py:75
  67.5 0.1 fusion.5
  67.6 1.2 gather_fusion
  68.8 0.9 collective-permute-done.2.other_ref
  69.7 16.4 %attention.1 = (bf16[128,512]{1,0:T(8,128)(2,1)}, bf16[128,512]{1,0:T(8,128)(2,1)}, bf16[128,1024]{1,0:T(8,128)(2,1)S(1)}, bf16[2048,256]{1,0:T(8,128)(2,1)S(1)}, bf16[2048,256]{1,0:T(8,128)(2,1)S(1)}) custom-call(s32[68]{0:T(128)S(1)} %broadcast_multiply_fusion.base_ref, bf16[128,512]{1,0:T(8,128)(2,1)S(1)} %bitcast.31, ...), custom_call_target="tpu_custom_call" | custom-call | flops 6442450944 | bytes 6291456 | tf_op jit(solution)/shard_map/attention/pallas_call | solution.py:246
  86.0 2.3 %collective-permute-start.3 = (bf16[2048,256]{1,0:T(8,128)(2,1)S(1)}, bf16[2048,256]{1,0:T(8,128)(2,1)S(1)}, u32[]{:S(2)}, u32[]{:S(2)}) collective-permute-start(bf16[2048,256]{1,0:T(8,128)(2,1)S(1)} %get-tuple-element.25), channel_id=1, source_target_pairs={{0,1},{1,0},{2,3},{3,2},{4,5},{5,4},{6,7},{7,6},{8,9},{9,8},{10,11... | collective-permute-start | bytes 3145736 | tf_op jit(solution)/shard_map/ppermute | solution.py:75
  88.3 2.3 %collective-permute-done.3 = bf16[2048,256]{1,0:T(8,128)(2,1)S(1)} collective-permute-done((bf16[2048,256]{1,0:T(8,128)(2,1)S(1)}, bf16[2048,256]{1,0:T(8,128)(2,1)S(1)}, u32[]{:S(2)}, u32[]{:S(2)}) %collective-permute-start.3) | collective-permute-done | bytes 1048608 | tf_op jit(solution)/shard_map/ppermute | solution.py:75
  90.6 1.3 add_convert_fusion
  91.8 4.4 %all-to-all-start.3 = ((bf16[4,8,64,256]{3,2,1,0:T(8,128)(2,1)}), bf16[4,8,64,256]{3,2,1,0:T(8,128)(2,1)}, u32[]{:S(2)}, u32[]{:S(2)}) async-start(bf16[4,8,64,256]{3,2,1,0:T(8,128)(2,1)} %bitcast.33), calls=%async_computation.3 | async-start | bytes 2097152 | tf_op jit(solution)/shard_map/all_to_all | solution.py:92
  96.2 7.3 %collective-permute-start.4 = (bf16[128,1024]{1,0:T(8,128)(2,1)S(1)}, bf16[128,1024]{1,0:T(8,128)(2,1)S(1)}, u32[]{:S(2)}, u32[]{:S(2)}) collective-permute-start(bf16[128,1024]{1,0:T(8,128)(2,1)S(1)} %get-tuple-element.26), channel_id=1, source_target_pairs={{0,280},{8,272},{16,264},{24,256},{32,312},{40,304},{48,296},{56,2... | collective-permute-start | bytes 786440 | tf_op jit(solution)/shard_map/ppermute | solution.py:88
  103.5 10.0 %collective-permute-done.4.back_ref = bf16[128,1024]{1,0:T(8,128)(2,1)S(1)} collective-permute-done((bf16[128,1024]{1,0:T(8,128)(2,1)S(1)}, bf16[128,1024]{1,0:T(8,128)(2,1)S(1)}, u32[]{:S(2)}, u32[]{:S(2)}) %collective-permute-start.4) | collective-permute-done | bytes 262176 | tf_op jit(solution)/shard_map/ppermute | solution.py:88
  113.5 0.0 all-to-all-done.3
  113.5 1.4 reduce_sum.34
  115.0 14.1 %all_to_all.31 = bf16[8,64,256]{2,1,0:T(8,128)(2,1)S(1)} all-to-all(bf16[8,64,256]{2,1,0:T(8,128)(2,1)S(1)} %reduce_sum.34), channel_id=1, replica_groups={{0,8,16,24,224,232,240,248},{32,40,48,56,192,200,208,216},{64,72,80,88,..., dimensions={0} | all-to-all | bytes 524288 | tf_op jit(solution)/shard_map/all_to_all | solution.py:92
  129.1 10.5 %all_to_all.32 = bf16[8,64,256]{2,1,0:T(8,128)(2,1)S(1)} all-to-all(bf16[8,64,256]{2,1,0:T(8,128)(2,1)S(1)} %broadcast_in_dim.37), channel_id=1, replica_groups=mesh['section'=2,'ctx'=32,'tp'=8] {'tp'}, dimensions={0} | all-to-all | bytes 524288 | tf_op jit(solution)/shard_map/all_to_all | solution.py:312
  139.6 1.5 %kv_unproject.1 = (bf16[128,1024]{1,0:T(8,128)(2,1)}, bf16[128,512]{1,0:T(8,128)(2,1)}, bf16[128,512]{1,0:T(8,128)(2,1)}) custom-call(bf16[4,128,256]{2,1,0:T(8,128)(2,1)S(1)} %bitcast.27, bf16[1024,1024]{1,0:T(8,128)(2,1)S(1)} %bitcast.26, bf16[128,1024]{1,0:T(8,128)(2,1)S(1)} %collective-permute-done.4.back_ref), custom_call_target="tpu_custom_call" | custom-call | tf_op jit(solution)/shard_map/kv_unproject/pallas_call | solution.py:123
  (19 shorter events, 0.2 us)
Async XLA Ops:
  0.6 66.9 %copy-start = (s32[64]{0:T(128)S(1)}, s32[64]{0:T(128)}, u32[]{:S(2)}) copy-start(s32[64]{0:T(128)} %param.13) | copy-start | bytes 772
  0.6 1.6 %copy-start.1 = (bf16[1,1024,1024]{2,1,0:T(8,128)(2,1)S(1)}, bf16[1,1024,1024]{2,1,0:T(8,128)(2,1)}, u32[]{:S(2)}) copy-start(bf16[1,1024,1024]{2,1,0:T(8,128)(2,1)} %param.8) | copy-start | bytes 6291460
  2.2 0.9 copy-start.3
  3.2 11.5 %copy-start.6 = (bf16[1,128,512]{2,1,0:T(8,128)(2,1)S(1)}, bf16[1,128,512]{2,1,0:T(8,128)(2,1)}, u32[]{:S(2)}) copy-start(bf16[1,128,512]{2,1,0:T(8,128)(2,1)} %param.10) | copy-start | bytes 393220
  4.4 19.8 %all-to-all-start = ((f32[8,64,256]{2,1,0:T(8,128)}), f32[8,64,256]{2,1,0:T(8,128)S(1)}, u32[]{:S(2)}, u32[]{:S(2)}) async-start(f32[8,64,256]{2,1,0:T(8,128)} %bitcast.8), calls=%async_computation | async-start | bytes 1048576 | tf_op jit(solution)/shard_map/all_to_all | solution.py:286
  14.7 13.0 %collective-permute-start = (bf16[128,512]{1,0:T(8,128)(2,1)S(1)}, bf16[128,512]{1,0:T(8,128)(2,1)S(1)}, u32[]{:S(2)}, u32[]{:S(2)}) collective-permute-start(bf16[128,512]{1,0:T(8,128)(2,1)S(1)} %bitcast.35), channel_id=1, source_target_pairs={{0,280},{8,272},{16,264},{24,256},{32,312},{40,304},{48,296},{56,2... | collective-permute-start | bytes 393224 | tf_op jit(solution)/shard_map/ppermute | solution.py:88
  24.2 24.6 %copy-start.7 = (bf16[1,128,512]{2,1,0:T(8,128)(2,1)S(1)}, bf16[1,128,512]{2,1,0:T(8,128)(2,1)}, u32[]{:S(2)}) copy-start(bf16[1,128,512]{2,1,0:T(8,128)(2,1)} %param.12) | copy-start | bytes 393220
  44.2 25.5 %copy-start.4 = (bf16[1,128,512]{2,1,0:T(8,128)(2,1)S(1)}, bf16[1,128,512]{2,1,0:T(8,128)(2,1)}, u32[]{:S(2)}) copy-start(bf16[1,128,512]{2,1,0:T(8,128)(2,1)} %param.9) | copy-start | bytes 393220
  44.2 25.5 %copy-start.5 = (bf16[1,128,512]{2,1,0:T(8,128)(2,1)S(1)}, bf16[1,128,512]{2,1,0:T(8,128)(2,1)}, u32[]{:S(2)}) copy-start(bf16[1,128,512]{2,1,0:T(8,128)(2,1)} %param.11) | copy-start | bytes 393220
  45.3 18.5 %all-to-all-start.2 = ((bf16[4,8,64,256]{3,2,1,0:T(8,128)(2,1)}), bf16[4,8,64,256]{3,2,1,0:T(8,128)(2,1)S(1)}, u32[]{:S(2)}, u32[]{:S(2)}) async-start(bf16[4,8,64,256]{3,2,1,0:T(8,128)(2,1)} %broadcast_in_dim.17), calls=%async_computation.2 | async-start | bytes 2097152 | tf_op jit(solution)/shard_map/all_to_all | solution.py:92
  48.8 11.8 %collective-permute-start.1 = (bf16[128,512]{1,0:T(8,128)(2,1)S(1)}, bf16[128,512]{1,0:T(8,128)(2,1)S(1)}, u32[]{:S(2)}, u32[]{:S(2)}) collective-permute-start(bf16[128,512]{1,0:T(8,128)(2,1)S(1)} %bitcast.36), channel_id=1, source_target_pairs={{0,280},{8,272},{16,264},{24,256},{32,312},{40,304},{48,296},{56,2... | collective-permute-start | bytes 393224 | tf_op jit(solution)/shard_map/ppermute | solution.py:88
  63.8 5.8 %collective-permute-start.2 = (bf16[2048,256]{1,0:T(8,128)(2,1)S(1)}, bf16[2048,256]{1,0:T(8,128)(2,1)S(1)}, u32[]{:S(2)}, u32[]{:S(2)}) collective-permute-start(bf16[2048,256]{1,0:T(8,128)(2,1)S(1)} %bitcast.28), channel_id=1, source_target_pairs={{0,1},{1,0},{2,3},{3,2},{4,5},{5,4},{6,7},{7,6},{8,9},{9,8},{10,11... | collective-permute-start | bytes 3145736 | tf_op jit(solution)/shard_map/ppermute | solution.py:75
  86.0 4.5 %collective-permute-start.3 = (bf16[2048,256]{1,0:T(8,128)(2,1)S(1)}, bf16[2048,256]{1,0:T(8,128)(2,1)S(1)}, u32[]{:S(2)}, u32[]{:S(2)}) collective-permute-start(bf16[2048,256]{1,0:T(8,128)(2,1)S(1)} %get-tuple-element.25), channel_id=1, source_target_pairs={{0,1},{1,0},{2,3},{3,2},{4,5},{5,4},{6,7},{7,6},{8,9},{9,8},{10,11... | collective-permute-start | bytes 3145736 | tf_op jit(solution)/shard_map/ppermute | solution.py:75
  91.8 47.7 %copy-start.2 = (bf16[1,1024,1024]{2,1,0:T(8,128)(2,1)S(1)}, bf16[1,1024,1024]{2,1,0:T(8,128)(2,1)}, u32[]{:S(2)}) copy-start(bf16[1,1024,1024]{2,1,0:T(8,128)(2,1)} %param.8) | copy-start | bytes 6291460
  91.8 21.7 %all-to-all-start.3 = ((bf16[4,8,64,256]{3,2,1,0:T(8,128)(2,1)}), bf16[4,8,64,256]{3,2,1,0:T(8,128)(2,1)}, u32[]{:S(2)}, u32[]{:S(2)}) async-start(bf16[4,8,64,256]{3,2,1,0:T(8,128)(2,1)} %bitcast.33), calls=%async_computation.3 | async-start | bytes 2097152 | tf_op jit(solution)/shard_map/all_to_all | solution.py:92
  96.2 17.3 %collective-permute-start.4 = (bf16[128,1024]{1,0:T(8,128)(2,1)S(1)}, bf16[128,1024]{1,0:T(8,128)(2,1)S(1)}, u32[]{:S(2)}, u32[]{:S(2)}) collective-permute-start(bf16[128,1024]{1,0:T(8,128)(2,1)S(1)} %get-tuple-element.26), channel_id=1, source_target_pairs={{0,280},{8,272},{16,264},{24,256},{32,312},{40,304},{48,296},{56,2... | collective-permute-start | bytes 786440 | tf_op jit(solution)/shard_map/ppermute | solution.py:88

commit v5 on v3

v5 whole, which is shorter than its diff:
```python
import math

import jax
import jax.numpy as jnp
from jax import lax
from jax.experimental import pallas as pl
from jax.experimental.pallas import tpu as pltpu
from jax.sharding import PartitionSpec as P

HEADS = 32
KVH = 4
HD = 128
SPAN = 64
N_SECTION = 2
N_Y = 8
N_Z = 4
N_CTX = 32
N_X = 4
N_CORE = 2
N_TP = 8
KEYS = N_CTX * SPAN * 2
ROWS = 128
HPD = 4
QROWS = HPD * ROWS
ALLROWS = 2 * QROWS
CHUNK = 512
NCHUNK = KEYS // CHUNK
EVERY = ("section", "ctx", "tp")
SCALE = HD ** (-0.5)
SCALE2 = SCALE * math.log2(math.e)
MIB = 1024 * 1024


def device_index(section, y, z, x, core):
    return (section * N_CTX + y * N_Z + z) * N_TP + x * N_CORE + core


def fold(u, w):
    return u + w * (N_Y - 1 - 2 * u)


def wide_groups():
    groups = []
    for section in range(N_SECTION):
        for x in range(N_X):
            for u in range(4):
                groups.append(
                    [device_index(section, fold(u, w), z, x, 0) for w in range(2) for z in range(N_Z)]
                )
            for z in range(N_Z):
                groups.append([device_index(section, y, z, x, 1) for y in range(N_Y)])
    return groups


def narrow_groups():
    groups = []
    for section in range(N_SECTION):
        for x in range(N_X):
            for w in range(2):
                for z in range(N_Z):
                    groups.append([device_index(section, fold(u, w), z, x, 0) for u in range(4)])
            for y in range(N_Y):
                groups.append([device_index(section, y, z, x, 1) for z in range(N_Z)])
    return groups


def block_owner(core):
    block = jnp.arange(N_CTX, dtype=jnp.int32)
    first, second = block // 8, block % 8
    owner_0 = fold(first, second // 4) * N_Z + second % 4
    owner_1 = second * N_Z + first
    return jnp.where(core == 0, owner_0, owner_1)


def swap_core(value):
    return lax.ppermute(value, "tp", [(i, i ^ 1) for i in range(N_TP)])


def mirror(ctx):
    return ctx - ctx % N_Z + N_Z - 1 - ctx % N_Z


def swap_section(value):
    pairs = [
        (section * N_CTX + ctx, (1 - section) * N_CTX + mirror(ctx))
        for section in range(N_SECTION)
        for ctx in range(N_CTX)
    ]
    return lax.ppermute(value, ("section", "ctx"), pairs)


def exchange(value, groups):
    return lax.all_to_all(value, EVERY, 0, 0, axis_index_groups=groups, tiled=True)


def project_kernel(x_ref, w_ref, o_ref):
    for g in range(KVH):
        o_ref[g] = nn(x_ref[...], w_ref[:, g * 2 * HD : (g + 1) * 2 * HD])


def project(features, weight):
    whole = pl.BlockSpec(memory_space=pltpu.VMEM)
    return pl.pallas_call(
        project_kernel,
        in_specs=[whole] * 2,
        out_specs=whole,
        out_shape=jax.ShapeDtypeStruct((KVH, ROWS, 2 * HD), jnp.float32),
        compiler_params=pltpu.CompilerParams(vmem_limit_bytes=16 * MIB),
        name="kv_project",
    )(features, weight)


def unproject_kernel(g_ref, w_ref, a_in, b_in, o_ref, a_out, b_out):
    a_out[...] = a_in[...]
    b_out[...] = b_in[...]
    total = nt(g_ref[0], w_ref[:, : 2 * HD])
    for g in range(1, KVH):
        total += nt(g_ref[g], w_ref[:, g * 2 * HD : (g + 1) * 2 * HD])
    o_ref[...] = total.astype(jnp.bfloat16)


def unproject(kv_grads, weight, out_b, grad_qb):
    whole = pl.BlockSpec(memory_space=pltpu.VMEM)
    return pl.pallas_call(
        unproject_kernel,
        in_specs=[whole] * 4,
        out_specs=[whole] * 3,
        out_shape=[
            jax.ShapeDtypeStruct((ROWS, weight.shape[0]), jnp.bfloat16),
            jax.ShapeDtypeStruct((ROWS, QROWS), jnp.bfloat16),
            jax.ShapeDtypeStruct((ROWS, QROWS), jnp.bfloat16),
        ],
        compiler_params=pltpu.CompilerParams(vmem_limit_bytes=16 * MIB),
        name="kv_unproject",
    )(kv_grads, weight, out_b, grad_qb)


def nt(a, b):
    return lax.dot_general(a, b, (((1,), (1,)), ((), ())), preferred_element_type=jnp.float32)


def nn(a, b):
    return jnp.dot(a, b, preferred_element_type=jnp.float32)


def attention_kernel(
    base_ref, qa_ref, qb_ref, ga_ref, gb_ref, own_ref, other_ref,
    oa_ref, gqa_ref, ob_ref, gqb_ref, gown_ref, gother_ref,
    q_s, g_s, kt_s, vt_s, s_s,
):
    for head in range(HPD):
        cols = slice(head * HD, (head + 1) * HD)
        rows_a = slice(head * ROWS, (head + 1) * ROWS)
        rows_b = slice(QROWS + head * ROWS, QROWS + (head + 1) * ROWS)
        q_s[rows_a, :] = qa_ref[:, cols]
        g_s[rows_a, :] = ga_ref[:, cols]
        q_s[rows_b, :] = qb_ref[:, cols]
        g_s[rows_b, :] = gb_ref[:, cols]
    queries = q_s[...]
    grads = g_s[...]

    def key_rows(c):
        ref = own_ref if c < NCHUNK // 2 else other_ref
        return ref, slice(c % (NCHUNK // 2) * CHUNK, (c % (NCHUNK // 2) + 1) * CHUNK)

    lane = lax.broadcasted_iota(jnp.int32, (1, ALLROWS), 1)
    row = lane % ROWS
    base_a = jnp.where(row < SPAN, base_ref[64], base_ref[65])
    base_b = jnp.where(row < SPAN, base_ref[66], base_ref[67])
    q_pos = jnp.where(lane < QROWS, base_a, base_b) + row % SPAN
    key_row = lax.broadcasted_iota(jnp.int32, (SPAN, ALLROWS), 0)

    top = jnp.full((8, ALLROWS), -1e30, jnp.float32)
    for c in range(NCHUNK):
        ref, rows = key_rows(c)
        start = c * CHUNK
        tile = nt(ref[rows, :HD], queries) * SCALE2
        kt_s[:, start : start + CHUNK] = ref[rows, :HD].T
        vt_s[:, start : start + CHUNK] = ref[rows, HD:].T
        for b in range(CHUNK // SPAN):
            base = base_ref[c * (CHUNK // SPAN) + b]
            part = jnp.where(key_row <= q_pos - base, tile[b * SPAN : (b + 1) * SPAN], -1e30)
            s_s[start + b * SPAN : start + (b + 1) * SPAN, :] = part
            top = jnp.maximum(top, jnp.max(part.reshape(SPAN // 8, 8, ALLROWS), axis=0))
    top = jnp.max(top, axis=0, keepdims=True)

    total = jnp.zeros((8, ALLROWS), jnp.float32)
    out = jnp.zeros((HD, ALLROWS), jnp.float32)
    for c in range(NCHUNK):
        start = c * CHUNK
        p = jnp.exp2(s_s[start : start + CHUNK, :] - top)
        total = total + jnp.sum(p.reshape(CHUNK // 8, 8, ALLROWS), axis=0)
        out = out + nn(vt_s[:, start : start + CHUNK], p.astype(jnp.bfloat16))
    inverse = 1.0 / jnp.sum(total, axis=0, keepdims=True)
    mixed = (out * inverse).astype(jnp.bfloat16).astype(jnp.float32)
    delta = jnp.sum(mixed * grads.astype(jnp.float32).T, axis=0, keepdims=True)

    grad_q = jnp.zeros((HD, ALLROWS), jnp.float32)
    for c in range(NCHUNK):
        ref, rows = key_rows(c)
        grad_ref = gown_ref if c < NCHUNK // 2 else gother_ref
        start = c * CHUNK
        p = jnp.exp2(s_s[start : start + CHUNK, :] - top) * inverse
        grad_p = nt(ref[rows, HD:], grads)
        grad_s = (p * (grad_p - delta)).astype(jnp.bfloat16)
        grad_ref[rows, HD:] = nn(p.astype(jnp.bfloat16), grads).astype(jnp.bfloat16)
        grad_ref[rows, :HD] = (nn(grad_s, queries) * SCALE).astype(jnp.bfloat16)
        grad_q = grad_q + nn(kt_s[:, start : start + CHUNK], grad_s)
    grad_q = grad_q * SCALE

    for head in range(HPD):
        cols = slice(head * HD, (head + 1) * HD)
        for first, o_ref, g_ref in ((0, oa_ref, gqa_ref), (QROWS, ob_ref, gqb_ref)):
            lanes = slice(first + head * ROWS, first + (head + 1) * ROWS)
            o_ref[:, cols] = mixed[:, lanes].T.astype(jnp.bfloat16)
            g_ref[:, cols] = grad_q[:, lanes].T.astype(jnp.bfloat16)


def attention(bases, qa, qb, ga, gb, own, other):
    half = KEYS // 2
    bf = jnp.bfloat16
    whole = pl.BlockSpec(memory_space=pltpu.VMEM)
    return pl.pallas_call(
        attention_kernel,
        in_specs=[pl.BlockSpec(memory_space=pltpu.SMEM)] + [whole] * 6,
        out_specs=[whole] * 6,
        out_shape=[
            jax.ShapeDtypeStruct((ROWS, HPD * HD), bf),
            jax.ShapeDtypeStruct((ROWS, HPD * HD), bf),
            jax.ShapeDtypeStruct((ROWS, HPD * HD), bf),
            jax.ShapeDtypeStruct((ROWS, HPD * HD), bf),
            jax.ShapeDtypeStruct((half, 2 * HD), bf),
            jax.ShapeDtypeStruct((half, 2 * HD), bf),
        ],
        scratch_shapes=[
            pltpu.VMEM((ALLROWS, HD), bf),
            pltpu.VMEM((ALLROWS, HD), bf),
            pltpu.VMEM((HD, KEYS), bf),
            pltpu.VMEM((HD, KEYS), bf),
            pltpu.VMEM((KEYS, ALLROWS), jnp.float32),
        ],
        compiler_params=pltpu.CompilerParams(vmem_limit_bytes=34 * MIB),
        cost_estimate=pl.CostEstimate(
            flops=24 * QROWS * KEYS * HD, bytes_accessed=6 * MIB, transcendentals=4 * QROWS * KEYS
        ),
        name="attention",
    )(bases, qa, qb, ga, gb, own, other)


def on_device(inputs, kv_weight, queries_a, queries_b, grads_a, grads_b, span_order):
    bf, f32 = jnp.bfloat16, jnp.float32
    weight = kv_weight[0]
    core = lax.axis_index("tp") % N_CORE
    ctx = lax.axis_index("ctx")
    wide, narrow = wide_groups(), narrow_groups()

    moved_q = swap_section(queries_b[0])
    moved_g = swap_section(grads_b[0])

    partial = project(inputs[0], weight)
    partial = lax.all_to_all(partial.reshape(N_TP, SPAN, 2 * HD), "tp", 0, 0, tiled=True)
    own = jnp.sum(partial, axis=0).astype(bf)

    own = exchange(jnp.broadcast_to(own[None], (8, SPAN, 2 * HD)), wide)
    own, moved_q = lax.optimization_barrier((own, moved_q))
    own = exchange(jnp.broadcast_to(own[None], (4, 8, SPAN, 2 * HD)), narrow)
    own, moved_g = lax.optimization_barrier((own, moved_g))
    own = own.reshape(N_CTX * SPAN, 2 * HD)
    other = swap_core(own)

    slots = jnp.concatenate(
        [2 * block_owner(core) + core, 2 * block_owner(1 - core) + 1 - core, 2 * ctx + jnp.arange(2), 2 * mirror(ctx) + jnp.arange(2)]
    )
    bases = span_order[slots] * SPAN

    out_a, grad_qa, out_b, grad_qb, grad_own, grad_other = attention(
        bases, queries_a[0], moved_q, grads_a[0], moved_g, own, other
    )
    out_b = swap_section(out_b)
    grad_qb = swap_section(grad_qb)
    grad_in = swap_core(grad_other)
    total = (grad_own.astype(f32) + grad_in.astype(f32)).astype(bf)
    total = exchange(total.reshape(4, 8, SPAN, 2 * HD), narrow)
    total, out_b = lax.optimization_barrier((total, out_b))
    total = jnp.sum(total.astype(f32), axis=0).astype(bf)
    total = exchange(total, wide)
    total, grad_qb = lax.optimization_barrier((total, grad_qb))
    total = jnp.sum(total.astype(f32), axis=0).astype(bf)
    total = lax.all_to_all(jnp.broadcast_to(total[None], (N_TP, SPAN, 2 * HD)), "tp", 0, 0, tiled=True)
    grad_x, out_b, grad_qb = unproject(
        total.reshape(KVH, ROWS, 2 * HD), weight, out_b, grad_qb
    )
    return out_a[None], out_b[None], grad_qa[None], grad_qb[None], grad_x[None]


def solution(mesh):
    split = P("section", "ctx", "tp")
    return jax.shard_map(
        on_device,
        mesh=mesh,
        in_specs=(split, P("section", "tp", None), split, split, split, split, P()),
        out_specs=(split,) * 5,
        check_vma=False,
    )
```

time: 156 us -> 144 us (0.923)
  waiting for transfers between devices: 42.6 us -> 33.5 us
  starting transfers between devices: 57.3 us -> 49.3 us
  blocking collectives: 27.1 us -> 31.5 us
    ppermute x4, waiting for transfers between devices: 35 us -> 16 us  [swap_section(): return lax.ppermute(value, ('section', 'ctx'), pairs)]
    all_to_all x2 -> x0, starting transfers between devices: 14.6 us -> none  [the longest x1 10.3 us: on_device(): lax.all_to_all(partial.reshape(N_TP, SPAN, 2 * HD), 'tp', 0, 0, tiled=True)]
    all_to_all x2 -> x4, waiting for transfers between devices: 0.49 us -> 14.5 us  [exchange(): lax.all_to_all(value, EVERY, 0, 0, axis_index_groups=groups, tiled=True)]
    ppermute x2, starting transfers between devices: 3.95 us -> 8.47 us  [swap_core(): return lax.ppermute(value, 'tp', [(i, i ^ 1) for i in range(N_TP)])]
    all_to_all x2, blocking collectives: 27.1 us -> 31.5 us  [the longest x1 18.6 us: on_device(): lax.all_to_all(partial.reshape(N_TP, SPAN, 2 * HD), 'tp', 0, 0, tiled=True)]
    all_to_all x2 -> x4, starting transfers between devices: 12.3 us -> 15.9 us  [exchange(): lax.all_to_all(value, EVERY, 0, 0, axis_index_groups=groups, tiled=True)]
    all_to_all x2 -> x0, waiting for transfers between devices: 3.34 us -> none  [the longest x1 3.33 us: on_device(): lax.all_to_all(partial.reshape(N_TP, SPAN, 2 * HD), 'tp', 0, 0, tiled=True)]
  transfers between devices with their start and end apart: 10 -> 10, of which waited for: 8 -> 9; matrix products, arithmetic and copies ran while one was open for 1% -> 1% of each run, Pallas kernels for 0% -> 0%
where the time goes in v5:
time: 144 us; the launch traced here: 143 us
  starting transfers between devices  49.3 us (34%)
  waiting for transfers between devices  33.5 us (23%)
  blocking collectives  31.5 us (22%)
  Pallas kernels  18.5 us (13%)
  local copies, waits for them, and re-layouts  5.65 us (4%)
  other arithmetic  3.65 us (3%)
    ppermute x4, starting transfers between devices, swap_section(): return lax.ppermute(value, ('section', 'ctx'), pairs)  24.9 us
    all_to_all x1, blocking collectives, on_device(): lax.all_to_all(partial.reshape(N_TP, SPAN, 2 * HD), 'tp', 0, 0, tiled=True)  18.6 us
    pallas_call x1, Pallas kernels, attention(): pl.pallas_call(attention_kernel, in_specs=[pl.BlockSpec(memory_space=pltp...  16.5 us
    ppermute x4, waiting for transfers between devices, swap_section(): return lax.ppermute(value, ('section', 'ctx'), pairs)  16 us
    all_to_all x4, starting transfers between devices, exchange(): lax.all_to_all(value, EVERY, 0, 0, axis_index_groups=groups, tiled=True)  15.9 us
    all_to_all x4, waiting for transfers between devices, exchange(): lax.all_to_all(value, EVERY, 0, 0, axis_index_groups=groups, tiled=True)  14.5 us
    all_to_all x1, blocking collectives, on_device(): lax.all_to_all(jnp.broadcast_to(total[None], (N_TP, SPAN, 2 * HD)), 'tp',...  12.9 us
    ppermute x2, starting transfers between devices, swap_core(): return lax.ppermute(value, 'tp', [(i, i ^ 1) for i in range(N_TP)])  8.47 us
  transfers between devices with their start and end apart: 10, of which 9 were waited for; matrix products, arithmetic and copies ran while one was open for 1% of the time, Pallas kernels for 0%

profile of v5, /device:TPU:1, one launch (start us, length us, event | category | flops | bytes accessed | tf_op | source)
XLA Modules:
  0.0 143.0 jit_solution(14483521941951577024)
XLA Ops:
  0.7 1.6 %copy-done.1 = bf16[1,1024,1024]{2,1,0:T(8,128)(2,1)S(1)} copy-done((bf16[1,1024,1024]{2,1,0:T(8,128)(2,1)S(1)}, bf16[1,1024,1024]{2,1,0:T(8,128)(2,1)}, u32[]{:S(2)}) %copy-start.1) | copy-done | bytes 2097176
  2.2 0.9 copy-done.3
  3.2 0.4 kv_project.1
  3.7 18.6 %all_to_all.30 = f32[8,64,256]{2,1,0:T(8,128)S(1)} all-to-all(f32[8,64,256]{2,1,0:T(8,128)S(1)} %bitcast.27), channel_id=1, replica_groups=mesh['section'=2,'ctx'=32,'tp'=8] {'tp'}, dimensions={0} | all-to-all | bytes 1048576 | tf_op jit(solution)/shard_map/all_to_all | solution.py:261
  22.3 0.7 broadcast_in_dim.16
  23.1 3.4 %all-to-all-start.1 = ((bf16[8,64,256]{2,1,0:T(8,128)(2,1)}), bf16[8,64,256]{2,1,0:T(8,128)(2,1)S(1)}, u32[]{:S(2)}, u32[]{:S(2)}) async-start(bf16[8,64,256]{2,1,0:T(8,128)(2,1)} %broadcast_in_dim.16), calls=%async_computation.1 | async-start | bytes 524288 | tf_op jit(solution)/shard_map/all_to_all | solution.py:93
  26.5 10.5 %collective-permute-start = (bf16[128,512]{1,0:T(8,128)(2,1)S(1)}, bf16[128,512]{1,0:T(8,128)(2,1)S(1)}, u32[]{:S(2)}, u32[]{:S(2)}) collective-permute-start(bf16[128,512]{1,0:T(8,128)(2,1)S(1)} %bitcast.36), channel_id=1, source_target_pairs={{0,280},{8,272},{16,264},{24,256},{32,312},{40,304},{48,296},{56,2... | collective-permute-start | bytes 393224 | tf_op jit(solution)/shard_map/ppermute | solution.py:89
  37.0 5.1 %collective-permute-done.qb_ref = bf16[128,512]{1,0:T(8,128)(2,1)S(1)} collective-permute-done((bf16[128,512]{1,0:T(8,128)(2,1)S(1)}, bf16[128,512]{1,0:T(8,128)(2,1)S(1)}, u32[]{:S(2)}, u32[]{:S(2)}) %collective-permute-start) | collective-permute-done | bytes 131104 | tf_op jit(solution)/shard_map/ppermute | solution.py:89
  42.1 1.1 broadcast_in_dim.17
  43.2 3.5 %all-to-all-start.2 = ((bf16[4,8,64,256]{3,2,1,0:T(8,128)(2,1)}), bf16[4,8,64,256]{3,2,1,0:T(8,128)(2,1)S(1)}, u32[]{:S(2)}, u32[]{:S(2)}) async-start(bf16[4,8,64,256]{3,2,1,0:T(8,128)(2,1)} %broadcast_in_dim.17), calls=%async_computation.2 | async-start | bytes 2097152 | tf_op jit(solution)/shard_map/all_to_all | solution.py:93
  46.8 6.0 %collective-permute-start.1 = (bf16[128,512]{1,0:T(8,128)(2,1)S(1)}, bf16[128,512]{1,0:T(8,128)(2,1)S(1)}, u32[]{:S(2)}, u32[]{:S(2)}) collective-permute-start(bf16[128,512]{1,0:T(8,128)(2,1)S(1)} %bitcast.37), channel_id=1, source_target_pairs={{0,280},{8,272},{16,264},{24,256},{32,312},{40,304},{48,296},{56,2... | collective-permute-start | bytes 393224 | tf_op jit(solution)/shard_map/ppermute | solution.py:89
  52.8 2.9 %collective-permute-done.1.gb_ref = bf16[128,512]{1,0:T(8,128)(2,1)S(1)} collective-permute-done((bf16[128,512]{1,0:T(8,128)(2,1)S(1)}, bf16[128,512]{1,0:T(8,128)(2,1)S(1)}, u32[]{:S(2)}, u32[]{:S(2)}) %collective-permute-start.1) | collective-permute-done | bytes 131104 | tf_op jit(solution)/shard_map/ppermute | solution.py:89
  55.7 6.1 %all-to-all-done.2 = bf16[4,8,64,256]{3,2,1,0:T(8,128)(2,1)S(1)} async-done(((bf16[4,8,64,256]{3,2,1,0:T(8,128)(2,1)}), bf16[4,8,64,256]{3,2,1,0:T(8,128)(2,1)S(1)}, u32[]{:S(2)}, u32[]{:S(2)}) %all-to-all-start.2) | async-done | bytes 1048608 | tf_op jit(solution)/shard_map/all_to_all | solution.py:93
  61.8 6.2 %collective-permute-start.2 = (bf16[2048,256]{1,0:T(8,128)(2,1)S(1)}, bf16[2048,256]{1,0:T(8,128)(2,1)S(1)}, u32[]{:S(2)}, u32[]{:S(2)}) collective-permute-start(bf16[2048,256]{1,0:T(8,128)(2,1)S(1)} %bitcast.29), channel_id=1, source_target_pairs={{0,1},{1,0},{2,3},{3,2},{4,5},{5,4},{6,7},{7,6},{8,9},{9,8},{10,11... | collective-permute-start | bytes 3145736 | tf_op jit(solution)/shard_map/ppermute | solution.py:76
  68.1 0.1 fusion.5
  68.2 1.2 gather_fusion
  69.4 0.9 collective-permute-done.2.other_ref
  70.3 16.5 %attention.1 = (bf16[128,512]{1,0:T(8,128)(2,1)}, bf16[128,512]{1,0:T(8,128)(2,1)}, bf16[128,512]{1,0:T(8,128)(2,1)S(1)}, bf16[128,512]{1,0:T(8,128)(2,1)S(1)}, ...) custom-call(s32[68]{0:T(128)S(1)} %broadcast_multiply_fusion.base_ref, bf16[128,512]{1,0:T(8,128)(2,1)S(1)} %bitcast.32, ...), custom_call_target="tpu_custom_call" | custom-call | flops 6442450944 | bytes 6291456 | tf_op jit(solution)/shard_map/attention/pallas_call | solution.py:223
  86.8 2.3 %collective-permute-start.3 = (bf16[2048,256]{1,0:T(8,128)(2,1)S(1)}, bf16[2048,256]{1,0:T(8,128)(2,1)S(1)}, u32[]{:S(2)}, u32[]{:S(2)}) collective-permute-start(bf16[2048,256]{1,0:T(8,128)(2,1)S(1)} %get-tuple-element.28), channel_id=1, source_target_pairs={{0,1},{1,0},{2,3},{3,2},{4,5},{5,4},{6,7},{7,6},{8,9},{9,8},{10,11... | collective-permute-start | bytes 3145736 | tf_op jit(solution)/shard_map/ppermute | solution.py:76
  89.1 2.3 %collective-permute-done.3 = bf16[2048,256]{1,0:T(8,128)(2,1)S(1)} collective-permute-done((bf16[2048,256]{1,0:T(8,128)(2,1)S(1)}, bf16[2048,256]{1,0:T(8,128)(2,1)S(1)}, u32[]{:S(2)}, u32[]{:S(2)}) %collective-permute-start.3) | collective-permute-done | bytes 1048608 | tf_op jit(solution)/shard_map/ppermute | solution.py:76
  91.3 1.3 add_convert_fusion
  92.6 4.4 %all-to-all-start.3 = ((bf16[4,8,64,256]{3,2,1,0:T(8,128)(2,1)}), bf16[4,8,64,256]{3,2,1,0:T(8,128)(2,1)}, u32[]{:S(2)}, u32[]{:S(2)}) async-start(bf16[4,8,64,256]{3,2,1,0:T(8,128)(2,1)} %bitcast.34), calls=%async_computation.3 | async-start | bytes 2097152 | tf_op jit(solution)/shard_map/all_to_all | solution.py:93
  97.0 5.2 %collective-permute-start.4 = (bf16[128,512]{1,0:T(8,128)(2,1)S(1)}, bf16[128,512]{1,0:T(8,128)(2,1)S(1)}, u32[]{:S(2)}, u32[]{:S(2)}) collective-permute-start(bf16[128,512]{1,0:T(8,128)(2,1)S(1)} %get-tuple-element.29), channel_id=1, source_target_pairs={{0,280},{8,272},{16,264},{24,256},{32,312},{40,304},{48,296},{56,2... | collective-permute-start | bytes 393224 | tf_op jit(solution)/shard_map/ppermute | solution.py:89
  102.2 4.0 %collective-permute-done.4.a_in = bf16[128,512]{1,0:T(8,128)(2,1)S(1)} collective-permute-done((bf16[128,512]{1,0:T(8,128)(2,1)S(1)}, bf16[128,512]{1,0:T(8,128)(2,1)S(1)}, u32[]{:S(2)}, u32[]{:S(2)}) %collective-permute-start.4) | collective-permute-done | bytes 131104 | tf_op jit(solution)/shard_map/ppermute | solution.py:89
  106.2 5.9 %all-to-all-done.3 = bf16[4,8,64,256]{3,2,1,0:T(8,128)(2,1)} async-done(((bf16[4,8,64,256]{3,2,1,0:T(8,128)(2,1)}), bf16[4,8,64,256]{3,2,1,0:T(8,128)(2,1)}, u32[]{:S(2)}, u32[]{:S(2)}) %all-to-all-start.3) | async-done | bytes 1048608 | tf_op jit(solution)/shard_map/all_to_all | solution.py:93
  112.1 2.2 %reduce_sum.34 = bf16[8,64,256]{2,1,0:T(8,128)(2,1)} reduce(bf16[4,8,64,256]{3,2,1,0:T(8,128)(2,1)} %all-to-all-done.3, bf16[]{:T(256)} %constant.100.clone.1), dimensions={0}, to_apply=%region_1.2 | reduce | flops 393216 | bytes 1310722 | tf_op jit(solution)/shard_map/reduce_sum | solution.py:285
  114.3 4.6 %all-to-all-start.4 = ((bf16[8,64,256]{2,1,0:T(8,128)(2,1)}), bf16[8,64,256]{2,1,0:T(8,128)(2,1)S(1)}, u32[]{:S(2)}, u32[]{:S(2)}) async-start(bf16[8,64,256]{2,1,0:T(8,128)(2,1)} %reduce_sum.34), calls=%async_computation.4 | async-start | bytes 524288 | tf_op jit(solution)/shard_map/all_to_all | solution.py:93
  118.8 3.2 %collective-permute-start.5 = (bf16[128,512]{1,0:T(8,128)(2,1)S(1)}, bf16[128,512]{1,0:T(8,128)(2,1)S(1)}, u32[]{:S(2)}, u32[]{:S(2)}) collective-permute-start(bf16[128,512]{1,0:T(8,128)(2,1)S(1)} %get-tuple-element.31), channel_id=1, source_target_pairs={{0,280},{8,272},{16,264},{24,256},{32,312},{40,304},{48,296},{56,2... | collective-permute-start | bytes 393224 | tf_op jit(solution)/shard_map/ppermute | solution.py:89
  122.0 4.0 %collective-permute-done.5.b_in = bf16[128,512]{1,0:T(8,128)(2,1)S(1)} collective-permute-done((bf16[128,512]{1,0:T(8,128)(2,1)S(1)}, bf16[128,512]{1,0:T(8,128)(2,1)S(1)}, u32[]{:S(2)}, u32[]{:S(2)}) %collective-permute-start.5) | collective-permute-done | bytes 131104 | tf_op jit(solution)/shard_map/ppermute | solution.py:89
  126.0 2.4 %all-to-all-done.4 = bf16[8,64,256]{2,1,0:T(8,128)(2,1)S(1)} async-done(((bf16[8,64,256]{2,1,0:T(8,128)(2,1)}), bf16[8,64,256]{2,1,0:T(8,128)(2,1)S(1)}, u32[]{:S(2)}, u32[]{:S(2)}) %all-to-all-start.4) | async-done | bytes 262176 | tf_op jit(solution)/shard_map/all_to_all | solution.py:93
  128.6 12.9 %all_to_all.31 = bf16[8,64,256]{2,1,0:T(8,128)(2,1)S(1)} all-to-all(bf16[8,64,256]{2,1,0:T(8,128)(2,1)S(1)} %broadcast_in_dim.37), channel_id=1, replica_groups=mesh['section'=2,'ctx'=32,'tp'=8] {'tp'}, dimensions={0} | all-to-all | bytes 524288 | tf_op jit(solution)/shard_map/all_to_all | solution.py:289
  141.4 1.5 %kv_unproject.1 = (bf16[128,1024]{1,0:T(8,128)(2,1)}, bf16[128,512]{1,0:T(8,128)(2,1)}, bf16[128,512]{1,0:T(8,128)(2,1)}) custom-call(bf16[4,128,256]{2,1,0:T(8,128)(2,1)S(1)} %bitcast.28, bf16[1024,1024]{1,0:T(8,128)(2,1)S(1)} %bitcast.26, bf16[128,512]{1,0:T(8,128)(2,1)S(1)} %collective-permute-done.4.a_in, bf16[128,512]{1,0:T(8,128)(2,1)S(1)} %collective-permute-done.5.b_in), custom_call_target="tpu_custom_call" | custom-call | tf_op jit(solution)/shard_map/kv_unproject/pallas_call | solution.py:124
  (22 shorter events, 0.2 us)
Async XLA Ops:
  0.6 67.5 %copy-start = (s32[64]{0:T(128)S(1)}, s32[64]{0:T(128)}, u32[]{:S(2)}) copy-start(s32[64]{0:T(128)} %param.13) | copy-start | bytes 772
  0.6 1.6 %copy-start.1 = (bf16[1,1024,1024]{2,1,0:T(8,128)(2,1)S(1)}, bf16[1,1024,1024]{2,1,0:T(8,128)(2,1)}, u32[]{:S(2)}) copy-start(bf16[1,1024,1024]{2,1,0:T(8,128)(2,1)} %param.8) | copy-start | bytes 6291460
  2.2 0.9 copy-start.3
  3.2 23.3 %copy-start.6 = (bf16[1,128,512]{2,1,0:T(8,128)(2,1)S(1)}, bf16[1,128,512]{2,1,0:T(8,128)(2,1)}, u32[]{:S(2)}) copy-start(bf16[1,128,512]{2,1,0:T(8,128)(2,1)} %param.10) | copy-start | bytes 393220
  22.3 24.4 %copy-start.7 = (bf16[1,128,512]{2,1,0:T(8,128)(2,1)S(1)}, bf16[1,128,512]{2,1,0:T(8,128)(2,1)}, u32[]{:S(2)}) copy-start(bf16[1,128,512]{2,1,0:T(8,128)(2,1)} %param.12) | copy-start | bytes 393220
  23.1 19.1 %all-to-all-start.1 = ((bf16[8,64,256]{2,1,0:T(8,128)(2,1)}), bf16[8,64,256]{2,1,0:T(8,128)(2,1)S(1)}, u32[]{:S(2)}, u32[]{:S(2)}) async-start(bf16[8,64,256]{2,1,0:T(8,128)(2,1)} %broadcast_in_dim.16), calls=%async_computation.1 | async-start | bytes 524288 | tf_op jit(solution)/shard_map/all_to_all | solution.py:93
  26.5 43.8 %copy-start.4 = (bf16[1,128,512]{2,1,0:T(8,128)(2,1)S(1)}, bf16[1,128,512]{2,1,0:T(8,128)(2,1)}, u32[]{:S(2)}) copy-start(bf16[1,128,512]{2,1,0:T(8,128)(2,1)} %param.9) | copy-start | bytes 393220
  26.5 43.8 %copy-start.5 = (bf16[1,128,512]{2,1,0:T(8,128)(2,1)S(1)}, bf16[1,128,512]{2,1,0:T(8,128)(2,1)}, u32[]{:S(2)}) copy-start(bf16[1,128,512]{2,1,0:T(8,128)(2,1)} %param.11) | copy-start | bytes 393220
  26.5 15.6 %collective-permute-start = (bf16[128,512]{1,0:T(8,128)(2,1)S(1)}, bf16[128,512]{1,0:T(8,128)(2,1)S(1)}, u32[]{:S(2)}, u32[]{:S(2)}) collective-permute-start(bf16[128,512]{1,0:T(8,128)(2,1)S(1)} %bitcast.36), channel_id=1, source_target_pairs={{0,280},{8,272},{16,264},{24,256},{32,312},{40,304},{48,296},{56,2... | collective-permute-start | bytes 393224 | tf_op jit(solution)/shard_map/ppermute | solution.py:89
  43.2 18.5 %all-to-all-start.2 = ((bf16[4,8,64,256]{3,2,1,0:T(8,128)(2,1)}), bf16[4,8,64,256]{3,2,1,0:T(8,128)(2,1)S(1)}, u32[]{:S(2)}, u32[]{:S(2)}) async-start(bf16[4,8,64,256]{3,2,1,0:T(8,128)(2,1)} %broadcast_in_dim.17), calls=%async_computation.2 | async-start | bytes 2097152 | tf_op jit(solution)/shard_map/all_to_all | solution.py:93
  46.8 8.9 %collective-permute-start.1 = (bf16[128,512]{1,0:T(8,128)(2,1)S(1)}, bf16[128,512]{1,0:T(8,128)(2,1)S(1)}, u32[]{:S(2)}, u32[]{:S(2)}) collective-permute-start(bf16[128,512]{1,0:T(8,128)(2,1)S(1)} %bitcast.37), channel_id=1, source_target_pairs={{0,280},{8,272},{16,264},{24,256},{32,312},{40,304},{48,296},{56,2... | collective-permute-start | bytes 393224 | tf_op jit(solution)/shard_map/ppermute | solution.py:89
  61.8 8.5 %collective-permute-start.2 = (bf16[2048,256]{1,0:T(8,128)(2,1)S(1)}, bf16[2048,256]{1,0:T(8,128)(2,1)S(1)}, u32[]{:S(2)}, u32[]{:S(2)}) collective-permute-start(bf16[2048,256]{1,0:T(8,128)(2,1)S(1)} %bitcast.29), channel_id=1, source_target_pairs={{0,1},{1,0},{2,3},{3,2},{4,5},{5,4},{6,7},{7,6},{8,9},{9,8},{10,11... | collective-permute-start | bytes 3145736 | tf_op jit(solution)/shard_map/ppermute | solution.py:76
  86.8 4.5 %collective-permute-start.3 = (bf16[2048,256]{1,0:T(8,128)(2,1)S(1)}, bf16[2048,256]{1,0:T(8,128)(2,1)S(1)}, u32[]{:S(2)}, u32[]{:S(2)}) collective-permute-start(bf16[2048,256]{1,0:T(8,128)(2,1)S(1)} %get-tuple-element.28), channel_id=1, source_target_pairs={{0,1},{1,0},{2,3},{3,2},{4,5},{5,4},{6,7},{7,6},{8,9},{9,8},{10,11... | collective-permute-start | bytes 3145736 | tf_op jit(solution)/shard_map/ppermute | solution.py:76
  92.6 48.8 %copy-start.2 = (bf16[1,1024,1024]{2,1,0:T(8,128)(2,1)S(1)}, bf16[1,1024,1024]{2,1,0:T(8,128)(2,1)}, u32[]{:S(2)}) copy-start(bf16[1,1024,1024]{2,1,0:T(8,128)(2,1)} %param.8) | copy-start | bytes 6291460
  92.6 19.5 %all-to-all-start.3 = ((bf16[4,8,64,256]{3,2,1,0:T(8,128)(2,1)}), bf16[4,8,64,256]{3,2,1,0:T(8,128)(2,1)}, u32[]{:S(2)}, u32[]{:S(2)}) async-start(bf16[4,8,64,256]{3,2,1,0:T(8,128)(2,1)} %bitcast.34), calls=%async_computation.3 | async-start | bytes 2097152 | tf_op jit(solution)/shard_map/all_to_all | solution.py:93
  97.0 9.2 %collective-permute-start.4 = (bf16[128,512]{1,0:T(8,128)(2,1)S(1)}, bf16[128,512]{1,0:T(8,128)(2,1)S(1)}, u32[]{:S(2)}, u32[]{:S(2)}) collective-permute-start(bf16[128,512]{1,0:T(8,128)(2,1)S(1)} %get-tuple-element.29), channel_id=1, source_target_pairs={{0,280},{8,272},{16,264},{24,256},{32,312},{40,304},{48,296},{56,2... | collective-permute-start | bytes 393224 | tf_op jit(solution)/shard_map/ppermute | solution.py:89
  114.3 14.2 %all-to-all-start.4 = ((bf16[8,64,256]{2,1,0:T(8,128)(2,1)}), bf16[8,64,256]{2,1,0:T(8,128)(2,1)S(1)}, u32[]{:S(2)}, u32[]{:S(2)}) async-start(bf16[8,64,256]{2,1,0:T(8,128)(2,1)} %reduce_sum.34), calls=%async_computation.4 | async-start | bytes 524288 | tf_op jit(solution)/shard_map/all_to_all | solution.py:93
  118.8 7.2 %collective-permute-start.5 = (bf16[128,512]{1,0:T(8,128)(2,1)S(1)}, bf16[128,512]{1,0:T(8,128)(2,1)S(1)}, u32[]{:S(2)}, u32[]{:S(2)}) collective-permute-start(bf16[128,512]{1,0:T(8,128)(2,1)S(1)} %get-tuple-element.31), channel_id=1, source_target_pairs={{0,280},{8,272},{16,264},{24,256},{32,312},{40,304},{48,296},{56,2... | collective-permute-start | bytes 393224 | tf_op jit(solution)/shard_map/ppermute | solution.py:89

commit v6 on v5

--- a/solution.py
+++ b/solution.py
@@ -110,20 +110,20 @@
     )(features, weight)
 
 
-def unproject_kernel(g_ref, w_ref, a_in, b_in, o_ref, a_out, b_out):
-    a_out[...] = a_in[...]
-    b_out[...] = b_in[...]
+def unproject_kernel(g_ref, w_ref, back_ref, o_ref, a_out, b_out):
+    a_out[...] = back_ref[:, :QROWS]
+    b_out[...] = back_ref[:, QROWS:]
     total = nt(g_ref[0], w_ref[:, : 2 * HD])
     for g in range(1, KVH):
         total += nt(g_ref[g], w_ref[:, g * 2 * HD : (g + 1) * 2 * HD])
     o_ref[...] = total.astype(jnp.bfloat16)
 
 
-def unproject(kv_grads, weight, out_b, grad_qb):
+def unproject(kv_grads, weight, back):
     whole = pl.BlockSpec(memory_space=pltpu.VMEM)
     return pl.pallas_call(
         unproject_kernel,
-        in_specs=[whole] * 4,
+        in_specs=[whole] * 3,
         out_specs=[whole] * 3,
         out_shape=[
             jax.ShapeDtypeStruct((ROWS, weight.shape[0]), jnp.bfloat16),
@@ -132,7 +132,7 @@
         ],
         compiler_params=pltpu.CompilerParams(vmem_limit_bytes=16 * MIB),
         name="kv_unproject",
-    )(kv_grads, weight, out_b, grad_qb)
+    )(kv_grads, weight, back)
 
 
 def nt(a, b):
@@ -144,8 +144,8 @@
 
 
 def attention_kernel(
-    base_ref, qa_ref, qb_ref, ga_ref, gb_ref, own_ref, other_ref,
-    oa_ref, gqa_ref, ob_ref, gqb_ref, gown_ref, gother_ref,
+    base_ref, qa_ref, ga_ref, moved_ref, own_ref, other_ref,
+    oa_ref, gqa_ref, back_ref, gown_ref, gother_ref,
     q_s, g_s, kt_s, vt_s, s_s,
 ):
     for head in range(HPD):
@@ -154,8 +154,8 @@
         rows_b = slice(QROWS + head * ROWS, QROWS + (head + 1) * ROWS)
         q_s[rows_a, :] = qa_ref[:, cols]
         g_s[rows_a, :] = ga_ref[:, cols]
-        q_s[rows_b, :] = qb_ref[:, cols]
-        g_s[rows_b, :] = gb_ref[:, cols]
+        q_s[rows_b, :] = moved_ref[:, cols]
+        g_s[rows_b, :] = moved_ref[:, QROWS + head * HD : QROWS + (head + 1) * HD]
     queries = q_s[...]
     grads = g_s[...]
 
@@ -210,25 +210,25 @@
 
     for head in range(HPD):
         cols = slice(head * HD, (head + 1) * HD)
-        for first, o_ref, g_ref in ((0, oa_ref, gqa_ref), (QROWS, ob_ref, gqb_ref)):
-            lanes = slice(first + head * ROWS, first + (head + 1) * ROWS)
-            o_ref[:, cols] = mixed[:, lanes].T.astype(jnp.bfloat16)
-            g_ref[:, cols] = grad_q[:, lanes].T.astype(jnp.bfloat16)
-
-
-def attention(bases, qa, qb, ga, gb, own, other):
+        late_cols = slice(QROWS + head * HD, QROWS + (head + 1) * HD)
+        oa_ref[:, cols] = mixed[:, cols].T.astype(jnp.bfloat16)
+        gqa_ref[:, cols] = grad_q[:, cols].T.astype(jnp.bfloat16)
+        back_ref[:, cols] = mixed[:, late_cols].T.astype(jnp.bfloat16)
+        back_ref[:, late_cols] = grad_q[:, late_cols].T.astype(jnp.bfloat16)
+
+
+def attention(bases, qa, ga, moved, own, other):
     half = KEYS // 2
     bf = jnp.bfloat16
     whole = pl.BlockSpec(memory_space=pltpu.VMEM)
     return pl.pallas_call(
         attention_kernel,
-        in_specs=[pl.BlockSpec(memory_space=pltpu.SMEM)] + [whole] * 6,
-        out_specs=[whole] * 6,
+        in_specs=[pl.BlockSpec(memory_space=pltpu.SMEM)] + [whole] * 5,
+        out_specs=[whole] * 5,
         out_shape=[
-            jax.ShapeDtypeStruct((ROWS, HPD * HD), bf),
-            jax.ShapeDtypeStruct((ROWS, HPD * HD), bf),
-            jax.ShapeDtypeStruct((ROWS, HPD * HD), bf),
-            jax.ShapeDtypeStruct((ROWS, HPD * HD), bf),
+            jax.ShapeDtypeStruct((ROWS, QROWS), bf),
+            jax.ShapeDtypeStruct((ROWS, QROWS), bf),
+            jax.ShapeDtypeStruct((ROWS, ALLROWS), bf),
             jax.ShapeDtypeStruct((half, 2 * HD), bf),
             jax.ShapeDtypeStruct((half, 2 * HD), bf),
         ],
@@ -244,7 +244,7 @@
             flops=24 * QROWS * KEYS * HD, bytes_accessed=6 * MIB, transcendentals=4 * QROWS * KEYS
         ),
         name="attention",
-    )(bases, qa, qb, ga, gb, own, other)
+    )(bases, qa, ga, moved, own, other)
 
 
 def on_device(inputs, kv_weight, queries_a, queries_b, grads_a, grads_b, span_order):
@@ -254,17 +254,15 @@
     ctx = lax.axis_index("ctx")
     wide, narrow = wide_groups(), narrow_groups()
 
-    moved_q = swap_section(queries_b[0])
-    moved_g = swap_section(grads_b[0])
+    moved = swap_section(jnp.concatenate([queries_b[0], grads_b[0]], axis=1))
 
     partial = project(inputs[0], weight)
     partial = lax.all_to_all(partial.reshape(N_TP, SPAN, 2 * HD), "tp", 0, 0, tiled=True)
     own = jnp.sum(partial, axis=0).astype(bf)
 
     own = exchange(jnp.broadcast_to(own[None], (8, SPAN, 2 * HD)), wide)
-    own, moved_q = lax.optimization_barrier((own, moved_q))
     own = exchange(jnp.broadcast_to(own[None], (4, 8, SPAN, 2 * HD)), narrow)
-    own, moved_g = lax.optimization_barrier((own, moved_g))
+    own, moved = lax.optimization_barrier((own, moved))
     own = own.reshape(N_CTX * SPAN, 2 * HD)
     other = swap_core(own)
 
@@ -273,22 +271,20 @@
     )
     bases = span_order[slots] * SPAN
 
-    out_a, grad_qa, out_b, grad_qb, grad_own, grad_other = attention(
-        bases, queries_a[0], moved_q, grads_a[0], moved_g, own, other
+    out_a, grad_qa, back, grad_own, grad_other = attention(
+        bases, queries_a[0], grads_a[0], moved, own, other
     )
-    out_b = swap_section(out_b)
-    grad_qb = swap_section(grad_qb)
+    back = swap_section(back)
     grad_in = swap_core(grad_other)
     total = (grad_own.astype(f32) + grad_in.astype(f32)).astype(bf)
     total = exchange(total.reshape(4, 8, SPAN, 2 * HD), narrow)
-    total, out_b = lax.optimization_barrier((total, out_b))
+    total, back = lax.optimization_barrier((total, back))
     total = jnp.sum(total.astype(f32), axis=0).astype(bf)
     total = exchange(total, wide)
-    total, grad_qb = lax.optimization_barrier((total, grad_qb))
     total = jnp.sum(total.astype(f32), axis=0).astype(bf)
     total = lax.all_to_all(jnp.broadcast_to(total[None], (N_TP, SPAN, 2 * HD)), "tp", 0, 0, tiled=True)
     grad_x, out_b, grad_qb = unproject(
-        total.reshape(KVH, ROWS, 2 * HD), weight, out_b, grad_qb
+        total.reshape(KVH, ROWS, 2 * HD), weight, back
     )
     return out_a[None], out_b[None], grad_qa[None], grad_qb[None], grad_x[None]
 

time: 144 us -> 140 us (0.972)
  blocking collectives: 31.5 us -> 55 us
  starting transfers between devices: 49.3 us -> 31.5 us
  waiting for transfers between devices: 33.5 us -> 26.1 us
    all_to_all x0 -> x2, blocking collectives: none -> 23.6 us  [exchange(): lax.all_to_all(value, EVERY, 0, 0, axis_index_groups=groups, tiled=True)]
    all_to_all x4 -> x2, waiting for transfers between devices: 14.5 us -> 0.01 us  [exchange(): lax.all_to_all(value, EVERY, 0, 0, axis_index_groups=groups, tiled=True)]
    ppermute x4 -> x2, starting transfers between devices: 24.9 us -> 14.4 us  [swap_section(): return lax.ppermute(value, ('section', 'ctx'), pairs)]
    ppermute x4 -> x2, waiting for transfers between devices: 16 us -> 23 us  [swap_section(): return lax.ppermute(value, ('section', 'ctx'), pairs)]
    ppermute x2, starting transfers between devices: 8.47 us -> 4.85 us  [swap_core(): return lax.ppermute(value, 'tp', [(i, i ^ 1) for i in range(N_TP)])]
    all_to_all x4 -> x2, starting transfers between devices: 15.9 us -> 12.3 us  [exchange(): lax.all_to_all(value, EVERY, 0, 0, axis_index_groups=groups, tiled=True)]
  transfers between devices with their start and end apart: 10 -> 6, of which waited for: 9 -> 4; matrix products, arithmetic and copies ran while one was open for 1% -> 1% of each run, Pallas kernels for 0% -> 0%
where the time goes in v6:
time: 140 us
  blocking collectives  55 us (39%)
  starting transfers between devices  31.5 us (22%)
  waiting for transfers between devices  26.1 us (19%)
  Pallas kernels  18.5 us (13%)
  local copies, waits for them, and re-layouts  4.93 us (4%)
  other arithmetic  2.9 us (2%)
    all_to_all x2, blocking collectives, exchange(): lax.all_to_all(value, EVERY, 0, 0, axis_index_groups=groups, tiled=True)  23.6 us
    ppermute x2, waiting for transfers between devices, swap_section(): return lax.ppermute(value, ('section', 'ctx'), pairs)  23 us
    all_to_all x1, blocking collectives, on_device(): lax.all_to_all(partial.reshape(N_TP, SPAN, 2 * HD), 'tp', 0, 0, tiled=True)  18.6 us
    pallas_call x1, Pallas kernels, attention(): pl.pallas_call(attention_kernel, in_specs=[pl.BlockSpec(memory_space=pltp...  16.5 us
    ppermute x2, starting transfers between devices, swap_section(): return lax.ppermute(value, ('section', 'ctx'), pairs)  14.4 us
    all_to_all x1, blocking collectives, on_device(): lax.all_to_all(jnp.broadcast_to(total[None], (N_TP, SPAN, 2 * HD)), 'tp',...  12.8 us
    all_to_all x2, starting transfers between devices, exchange(): lax.all_to_all(value, EVERY, 0, 0, axis_index_groups=groups, tiled=True)  12.3 us
    ppermute x2, starting transfers between devices, swap_core(): return lax.ppermute(value, 'tp', [(i, i ^ 1) for i in range(N_TP)])  4.85 us
  transfers between devices with their start and end apart: 6, of which 4 were waited for; matrix products, arithmetic and copies ran while one was open for 1% of the time, Pallas kernels for 0%

profile of v6, /device:TPU:1, one launch (start us, length us, event | category | flops | bytes accessed | tf_op | source)
XLA Modules:
  0.0 139.8 jit_solution(13699441858748649820)
XLA Ops:
  0.6 0.0 copy-start
  0.6 0.0 copy-start.1
  0.7 1.6 %copy-done.1 = bf16[1,1024,1024]{2,1,0:T(8,128)(2,1)S(1)} copy-done((bf16[1,1024,1024]{2,1,0:T(8,128)(2,1)S(1)}, bf16[1,1024,1024]{2,1,0:T(8,128)(2,1)}, u32[]{:S(2)}) %copy-start.1) | copy-done | bytes 2097176
  2.2 0.9 copy-done.3
  3.2 0.4 kv_project.1
  3.6 18.6 %all_to_all.30 = f32[8,64,256]{2,1,0:T(8,128)S(1)} all-to-all(f32[8,64,256]{2,1,0:T(8,128)S(1)} %bitcast.27), channel_id=1, replica_groups=mesh['section'=2,'ctx'=32,'tp'=8] {'tp'}, dimensions={0} | all-to-all | bytes 1048576 | tf_op jit(solution)/shard_map/all_to_all | solution.py:260
  22.3 0.0 copy-start.6
  22.3 0.0 copy-start.7
  22.4 12.4 %all_to_all.31 = bf16[8,64,256]{2,1,0:T(8,128)(2,1)S(1)} all-to-all(bf16[8,64,256]{2,1,0:T(8,128)(2,1)S(1)} %broadcast_in_dim.16), channel_id=1, replica_groups={{0,8,16,24,224,232,240,248},{32,40,48,56,192,200,208,216},{64,72,80,88,..., dimensions={0} | all-to-all | bytes 524288 | tf_op jit(solution)/shard_map/all_to_all | solution.py:93
  34.8 1.1 broadcast_in_dim.17
  35.9 7.9 %all-to-all-start.2 = ((bf16[4,8,64,256]{3,2,1,0:T(8,128)(2,1)}), bf16[4,8,64,256]{3,2,1,0:T(8,128)(2,1)S(1)}, u32[]{:S(2)}, u32[]{:S(2)}) async-start(bf16[4,8,64,256]{3,2,1,0:T(8,128)(2,1)} %broadcast_in_dim.17), calls=%async_computation.2 | async-start | bytes 2097152 | tf_op jit(solution)/shard_map/all_to_all | solution.py:93
  43.8 0.0 copy-done.6
  43.8 0.0 copy-done.7
  43.9 8.2 %collective-permute-start = (bf16[128,1024]{1,0:T(8,128)(2,1)S(1)}, bf16[128,1024]{1,0:T(8,128)(2,1)S(1)}, u32[]{:S(2)}, u32[]{:S(2)}) collective-permute-start(bf16[128,1024]{1,0:T(8,128)(2,1)S(1)} %pad_maximum_fusion), channel_id=1, source_target_pairs={{0,280},{8,272},{16,264},{24,256},{32,312},{40,304},{48,296},{56,2... | collective-permute-start | bytes 786440 | tf_op jit(solution)/shard_map/ppermute | solution.py:89
  52.1 11.4 %collective-permute-done.moved_ref = bf16[128,1024]{1,0:T(8,128)(2,1)S(1)} collective-permute-done((bf16[128,1024]{1,0:T(8,128)(2,1)S(1)}, bf16[128,1024]{1,0:T(8,128)(2,1)S(1)}, u32[]{:S(2)}, u32[]{:S(2)}) %collective-permute-start) | collective-permute-done | bytes 262176 | tf_op jit(solution)/shard_map/ppermute | solution.py:89
  63.5 0.0 all-to-all-done.2
  63.5 2.6 %collective-permute-start.1 = (bf16[2048,256]{1,0:T(8,128)(2,1)S(1)}, bf16[2048,256]{1,0:T(8,128)(2,1)S(1)}, u32[]{:S(2)}, u32[]{:S(2)}) collective-permute-start(bf16[2048,256]{1,0:T(8,128)(2,1)S(1)} %bitcast.29), channel_id=1, source_target_pairs={{0,1},{1,0},{2,3},{3,2},{4,5},{5,4},{6,7},{7,6},{8,9},{9,8},{10,11... | collective-permute-start | bytes 3145736 | tf_op jit(solution)/shard_map/ppermute | solution.py:76
  66.2 0.1 fusion.5
  66.3 1.2 gather_fusion
  67.5 0.9 collective-permute-done.1.other_ref
  68.4 16.5 %attention.1 = (bf16[128,512]{1,0:T(8,128)(2,1)}, bf16[128,512]{1,0:T(8,128)(2,1)}, bf16[128,1024]{1,0:T(8,128)(2,1)S(1)}, bf16[2048,256]{1,0:T(8,128)(2,1)S(1)}, bf16[2048,256]{1,0:T(8,128)(2,1)S(1)}) custom-call(s32[68]{0:T(128)S(1)} %broadcast_multiply_fusion.base_ref, bf16[128,512]{1,0:T(8,128)(2,1)S(1)} %bitcast.32, bf16[128,512]{1,0:T(8,128)(2,1)S(1)} %bitcast.33, ...), custom_call_target="tpu_custom_call" | custom-call | flops 6442450944 | bytes 6291456 | tf_op jit(solution)/shard_map/attention/pallas_call | solution.py:224
  84.9 2.3 %collective-permute-start.2 = (bf16[2048,256]{1,0:T(8,128)(2,1)S(1)}, bf16[2048,256]{1,0:T(8,128)(2,1)S(1)}, u32[]{:S(2)}, u32[]{:S(2)}) collective-permute-start(bf16[2048,256]{1,0:T(8,128)(2,1)S(1)} %get-tuple-element.21), channel_id=1, source_target_pairs={{0,1},{1,0},{2,3},{3,2},{4,5},{5,4},{6,7},{7,6},{8,9},{9,8},{10,11... | collective-permute-start | bytes 3145736 | tf_op jit(solution)/shard_map/ppermute | solution.py:76
  87.1 2.3 %collective-permute-done.2 = bf16[2048,256]{1,0:T(8,128)(2,1)S(1)} collective-permute-done((bf16[2048,256]{1,0:T(8,128)(2,1)S(1)}, bf16[2048,256]{1,0:T(8,128)(2,1)S(1)}, u32[]{:S(2)}, u32[]{:S(2)}) %collective-permute-start.2) | collective-permute-done | bytes 1048608 | tf_op jit(solution)/shard_map/ppermute | solution.py:76
  89.4 1.3 add_convert_fusion
  90.7 4.4 %all-to-all-start.3 = ((bf16[4,8,64,256]{3,2,1,0:T(8,128)(2,1)}), bf16[4,8,64,256]{3,2,1,0:T(8,128)(2,1)}, u32[]{:S(2)}, u32[]{:S(2)}) async-start(bf16[4,8,64,256]{3,2,1,0:T(8,128)(2,1)} %bitcast.34), calls=%async_computation.3 | async-start | bytes 2097152 | tf_op jit(solution)/shard_map/all_to_all | solution.py:93
  95.1 6.2 %collective-permute-start.3 = (bf16[128,1024]{1,0:T(8,128)(2,1)S(1)}, bf16[128,1024]{1,0:T(8,128)(2,1)S(1)}, u32[]{:S(2)}, u32[]{:S(2)}) collective-permute-start(bf16[128,1024]{1,0:T(8,128)(2,1)S(1)} %get-tuple-element.22), channel_id=1, source_target_pairs={{0,280},{8,272},{16,264},{24,256},{32,312},{40,304},{48,296},{56,2... | collective-permute-start | bytes 786440 | tf_op jit(solution)/shard_map/ppermute | solution.py:89
  101.2 11.6 %collective-permute-done.3.back_ref = bf16[128,1024]{1,0:T(8,128)(2,1)S(1)} collective-permute-done((bf16[128,1024]{1,0:T(8,128)(2,1)S(1)}, bf16[128,1024]{1,0:T(8,128)(2,1)S(1)}, u32[]{:S(2)}, u32[]{:S(2)}) %collective-permute-start.3) | collective-permute-done | bytes 262176 | tf_op jit(solution)/shard_map/ppermute | solution.py:89
  112.8 0.0 all-to-all-done.3
  112.8 1.4 %reduce_sum.34 = bf16[8,64,256]{2,1,0:T(8,128)(2,1)S(1)} reduce(bf16[4,8,64,256]{3,2,1,0:T(8,128)(2,1)} %all-to-all-done.3, bf16[]{:T(256)} %constant.100.clone.1), dimensions={0}, to_apply=%region_1.2 | reduce | flops 393216 | bytes 1310722 | tf_op jit(solution)/shard_map/reduce_sum | solution.py:282
  114.2 11.2 %all_to_all.32 = bf16[8,64,256]{2,1,0:T(8,128)(2,1)S(1)} all-to-all(bf16[8,64,256]{2,1,0:T(8,128)(2,1)S(1)} %reduce_sum.34), channel_id=1, replica_groups={{0,8,16,24,224,232,240,248},{32,40,48,56,192,200,208,216},{64,72,80,88,..., dimensions={0} | all-to-all | bytes 524288 | tf_op jit(solution)/shard_map/all_to_all | solution.py:93
  125.5 12.8 %all_to_all.33 = bf16[8,64,256]{2,1,0:T(8,128)(2,1)S(1)} all-to-all(bf16[8,64,256]{2,1,0:T(8,128)(2,1)S(1)} %broadcast_in_dim.37), channel_id=1, replica_groups=mesh['section'=2,'ctx'=32,'tp'=8] {'tp'}, dimensions={0} | all-to-all | bytes 524288 | tf_op jit(solution)/shard_map/all_to_all | solution.py:285
  138.3 1.5 %kv_unproject.1 = (bf16[128,1024]{1,0:T(8,128)(2,1)}, bf16[128,512]{1,0:T(8,128)(2,1)}, bf16[128,512]{1,0:T(8,128)(2,1)}) custom-call(bf16[4,128,256]{2,1,0:T(8,128)(2,1)S(1)} %bitcast.28, bf16[1024,1024]{1,0:T(8,128)(2,1)S(1)} %bitcast.26, bf16[128,1024]{1,0:T(8,128)(2,1)S(1)} %collective-permute-done.3.back_ref), custom_call_target="tpu_custom_call" | custom-call | tf_op jit(solution)/shard_map/kv_unproject/pallas_call | solution.py:124
  (17 shorter events, 0.2 us)
Async XLA Ops:
  0.6 65.6 %copy-start = (s32[64]{0:T(128)S(1)}, s32[64]{0:T(128)}, u32[]{:S(2)}) copy-start(s32[64]{0:T(128)} %param.13) | copy-start | bytes 772
  0.6 1.6 %copy-start.1 = (bf16[1,1024,1024]{2,1,0:T(8,128)(2,1)S(1)}, bf16[1,1024,1024]{2,1,0:T(8,128)(2,1)}, u32[]{:S(2)}) copy-start(bf16[1,1024,1024]{2,1,0:T(8,128)(2,1)} %param.8) | copy-start | bytes 6291460
  2.2 0.9 copy-start.3
  22.3 21.5 %copy-start.6 = (bf16[1,128,512]{2,1,0:T(8,128)(2,1)S(1)}, bf16[1,128,512]{2,1,0:T(8,128)(2,1)}, u32[]{:S(2)}) copy-start(bf16[1,128,512]{2,1,0:T(8,128)(2,1)} %param.12) | copy-start | bytes 393220
  22.3 21.5 %copy-start.7 = (bf16[1,128,512]{2,1,0:T(8,128)(2,1)S(1)}, bf16[1,128,512]{2,1,0:T(8,128)(2,1)}, u32[]{:S(2)}) copy-start(bf16[1,128,512]{2,1,0:T(8,128)(2,1)} %param.10) | copy-start | bytes 393220
  34.8 33.6 %copy-start.4 = (bf16[1,128,512]{2,1,0:T(8,128)(2,1)S(1)}, bf16[1,128,512]{2,1,0:T(8,128)(2,1)}, u32[]{:S(2)}) copy-start(bf16[1,128,512]{2,1,0:T(8,128)(2,1)} %param.9) | copy-start | bytes 393220
  34.8 33.6 %copy-start.5 = (bf16[1,128,512]{2,1,0:T(8,128)(2,1)S(1)}, bf16[1,128,512]{2,1,0:T(8,128)(2,1)}, u32[]{:S(2)}) copy-start(bf16[1,128,512]{2,1,0:T(8,128)(2,1)} %param.11) | copy-start | bytes 393220
  35.9 27.6 %all-to-all-start.2 = ((bf16[4,8,64,256]{3,2,1,0:T(8,128)(2,1)}), bf16[4,8,64,256]{3,2,1,0:T(8,128)(2,1)S(1)}, u32[]{:S(2)}, u32[]{:S(2)}) async-start(bf16[4,8,64,256]{3,2,1,0:T(8,128)(2,1)} %broadcast_in_dim.17), calls=%async_computation.2 | async-start | bytes 2097152 | tf_op jit(solution)/shard_map/all_to_all | solution.py:93
  43.9 19.7 %collective-permute-start = (bf16[128,1024]{1,0:T(8,128)(2,1)S(1)}, bf16[128,1024]{1,0:T(8,128)(2,1)S(1)}, u32[]{:S(2)}, u32[]{:S(2)}) collective-permute-start(bf16[128,1024]{1,0:T(8,128)(2,1)S(1)} %pad_maximum_fusion), channel_id=1, source_target_pairs={{0,280},{8,272},{16,264},{24,256},{32,312},{40,304},{48,296},{56,2... | collective-permute-start | bytes 786440 | tf_op jit(solution)/shard_map/ppermute | solution.py:89
  63.5 4.9 %collective-permute-start.1 = (bf16[2048,256]{1,0:T(8,128)(2,1)S(1)}, bf16[2048,256]{1,0:T(8,128)(2,1)S(1)}, u32[]{:S(2)}, u32[]{:S(2)}) collective-permute-start(bf16[2048,256]{1,0:T(8,128)(2,1)S(1)} %bitcast.29), channel_id=1, source_target_pairs={{0,1},{1,0},{2,3},{3,2},{4,5},{5,4},{6,7},{7,6},{8,9},{9,8},{10,11... | collective-permute-start | bytes 3145736 | tf_op jit(solution)/shard_map/ppermute | solution.py:76
  84.9 4.5 %collective-permute-start.2 = (bf16[2048,256]{1,0:T(8,128)(2,1)S(1)}, bf16[2048,256]{1,0:T(8,128)(2,1)S(1)}, u32[]{:S(2)}, u32[]{:S(2)}) collective-permute-start(bf16[2048,256]{1,0:T(8,128)(2,1)S(1)} %get-tuple-element.21), channel_id=1, source_target_pairs={{0,1},{1,0},{2,3},{3,2},{4,5},{5,4},{6,7},{7,6},{8,9},{9,8},{10,11... | collective-permute-start | bytes 3145736 | tf_op jit(solution)/shard_map/ppermute | solution.py:76
  90.7 47.6 %copy-start.2 = (bf16[1,1024,1024]{2,1,0:T(8,128)(2,1)S(1)}, bf16[1,1024,1024]{2,1,0:T(8,128)(2,1)}, u32[]{:S(2)}) copy-start(bf16[1,1024,1024]{2,1,0:T(8,128)(2,1)} %param.8) | copy-start | bytes 6291460
  90.7 22.1 %all-to-all-start.3 = ((bf16[4,8,64,256]{3,2,1,0:T(8,128)(2,1)}), bf16[4,8,64,256]{3,2,1,0:T(8,128)(2,1)}, u32[]{:S(2)}, u32[]{:S(2)}) async-start(bf16[4,8,64,256]{3,2,1,0:T(8,128)(2,1)} %bitcast.34), calls=%async_computation.3 | async-start | bytes 2097152 | tf_op jit(solution)/shard_map/all_to_all | solution.py:93
  95.1 17.7 %collective-permute-start.3 = (bf16[128,1024]{1,0:T(8,128)(2,1)S(1)}, bf16[128,1024]{1,0:T(8,128)(2,1)S(1)}, u32[]{:S(2)}, u32[]{:S(2)}) collective-permute-start(bf16[128,1024]{1,0:T(8,128)(2,1)S(1)} %get-tuple-element.22), channel_id=1, source_target_pairs={{0,280},{8,272},{16,264},{24,256},{32,312},{40,304},{48,296},{56,2... | collective-permute-start | bytes 786440 | tf_op jit(solution)/shard_map/ppermute | solution.py:89

commit v7 on v6

--- a/solution.py
+++ b/solution.py
@@ -35,8 +35,8 @@
     return (section * N_CTX + y * N_Z + z) * N_TP + x * N_CORE + core
 
 
-def fold(u, w):
-    return u + w * (N_Y - 1 - 2 * u)
+def pair_y(u, w):
+    return 2 * u + w
 
 
 def wide_groups():
@@ -45,7 +45,7 @@
         for x in range(N_X):
             for u in range(4):
                 groups.append(
-                    [device_index(section, fold(u, w), z, x, 0) for w in range(2) for z in range(N_Z)]
+                    [device_index(section, pair_y(u, w), z, x, 0) for w in range(2) for z in range(N_Z)]
                 )
             for z in range(N_Z):
                 groups.append([device_index(section, y, z, x, 1) for y in range(N_Y)])
@@ -58,7 +58,7 @@
         for x in range(N_X):
             for w in range(2):
                 for z in range(N_Z):
-                    groups.append([device_index(section, fold(u, w), z, x, 0) for u in range(4)])
+                    groups.append([device_index(section, pair_y(u, w), z, x, 0) for u in range(4)])
             for y in range(N_Y):
                 groups.append([device_index(section, y, z, x, 1) for z in range(N_Z)])
     return groups
@@ -67,7 +67,7 @@
 def block_owner(core):
     block = jnp.arange(N_CTX, dtype=jnp.int32)
     first, second = block // 8, block % 8
-    owner_0 = fold(first, second // 4) * N_Z + second % 4
+    owner_0 = pair_y(first, second // 4) * N_Z + second % 4
     owner_1 = second * N_Z + first
     return jnp.where(core == 0, owner_0, owner_1)
 

time: 140 us -> 138 us (0.986)
  waiting for transfers between devices: 26.1 us -> 24.3 us
    all_to_all x1, blocking collectives: 12.8 us -> 9.41 us  [on_device(): lax.all_to_all(jnp.broadcast_to(total[None], (N_TP, SPAN, 2 * HD)), 'tp',...]
    ppermute x2, waiting for transfers between devices: 23 us -> 20 us  [swap_section(): return lax.ppermute(value, ('section', 'ctx'), pairs)]
    all_to_all x2, blocking collectives: 23.6 us -> 26.6 us  [exchange(): lax.all_to_all(value, EVERY, 0, 0, axis_index_groups=groups, tiled=True)]
  transfers between devices with their start and end apart: 6 -> 6, of which waited for: 4 -> 5; matrix products, arithmetic and copies ran while one was open for 1% -> 1% of each run, Pallas kernels for 0% -> 0%
where the time goes in v7:
time: 138 us; the launch traced here: 137 us
  blocking collectives  54.6 us (40%)
  starting transfers between devices  31 us (22%)
  waiting for transfers between devices  24.3 us (18%)
  Pallas kernels  18.5 us (13%)
  local copies, waits for them, and re-layouts  4.93 us (4%)
  other arithmetic  2.9 us (2%)
    all_to_all x2, blocking collectives, exchange(): lax.all_to_all(value, EVERY, 0, 0, axis_index_groups=groups, tiled=True)  26.6 us
    ppermute x2, waiting for transfers between devices, swap_section(): return lax.ppermute(value, ('section', 'ctx'), pairs)  20 us
    all_to_all x1, blocking collectives, on_device(): lax.all_to_all(partial.reshape(N_TP, SPAN, 2 * HD), 'tp', 0, 0, tiled=True)  18.6 us
    pallas_call x1, Pallas kernels, attention(): pl.pallas_call(attention_kernel, in_specs=[pl.BlockSpec(memory_space=pltp...  16.5 us
    ppermute x2, starting transfers between devices, swap_section(): return lax.ppermute(value, ('section', 'ctx'), pairs)  13.8 us
    all_to_all x2, starting transfers between devices, exchange(): lax.all_to_all(value, EVERY, 0, 0, axis_index_groups=groups, tiled=True)  13.3 us
    all_to_all x1, blocking collectives, on_device(): lax.all_to_all(jnp.broadcast_to(total[None], (N_TP, SPAN, 2 * HD)), 'tp',...  9.41 us
    ppermute x2, starting transfers between devices, swap_core(): return lax.ppermute(value, 'tp', [(i, i ^ 1) for i in range(N_TP)])  3.94 us
  transfers between devices with their start and end apart: 6, of which 5 were waited for; matrix products, arithmetic and copies ran while one was open for 1% of the time, Pallas kernels for 0%

profile of v7, /device:TPU:1, one launch (start us, length us, event | category | flops | bytes accessed | tf_op | source)
XLA Modules:
  0.0 137.1 jit_solution(16605334881650418774)
XLA Ops:
  0.6 0.0 copy-start
  0.6 0.0 copy-start.1
  0.7 1.6 %copy-done.1 = bf16[1,1024,1024]{2,1,0:T(8,128)(2,1)S(1)} copy-done((bf16[1,1024,1024]{2,1,0:T(8,128)(2,1)S(1)}, bf16[1,1024,1024]{2,1,0:T(8,128)(2,1)}, u32[]{:S(2)}) %copy-start.1) | copy-done | bytes 2097176
  2.2 0.9 copy-done.3
  3.2 0.4 kv_project.1
  3.6 18.6 %all_to_all.30 = f32[8,64,256]{2,1,0:T(8,128)S(1)} all-to-all(f32[8,64,256]{2,1,0:T(8,128)S(1)} %bitcast.27), channel_id=1, replica_groups=mesh['section'=2,'ctx'=32,'tp'=8] {'tp'}, dimensions={0} | all-to-all | bytes 1048576 | tf_op jit(solution)/shard_map/all_to_all | solution.py:260
  22.3 0.0 copy-start.6
  22.3 0.0 copy-start.7
  22.4 12.7 %all_to_all.31 = bf16[8,64,256]{2,1,0:T(8,128)(2,1)S(1)} all-to-all(bf16[8,64,256]{2,1,0:T(8,128)(2,1)S(1)} %broadcast_in_dim.16), channel_id=1, replica_groups={{0,8,16,24,32,40,48,56},{64,72,80,88,96,104,112,120},{128,136,144,152,1..., dimensions={0} | all-to-all | bytes 524288 | tf_op jit(solution)/shard_map/all_to_all | solution.py:93
  35.1 1.1 broadcast_in_dim.17
  36.2 7.9 %all-to-all-start.2 = ((bf16[4,8,64,256]{3,2,1,0:T(8,128)(2,1)}), bf16[4,8,64,256]{3,2,1,0:T(8,128)(2,1)S(1)}, u32[]{:S(2)}, u32[]{:S(2)}) async-start(bf16[4,8,64,256]{3,2,1,0:T(8,128)(2,1)} %broadcast_in_dim.17), calls=%async_computation.2 | async-start | bytes 2097152 | tf_op jit(solution)/shard_map/all_to_all | solution.py:93
  44.1 8.2 %collective-permute-start = (bf16[128,1024]{1,0:T(8,128)(2,1)S(1)}, bf16[128,1024]{1,0:T(8,128)(2,1)S(1)}, u32[]{:S(2)}, u32[]{:S(2)}) collective-permute-start(bf16[128,1024]{1,0:T(8,128)(2,1)S(1)} %pad_maximum_fusion), channel_id=1, source_target_pairs={{0,280},{8,272},{16,264},{24,256},{32,312},{40,304},{48,296},{56,2... | collective-permute-start | bytes 786440 | tf_op jit(solution)/shard_map/ppermute | solution.py:89
  52.3 10.4 %collective-permute-done.moved_ref = bf16[128,1024]{1,0:T(8,128)(2,1)S(1)} collective-permute-done((bf16[128,1024]{1,0:T(8,128)(2,1)S(1)}, bf16[128,1024]{1,0:T(8,128)(2,1)S(1)}, u32[]{:S(2)}, u32[]{:S(2)}) %collective-permute-start) | collective-permute-done | bytes 262176 | tf_op jit(solution)/shard_map/ppermute | solution.py:89
  62.7 0.0 all-to-all-done.2
  62.7 1.9 %collective-permute-start.1 = (bf16[2048,256]{1,0:T(8,128)(2,1)S(1)}, bf16[2048,256]{1,0:T(8,128)(2,1)S(1)}, u32[]{:S(2)}, u32[]{:S(2)}) collective-permute-start(bf16[2048,256]{1,0:T(8,128)(2,1)S(1)} %bitcast.29), channel_id=1, source_target_pairs={{0,1},{1,0},{2,3},{3,2},{4,5},{5,4},{6,7},{7,6},{8,9},{9,8},{10,11... | collective-permute-start | bytes 3145736 | tf_op jit(solution)/shard_map/ppermute | solution.py:76
  64.7 0.1 fusion.5
  64.8 0.0 copy-done
  64.8 1.2 gather_fusion
  66.0 1.2 collective-permute-done.1.other_ref
  67.2 0.0 copy-done.5
  67.2 16.5 %attention.1 = (bf16[128,512]{1,0:T(8,128)(2,1)}, bf16[128,512]{1,0:T(8,128)(2,1)}, bf16[128,1024]{1,0:T(8,128)(2,1)S(1)}, bf16[2048,256]{1,0:T(8,128)(2,1)S(1)}, bf16[2048,256]{1,0:T(8,128)(2,1)S(1)}) custom-call(s32[68]{0:T(128)S(1)} %broadcast_multiply_fusion.base_ref, bf16[128,512]{1,0:T(8,128)(2,1)S(1)} %bitcast.32, bf16[128,512]{1,0:T(8,128)(2,1)S(1)} %bitcast.33, ...), custom_call_target="tpu_custom_call" | custom-call | flops 6442450944 | bytes 6291456 | tf_op jit(solution)/shard_map/attention/pallas_call | solution.py:224
  83.7 2.0 %collective-permute-start.2 = (bf16[2048,256]{1,0:T(8,128)(2,1)S(1)}, bf16[2048,256]{1,0:T(8,128)(2,1)S(1)}, u32[]{:S(2)}, u32[]{:S(2)}) collective-permute-start(bf16[2048,256]{1,0:T(8,128)(2,1)S(1)} %get-tuple-element.21), channel_id=1, source_target_pairs={{0,1},{1,0},{2,3},{3,2},{4,5},{5,4},{6,7},{7,6},{8,9},{9,8},{10,11... | collective-permute-start | bytes 3145736 | tf_op jit(solution)/shard_map/ppermute | solution.py:76
  85.8 2.5 %collective-permute-done.2 = bf16[2048,256]{1,0:T(8,128)(2,1)S(1)} collective-permute-done((bf16[2048,256]{1,0:T(8,128)(2,1)S(1)}, bf16[2048,256]{1,0:T(8,128)(2,1)S(1)}, u32[]{:S(2)}, u32[]{:S(2)}) %collective-permute-start.2) | collective-permute-done | bytes 1048608 | tf_op jit(solution)/shard_map/ppermute | solution.py:76
  88.3 1.3 add_convert_fusion
  89.6 5.4 %all-to-all-start.3 = ((bf16[4,8,64,256]{3,2,1,0:T(8,128)(2,1)}), bf16[4,8,64,256]{3,2,1,0:T(8,128)(2,1)}, u32[]{:S(2)}, u32[]{:S(2)}) async-start(bf16[4,8,64,256]{3,2,1,0:T(8,128)(2,1)} %bitcast.34), calls=%async_computation.3 | async-start | bytes 2097152 | tf_op jit(solution)/shard_map/all_to_all | solution.py:93
  95.0 5.6 %collective-permute-start.3 = (bf16[128,1024]{1,0:T(8,128)(2,1)S(1)}, bf16[128,1024]{1,0:T(8,128)(2,1)S(1)}, u32[]{:S(2)}, u32[]{:S(2)}) collective-permute-start(bf16[128,1024]{1,0:T(8,128)(2,1)S(1)} %get-tuple-element.22), channel_id=1, source_target_pairs={{0,280},{8,272},{16,264},{24,256},{32,312},{40,304},{48,296},{56,2... | collective-permute-start | bytes 786440 | tf_op jit(solution)/shard_map/ppermute | solution.py:89
  100.6 9.6 %collective-permute-done.3.back_ref = bf16[128,1024]{1,0:T(8,128)(2,1)S(1)} collective-permute-done((bf16[128,1024]{1,0:T(8,128)(2,1)S(1)}, bf16[128,1024]{1,0:T(8,128)(2,1)S(1)}, u32[]{:S(2)}, u32[]{:S(2)}) %collective-permute-start.3) | collective-permute-done | bytes 262176 | tf_op jit(solution)/shard_map/ppermute | solution.py:89
  110.2 0.6 all-to-all-done.3
  110.8 1.4 %reduce_sum.34 = bf16[8,64,256]{2,1,0:T(8,128)(2,1)S(1)} reduce(bf16[4,8,64,256]{3,2,1,0:T(8,128)(2,1)} %all-to-all-done.3, bf16[]{:T(256)} %constant.99.clone.1), dimensions={0}, to_apply=%region_1.2 | reduce | flops 393216 | bytes 1310722 | tf_op jit(solution)/shard_map/reduce_sum | solution.py:282
  112.2 13.9 %all_to_all.32 = bf16[8,64,256]{2,1,0:T(8,128)(2,1)S(1)} all-to-all(bf16[8,64,256]{2,1,0:T(8,128)(2,1)S(1)} %reduce_sum.34), channel_id=1, replica_groups={{0,8,16,24,32,40,48,56},{64,72,80,88,96,104,112,120},{128,136,144,152,1..., dimensions={0} | all-to-all | bytes 524288 | tf_op jit(solution)/shard_map/all_to_all | solution.py:93
  126.1 9.4 %all_to_all.33 = bf16[8,64,256]{2,1,0:T(8,128)(2,1)S(1)} all-to-all(bf16[8,64,256]{2,1,0:T(8,128)(2,1)S(1)} %broadcast_in_dim.37), channel_id=1, replica_groups=mesh['section'=2,'ctx'=32,'tp'=8] {'tp'}, dimensions={0} | all-to-all | bytes 524288 | tf_op jit(solution)/shard_map/all_to_all | solution.py:285
  135.5 1.5 %kv_unproject.1 = (bf16[128,1024]{1,0:T(8,128)(2,1)}, bf16[128,512]{1,0:T(8,128)(2,1)}, bf16[128,512]{1,0:T(8,128)(2,1)}) custom-call(bf16[4,128,256]{2,1,0:T(8,128)(2,1)S(1)} %bitcast.28, bf16[1024,1024]{1,0:T(8,128)(2,1)S(1)} %bitcast.26, bf16[128,1024]{1,0:T(8,128)(2,1)S(1)} %collective-permute-done.3.back_ref), custom_call_target="tpu_custom_call" | custom-call | tf_op jit(solution)/shard_map/kv_unproject/pallas_call | solution.py:124
  (17 shorter events, 0.2 us)
Async XLA Ops:
  0.6 64.1 %copy-start = (s32[64]{0:T(128)S(1)}, s32[64]{0:T(128)}, u32[]{:S(2)}) copy-start(s32[64]{0:T(128)} %param.13) | copy-start | bytes 772
  0.6 1.6 %copy-start.1 = (bf16[1,1024,1024]{2,1,0:T(8,128)(2,1)S(1)}, bf16[1,1024,1024]{2,1,0:T(8,128)(2,1)}, u32[]{:S(2)}) copy-start(bf16[1,1024,1024]{2,1,0:T(8,128)(2,1)} %param.8) | copy-start | bytes 6291460
  2.2 0.9 copy-start.3
  22.3 21.7 %copy-start.6 = (bf16[1,128,512]{2,1,0:T(8,128)(2,1)S(1)}, bf16[1,128,512]{2,1,0:T(8,128)(2,1)}, u32[]{:S(2)}) copy-start(bf16[1,128,512]{2,1,0:T(8,128)(2,1)} %param.12) | copy-start | bytes 393220
  22.3 21.7 %copy-start.7 = (bf16[1,128,512]{2,1,0:T(8,128)(2,1)S(1)}, bf16[1,128,512]{2,1,0:T(8,128)(2,1)}, u32[]{:S(2)}) copy-start(bf16[1,128,512]{2,1,0:T(8,128)(2,1)} %param.10) | copy-start | bytes 393220
  35.1 32.2 %copy-start.4 = (bf16[1,128,512]{2,1,0:T(8,128)(2,1)S(1)}, bf16[1,128,512]{2,1,0:T(8,128)(2,1)}, u32[]{:S(2)}) copy-start(bf16[1,128,512]{2,1,0:T(8,128)(2,1)} %param.9) | copy-start | bytes 393220
  35.1 32.2 %copy-start.5 = (bf16[1,128,512]{2,1,0:T(8,128)(2,1)S(1)}, bf16[1,128,512]{2,1,0:T(8,128)(2,1)}, u32[]{:S(2)}) copy-start(bf16[1,128,512]{2,1,0:T(8,128)(2,1)} %param.11) | copy-start | bytes 393220
  36.2 26.5 %all-to-all-start.2 = ((bf16[4,8,64,256]{3,2,1,0:T(8,128)(2,1)}), bf16[4,8,64,256]{3,2,1,0:T(8,128)(2,1)S(1)}, u32[]{:S(2)}, u32[]{:S(2)}) async-start(bf16[4,8,64,256]{3,2,1,0:T(8,128)(2,1)} %broadcast_in_dim.17), calls=%async_computation.2 | async-start | bytes 2097152 | tf_op jit(solution)/shard_map/all_to_all | solution.py:93
  44.1 18.6 %collective-permute-start = (bf16[128,1024]{1,0:T(8,128)(2,1)S(1)}, bf16[128,1024]{1,0:T(8,128)(2,1)S(1)}, u32[]{:S(2)}, u32[]{:S(2)}) collective-permute-start(bf16[128,1024]{1,0:T(8,128)(2,1)S(1)} %pad_maximum_fusion), channel_id=1, source_target_pairs={{0,280},{8,272},{16,264},{24,256},{32,312},{40,304},{48,296},{56,2... | collective-permute-start | bytes 786440 | tf_op jit(solution)/shard_map/ppermute | solution.py:89
  62.7 4.5 %collective-permute-start.1 = (bf16[2048,256]{1,0:T(8,128)(2,1)S(1)}, bf16[2048,256]{1,0:T(8,128)(2,1)S(1)}, u32[]{:S(2)}, u32[]{:S(2)}) collective-permute-start(bf16[2048,256]{1,0:T(8,128)(2,1)S(1)} %bitcast.29), channel_id=1, source_target_pairs={{0,1},{1,0},{2,3},{3,2},{4,5},{5,4},{6,7},{7,6},{8,9},{9,8},{10,11... | collective-permute-start | bytes 3145736 | tf_op jit(solution)/shard_map/ppermute | solution.py:76
  83.7 4.5 %collective-permute-start.2 = (bf16[2048,256]{1,0:T(8,128)(2,1)S(1)}, bf16[2048,256]{1,0:T(8,128)(2,1)S(1)}, u32[]{:S(2)}, u32[]{:S(2)}) collective-permute-start(bf16[2048,256]{1,0:T(8,128)(2,1)S(1)} %get-tuple-element.21), channel_id=1, source_target_pairs={{0,1},{1,0},{2,3},{3,2},{4,5},{5,4},{6,7},{7,6},{8,9},{9,8},{10,11... | collective-permute-start | bytes 3145736 | tf_op jit(solution)/shard_map/ppermute | solution.py:76
  89.6 46.0 %copy-start.2 = (bf16[1,1024,1024]{2,1,0:T(8,128)(2,1)S(1)}, bf16[1,1024,1024]{2,1,0:T(8,128)(2,1)}, u32[]{:S(2)}) copy-start(bf16[1,1024,1024]{2,1,0:T(8,128)(2,1)} %param.8) | copy-start | bytes 6291460
  89.6 21.2 %all-to-all-start.3 = ((bf16[4,8,64,256]{3,2,1,0:T(8,128)(2,1)}), bf16[4,8,64,256]{3,2,1,0:T(8,128)(2,1)}, u32[]{:S(2)}, u32[]{:S(2)}) async-start(bf16[4,8,64,256]{3,2,1,0:T(8,128)(2,1)} %bitcast.34), calls=%async_computation.3 | async-start | bytes 2097152 | tf_op jit(solution)/shard_map/all_to_all | solution.py:93
  95.0 15.2 %collective-permute-start.3 = (bf16[128,1024]{1,0:T(8,128)(2,1)S(1)}, bf16[128,1024]{1,0:T(8,128)(2,1)S(1)}, u32[]{:S(2)}, u32[]{:S(2)}) collective-permute-start(bf16[128,1024]{1,0:T(8,128)(2,1)S(1)} %get-tuple-element.22), channel_id=1, source_target_pairs={{0,280},{8,272},{16,264},{24,256},{32,312},{40,304},{48,296},{56,2... | collective-permute-start | bytes 786440 | tf_op jit(solution)/shard_map/ppermute | solution.py:89
